TPU v7x, 128 devices: a whole 4x4x4 slice. The times are simulated.
128 devices in a mesh: freq: 4 (over x), blk: 32 (over z, y, core).
Axes of the slice: x: 4, y: 4, z: 4, core: 2. Of those that a mesh axis runs over, the one named last changes fastest.
Arguments:
- series: bfloat16 [32, 128, 6000], P('blk', 'freq'), may hold values from -24 to 24
- tapers: float32 [5, 6000], replicated, may hold values from -0.078125 to 0.078125
- live_channels: int32 [32], P('blk'), may hold values from 64 to 128, as said below
- pair_offset: int32 [32, 5], P('blk'), may hold values from 0 to 4, as said below
- pair_count: int32 [32], P('blk'), may hold values from 1 to 5, as said below
Outputs:
- csdm: float32 [32, 5, 2, 16, 128, 128], P('blk', None, None, 'freq')
Inputs may be any that keep to these rules, and one draw needn't show every extreme that they name: `live_channels`: one block in every draw has all 128 channels working. `pair_offset`: the first pair_count[i] entries of row i are distinct offsets in ascending order, the used ones; the rest of the row holds the remaining offsets of 0 to 4 in ascending order. `pair_count`: some block in every draw uses all 5 slots.
All inputs are finite; a program needn't handle non-finite values.
Results may differ from a plain program's by a relative error of at most 0.0043.
Values may be sent and summed in bfloat16 or wider, within the bound.
No kernel may reach another device: no remote copies, remote signals or barrier semaphores. Data moves between devices by JAX's collectives and lax.ppermute only.
A program may use at most 128 MiB of HBM per device.

v0:
```python
import math

import jax
import jax.numpy as jnp
from jax import lax
from jax.sharding import PartitionSpec as P

NF = 2048
K = 5
BW = 128
REACH = 4
SLOTS = 5


def passed_along(shard, axis, by):
    peers = lax.axis_size(axis)
    return lax.ppermute(shard, axis, [(i, (i + by) % peers) for i in range(peers)])


def dft_table(first_bin, count, length, period):
    samples = jnp.arange(length, dtype=jnp.int32)
    bins = first_bin + jnp.arange(count, dtype=jnp.int32)
    phase = samples[:, None] * bins[None, :] % period
    angle = phase.astype(jnp.float32) * (2.0 * math.pi / period)
    return jnp.concatenate([jnp.cos(angle), -jnp.sin(angle)], axis=1).astype(jnp.bfloat16)


def taper_rows(series_rows, tapers, live_count, first_row):
    channel = first_row + jnp.arange(series_rows.shape[0], dtype=jnp.int32)
    weight_mask = (channel < live_count).astype(jnp.float32)
    return (
        series_rows.astype(jnp.float32)[None] * tapers[:, None, :] * weight_mask[None, :, None]
    ).astype(jnp.bfloat16)


def cross_band(mine, other):
    rotated = jnp.stack([-other[:, :, 1], other[:, :, 0]], axis=2)
    real_part = jnp.einsum("kcpbw,kdpbw->bcd", mine, other, preferred_element_type=jnp.float32)
    imag_part = jnp.einsum("kcpbw,kdpbw->bcd", mine, rotated, preferred_element_type=jnp.float32)
    return jnp.stack([real_part, imag_part]) * (1.0 / (K * BW))


def body(series, tapers, live_channels, pair_offset, pair_count):
    taper_count = tapers.shape[0]
    samples = series.shape[2]
    groups = lax.axis_size("freq")
    freq_dev = NF // groups
    period = 2 * NF
    live_count = live_channels[0]
    local_rows = series.shape[1]
    tapered = taper_rows(series[0], tapers, live_count, lax.axis_index("freq") * local_rows)
    flat_rows = tapered.reshape(taper_count * local_rows, samples)
    pieces = []
    for quarter in range(groups):
        table = dft_table(quarter * freq_dev, freq_dev, samples, period)
        product = jnp.dot(flat_rows, table, preferred_element_type=jnp.float32)
        pieces.append(product.reshape(taper_count, local_rows, 2, freq_dev))
    spectra_all = jnp.concatenate(pieces, axis=3).astype(jnp.bfloat16)
    owned = lax.all_to_all(spectra_all, "freq", split_axis=3, concat_axis=1, tiled=True)
    block_size = owned.shape[1]
    held = [owned]
    for distance in range(1, REACH + 1):
        held.append(passed_along(owned, "blk", -distance))
    stacked = jnp.stack(held)
    band_count = freq_dev // BW
    mine = owned.reshape(taper_count, block_size, 2, band_count, BW)
    results = []
    for position in range(SLOTS):
        live_slot = (position < pair_count[0]).astype(jnp.float32)
        offset = pair_offset[0, position]
        partner = lax.dynamic_index_in_dim(stacked, offset, 0, keepdims=False)
        results.append(
            cross_band(mine, partner.reshape(taper_count, block_size, 2, band_count, BW))
            * live_slot
        )
    output = jnp.stack(results)
    return output[None]


def solution(mesh):
    return jax.shard_map(
        body,
        mesh=mesh,
        in_specs=(P("blk", "freq", None), P(), P("blk"), P("blk", None), P("blk")),
        out_specs=P("blk", None, None, "freq", None, None),
        check_vma=False,
    )
```

profile of v0, /device:TPU:0, one launch (start us, length us, event | category | flops | bytes accessed | tf_op | source)
XLA Modules:
  0.0 493.2 jit_solution(12866524647963192125)
XLA Ops:
  0.0 50.4 %negate_convert_fusion.3 = (bf16[6000,512]{0,1:T(8,128)(2,1)}, bf16[6000,512]{0,1:T(8,128)(2,1)}) fusion(), kind=kLoop, calls=%fused_computation.40 | loop fusion | flops 52224000 | bytes 12288000 | tf_op jit(solution)/shard_map/convert.12
  51.1 52.7 %cosine_convert_fusion.2 = (bf16[6000,512]{0,1:T(8,128)(2,1)}, bf16[6000,512]{0,1:T(8,128)(2,1)}) fusion(s32[512]{0:T(512)S(1)} %iota_add_fusion.2), kind=kLoop, calls=%fused_computation.37 | loop fusion | flops 52224000 | bytes 12290048 | tf_op jit(solution)/shard_map/convert.9
  103.8 52.7 %cosine_convert_fusion.1 = (bf16[6000,512]{0,1:T(8,128)(2,1)}, bf16[6000,512]{0,1:T(8,128)(2,1)}) fusion(s32[512]{0:T(512)S(1)} %iota_add_fusion.1), kind=kLoop, calls=%fused_computation.33 | loop fusion | flops 52224000 | bytes 12290048 | tf_op jit(solution)/shard_map/convert.7
  156.6 13.4 %pad_maximum_fusion.1 = bf16[6000,1024]{0,1:T(8,128)(2,1)} fusion(bf16[6000,512]{0,1:T(8,128)(2,1)} %get-tuple-element.21, bf16[6000,512]{0,1:T(8,128)(2,1)} %get-tuple-element.20), kind=kLoop, calls=%fused_computation.25 | loop fusion | flops 24576000 | bytes 24576000 | tf_op jit(solution)/shard_map/concatenate | solution.py:25
  170.0 7.4 %pad_maximum_fusion.2 = bf16[6000,1024]{0,1:T(8,128)(2,1)} fusion(bf16[6000,512]{0,1:T(8,128)(2,1)S(1)} %bitcast.142, bf16[6000,512]{0,1:T(8,128)(2,1)S(1)} %bitcast.140), kind=kLoop, calls=%fused_computation.26 | loop fusion | flops 24576000 | bytes 24576000 | tf_op jit(solution)/shard_map/concatenate | solution.py:25
  177.4 8.8 %fusion.78 = bf16[5,32,2,512]{3,1,2,0:T(8,128)(2,1)S(1)} fusion(bf16[2,512,6000,1]{2,1,0,3:T(8,128)(2,1)} %bitcast.147, f32[32]{0:T(128)S(1)} %compare_convert_fusion, f32[5,6000]{1,0:T(8,128)S(1)} %copy-done.24, f32[32,6000]{1,0:T(8,128)S(1)} %bitcast_convert_fusion), kind=kOutput, calls=%fused_computation.102 | convolution fusion | flops 1969123840 | bytes 13503808 | tf_op jit(solution)/shard_map/dot_general | solution.py:56
  186.3 9.0 %fusion.81 = bf16[5,32,2,512]{3,1,2,0:T(8,128)(2,1)S(1)} fusion(bf16[2,512,6000,1]{2,1,0,3:T(8,128)(2,1)} %bitcast.148, f32[32]{0:T(128)S(1)} %compare_convert_fusion, f32[5,6000]{1,0:T(8,128)S(1)} %copy-done.24, f32[32,6000]{1,0:T(8,128)S(1)} %bitcast_convert_fusion), kind=kOutput, calls=%fused_computation.103 | convolution fusion | flops 1969123840 | bytes 13503808 | tf_op jit(solution)/shard_map/dot_general | solution.py:56
  195.3 9.9 %pad_maximum_fusion = bf16[6000,1024]{0,1:T(8,128)(2,1)} fusion(bf16[6000,512]{0,1:T(8,128)(2,1)S(1)} %bitcast.144, bf16[6000,512]{0,1:T(8,128)(2,1)} %get-tuple-element.32), kind=kLoop, calls=%fused_computation.24 | loop fusion | flops 24576000 | bytes 24576000 | tf_op jit(solution)/shard_map/concatenate | solution.py:25
  205.1 8.8 %fusion.75 = bf16[5,32,2,512]{3,1,2,0:T(8,128)(2,1)S(1)} fusion(bf16[2,512,6000,1]{2,1,0,3:T(8,128)(2,1)} %bitcast.150, f32[32]{0:T(128)S(1)} %compare_convert_fusion, f32[5,6000]{1,0:T(8,128)S(1)} %copy-done.24, f32[32,6000]{1,0:T(8,128)S(1)} %bitcast_convert_fusion), kind=kOutput, calls=%fused_computation.101 | convolution fusion | flops 1969123840 | bytes 13503808 | tf_op jit(solution)/shard_map/dot_general | solution.py:56
  214.0 51.7 %cosine_convert_fusion = (bf16[6000,512]{0,1:T(8,128)(2,1)S(1)}, bf16[6000,512]{0,1:T(8,128)(2,1)S(1)}) fusion(s32[512]{0:T(512)S(1)} %iota_add_fusion), kind=kLoop, calls=%fused_computation.29 | loop fusion | flops 52224000 | bytes 12290048 | tf_op jit(solution)/shard_map/convert.5
  265.7 7.4 %pad_maximum_fusion.3 = bf16[6000,1024]{0,1:T(8,128)(2,1)} fusion(bf16[6000,512]{0,1:T(8,128)(2,1)S(1)} %get-tuple-element.25, bf16[6000,512]{0,1:T(8,128)(2,1)S(1)} %get-tuple-element.24), kind=kLoop, calls=%fused_computation.27 | loop fusion | flops 24576000 | bytes 24576000 | tf_op jit(solution)/shard_map/concatenate | solution.py:25
  273.1 8.8 %fusion.84 = bf16[5,32,2,512]{3,1,2,0:T(8,128)(2,1)S(1)} fusion(bf16[2,512,6000,1]{2,1,0,3:T(8,128)(2,1)} %bitcast.149, f32[32]{0:T(128)S(1)} %compare_convert_fusion, f32[5,6000]{1,0:T(8,128)S(1)} %copy-done.24, f32[32,6000]{1,0:T(8,128)S(1)} %bitcast_convert_fusion), kind=kOutput, calls=%fused_computation.104 | convolution fusion | flops 1969123840 | bytes 13503808 | tf_op jit(solution)/shard_map/dot_general | solution.py:56
  282.1 7.8 %copy.80 = bf16[5,32,2,2048]{1,2,0,3:T(2,128)(2,1)} copy(bf16[5,32,2,2048]{3,1,2,0:T(8,128)(2,1)S(1)} %pad_maximum_fusion.4) | data formatting | bytes 2621440 | tf_op jit(solution)/shard_map/concatenate | solution.py:58
  289.9 6.5 %reshape.285 = bf16[4,2,81920]{2,1,0:T(2,128)(2,1)S(1)} reshape(bf16[2048,5,2,32]{3,2,1,0:T(2,128)(2,1)} %bitcast.145) | data formatting | bytes 2621440
  296.4 22.1 %all_to_all.18 = bf16[4,2,81920]{2,1,0:T(2,128)(2,1)S(1)} all-to-all(bf16[4,2,81920]{2,1,0:T(2,128)(2,1)S(1)} %reshape.285), channel_id=1, replica_groups=mesh['freq'=4,'blk'=32] {'freq'}, dimensions={0} | all-to-all | bytes 2621440 | tf_op jit(solution)/shard_map/all_to_all | solution.py:59
  318.5 4.1 reshape.286
  322.6 12.2 %copy.139 = bf16[5,32,2,4,512]{4,3,1,2,0:T(4,128)(2,1)S(1)} copy(bf16[5,32,2,4,512]{1,2,0,4,3:T(2,128)(2,1)} %bitcast.146) | data formatting | bytes 2621440 | tf_op jit(solution)/shard_map/all_to_all | solution.py:59
  335.2 4.8 collective-permute-start
  342.2 2.7 collective-permute-start.3
  357.1 10.7 %collective-permute-done = bf16[5,128,2,512]{3,1,2,0:T(8,128)(2,1)} collective-permute-done((bf16[5,128,2,512]{3,1,2,0:T(8,128)(2,1)S(1)}, bf16[5,128,2,512]{3,1,2,0:T(8,128)(2,1)}, u32[]{:S(2)}, u32[]{:S(2)}) %collective-permute-start) | collective-permute-done | bytes 1310752 | tf_op jit(solution)/shard_map/ppermute | solution.py:17
  369.2 68.8 %collective-permute-done.1 = bf16[5,128,2,512]{3,1,2,0:T(8,128)(2,1)} collective-permute-done((bf16[5,128,2,512]{3,1,2,0:T(8,128)(2,1)S(1)}, bf16[5,128,2,512]{3,1,2,0:T(8,128)(2,1)}, u32[]{:S(2)}, u32[]{:S(2)}) %collective-permute-start.1) | collective-permute-done | bytes 1310752 | tf_op jit(solution)/shard_map/ppermute | solution.py:17
  441.0 2.6 constant_dynamic-slice_fusion
  455.3 2.6 fusion.93
  465.3 2.6 fusion.87
  (121 shorter events, 53.4 us)
Async XLA Ops:
  0.0 50.4 %copy-start.17 = (bf16[1,32,6000]{2,1,0:T(8,128)(2,1)S(1)}, bf16[1,32,6000]{2,1,0:T(8,128)(2,1)}, u32[]{:S(2)}) copy-start(bf16[1,32,6000]{2,1,0:T(8,128)(2,1)} %param.5) | copy-start | bytes 1152004
  156.5 13.4 %slice-start = ((s8[6160384]{0:T(1024)(128)(4,1)}), s8[4194304]{0:T(1024)(128)(4,1)S(1)}, s32[]{:S(2)}) async-start(s8[6160384]{0:T(1024)(128)(4,1)} %bitcast.139), calls=%async_computation.1 | async-start | bytes 8388608
  156.5 13.4 %slice-start.2 = ((s8[6160384]{0:T(1024)(128)(4,1)}), s8[4194304]{0:T(1024)(128)(4,1)S(1)}, s32[]{:S(2)}) async-start(s8[6160384]{0:T(1024)(128)(4,1)} %bitcast.141), calls=%async_computation.3 | async-start | bytes 8388608
  156.5 13.4 %slice-start.1 = ((s8[6160384]{0:T(1024)(128)(4,1)}), s8[1966080]{0:T(1024)(128)(4,1)S(1)}, s32[]{:S(2)}) async-start(s8[6160384]{0:T(1024)(128)(4,1)} %bitcast.139), calls=%async_computation.2 | async-start | bytes 3932160
  156.5 13.4 %slice-start.3 = ((s8[6160384]{0:T(1024)(128)(4,1)}), s8[1966080]{0:T(1024)(128)(4,1)S(1)}, s32[]{:S(2)}) async-start(s8[6160384]{0:T(1024)(128)(4,1)} %bitcast.141), calls=%async_computation.4 | async-start | bytes 3932160
  170.0 7.4 %copy-start.24 = (f32[5,6000]{1,0:T(8,128)S(1)}, f32[5,6000]{1,0:T(8,128)}, u32[]{:S(2)}) copy-start(f32[5,6000]{1,0:T(8,128)} %param.6) | copy-start | bytes 360004
  186.2 9.0 %slice-start.4 = ((s8[6160384]{0:T(1024)(128)(4,1)}), s8[4194304]{0:T(1024)(128)(4,1)S(1)}, s32[]{:S(2)}) async-start(s8[6160384]{0:T(1024)(128)(4,1)} %bitcast.143), calls=%async_computation.5 | async-start | bytes 8388608
  186.3 9.0 %slice-start.5 = ((s8[6160384]{0:T(1024)(128)(4,1)}), s8[1966080]{0:T(1024)(128)(4,1)S(1)}, s32[]{:S(2)}) async-start(s8[6160384]{0:T(1024)(128)(4,1)} %bitcast.143), calls=%async_computation.6 | async-start | bytes 3932160
  322.6 22.3 %copy-start.23 = (s32[1,5]{1,0:T(1,128)S(1)}, s32[1,5]{1,0:T(1,128)}, u32[]{:S(2)}) copy-start(s32[1,5]{1,0:T(1,128)} %param.8) | copy-start | bytes 64
  335.2 32.6 %collective-permute-start = (bf16[5,128,2,512]{3,1,2,0:T(8,128)(2,1)S(1)}, bf16[5,128,2,512]{3,1,2,0:T(8,128)(2,1)}, u32[]{:S(2)}, u32[]{:S(2)}) collective-permute-start(bf16[5,128,2,512]{3,1,2,0:T(8,128)(2,1)S(1)} %bitcast.151), channel_id=1, source_target_pairs={{0,31},{1,0},{2,1},{3,2},{4,3},{5,4},{6,5},{7,6},{8,7},{9,8},{10,9... | collective-permute-start | bytes 3932168 | tf_op jit(solution)/shard_map/ppermute | solution.py:17
  340.0 98.0 %collective-permute-start.1 = (bf16[5,128,2,512]{3,1,2,0:T(8,128)(2,1)S(1)}, bf16[5,128,2,512]{3,1,2,0:T(8,128)(2,1)}, u32[]{:S(2)}, u32[]{:S(2)}) collective-permute-start(bf16[5,128,2,512]{3,1,2,0:T(8,128)(2,1)S(1)} %bitcast.152), channel_id=1, source_target_pairs={{0,30},{1,31},{2,0},{3,1},{4,2},{5,3},{6,4},{7,5},{8,6},{9,7},{10,... | collective-permute-start | bytes 3932168 | tf_op jit(solution)/shard_map/ppermute | solution.py:17
  341.8 97.6 %collective-permute-start.2 = (bf16[5,128,2,512]{3,1,2,0:T(8,128)(2,1)S(1)}, bf16[5,128,2,512]{3,1,2,0:T(8,128)(2,1)}, u32[]{:S(2)}, u32[]{:S(2)}) collective-permute-start(bf16[5,128,2,512]{3,1,2,0:T(8,128)(2,1)S(1)} %bitcast.153), channel_id=1, source_target_pairs={{0,29},{1,30},{2,31},{3,0},{4,1},{5,2},{6,3},{7,4},{8,5},{9,6},{10... | collective-permute-start | bytes 3932168 | tf_op jit(solution)/shard_map/ppermute | solution.py:17
  342.2 98.6 %collective-permute-start.3 = (bf16[5,128,2,512]{3,1,2,0:T(8,128)(2,1)S(1)}, bf16[5,128,2,512]{3,1,2,0:T(8,128)(2,1)S(1)}, u32[]{:S(2)}, u32[]{:S(2)}) collective-permute-start(bf16[5,128,2,512]{3,1,2,0:T(8,128)(2,1)S(1)} %bitcast.154), channel_id=1, source_target_pairs={{0,28},{1,29},{2,30},{3,31},{4,0},{5,1},{6,2},{7,3},{8,4},{9,5},{1... | collective-permute-start | bytes 3932168 | tf_op jit(solution)/shard_map/ppermute | solution.py:17
  465.3 3.6 copy-start.3
  468.8 5.0 %copy-start = (bf16[5,128,1,4,128]{1,4,3,2,0:T(8,128)(2,1)S(1)}, bf16[5,128,1,4,128]{1,4,3,2,0:T(8,128)(2,1)}, u32[]{:S(2)}) copy-start(bf16[5,128,1,4,128]{1,4,3,2,0:T(8,128)(2,1)} %get-tuple-element.13) | copy-start | bytes 1966084
  470.2 9.1 %copy-start.1 = (bf16[5,128,1,4,128]{1,4,3,2,0:T(8,128)(2,1)S(1)}, bf16[5,128,1,4,128]{1,4,3,2,0:T(8,128)(2,1)}, u32[]{:S(2)}) copy-start(bf16[5,128,1,4,128]{1,4,3,2,0:T(8,128)(2,1)} %get-tuple-element.15) | copy-start | bytes 1966084
  471.3 9.1 %copy-start.4 = (bf16[5,128,1,4,128]{1,4,3,2,0:T(8,128)(2,1)S(1)}, bf16[5,128,1,4,128]{1,4,3,2,0:T(8,128)(2,1)}, u32[]{:S(2)}) copy-start(bf16[5,128,1,4,128]{1,4,3,2,0:T(8,128)(2,1)} %get-tuple-element.16) | copy-start | bytes 1966084
  473.8 7.9 %copy-start.2 = (bf16[5,128,1,4,128]{1,4,3,2,0:T(8,128)(2,1)S(1)}, bf16[5,128,1,4,128]{1,4,3,2,0:T(8,128)(2,1)}, u32[]{:S(2)}) copy-start(bf16[5,128,1,4,128]{1,4,3,2,0:T(8,128)(2,1)} %get-tuple-element.17) | copy-start | bytes 1966084
  474.9 7.9 %copy-start.5 = (bf16[5,128,1,4,128]{1,4,3,2,0:T(8,128)(2,1)S(1)}, bf16[5,128,1,4,128]{1,4,3,2,0:T(8,128)(2,1)}, u32[]{:S(2)}) copy-start(bf16[5,128,1,4,128]{1,4,3,2,0:T(8,128)(2,1)} %get-tuple-element.18) | copy-start | bytes 1966084
  480.7 4.6 copy-start.7
  483.2 4.1 copy-start.9
  485.3 4.0 copy-start.6
  485.3 4.0 copy-start.11
  485.3 4.0 copy-start.12
  (11 other events, 19.1 us)
where the time goes:
time: 496 us; the launch traced here: 493 us
  other arithmetic  252 us (51%)
  waiting for transfers between devices  79.5 us (16%)
  local copies, waits for them, and re-layouts  65.5 us (13%)
  matrix products  52.9 us (11%)
  blocking collectives  22.1 us (4%)
  between operations  11.3 us (2%)
  starting transfers between devices  9.77 us (2%)
    another operation x4, other arithmetic  207 us
    ppermute x4, waiting for transfers between devices, passed_along(): lax.ppermute(shard, axis, [(i, (i + by) % peers) for i in range(peers)])  79.5 us
    concatenate x4, other arithmetic, dft_table(): jnp.concatenate([jnp.cos(angle), -jnp.sin(angle)], axis=1)  38.1 us
    dot_general x4, matrix products, body(): product = jnp.dot(flat_rows, table, preferred_element_type=jnp.float32)  35.4 us
    unnamed x78, local copies, waits for them, and re-layouts  27.3 us
    all_to_all x1, blocking collectives, body(): lax.all_to_all(spectra_all, 'freq', split_axis=3, concat_axis=1, tiled=True)  22.1 us
    all_to_all x2, local copies, waits for them, and re-layouts, body(): lax.all_to_all(spectra_all, 'freq', split_axis=3, concat_axis=1, tiled=True)  12.5 us
    dot_general x5, matrix products, cross_band(): jnp.einsum('kcpbw,kdpbw->bcd', mine, other, preferred_element_type=jnp.fl...  12 us
  transfers between devices with their start and end apart: 4, of which 2 were waited for; matrix products, arithmetic and copies ran while one was open for 1% of the time, Pallas kernels for 0%

commit v1 on v0

v1 whole, which is shorter than its diff:
```python
import functools

import jax
import jax.numpy as jnp
import ml_dtypes
import numpy as np
from jax import lax
from jax.experimental import pallas as pl
from jax.experimental.pallas import tpu as pltpu
from jax.sharding import Mesh
from jax.sharding import PartitionSpec as P

NF = 2048
K = 5
BW = 128
PERIOD = 2 * NF
HALF = PERIOD // 2
SLOTS = 5
RING = 4
OWNERS = RING * RING
VMEM_LIMIT = 56 * 1024 * 1024


def half_period_tables():
    samples = np.arange(HALF, dtype=np.int64)
    bins = np.stack(
        [
            np.concatenate(
                [(RING * (owner % RING) + owner // RING) * BW + 2 * np.arange(BW // 2) + parity
                 for owner in range(OWNERS)]
            )
            for parity in range(2)
        ]
    )
    angle = ((samples[None, :, None] * bins[:, None, :]) % PERIOD) * (2.0 * np.pi / PERIOD)
    parts = np.stack([np.cos(angle), -np.sin(angle)], axis=2)
    parts = parts.reshape(2, HALF, 2, OWNERS, BW // 2).transpose(3, 0, 1, 2, 4)
    parts = parts.reshape(OWNERS // 2, 2, 2, HALF, BW).transpose(0, 2, 3, 1, 4)
    return parts.reshape(OWNERS // 2, 2, HALF, 2 * BW).astype(ml_dtypes.bfloat16)


def spectra_kernel(scalars, series, tapers, table, out, even, odd):
    rows, samples = series.shape

    @pl.when(pl.program_id(0) == 0)
    def _():
        live, first = scalars[0], scalars[1]
        channel = first + lax.broadcasted_iota(jnp.int32, (rows, HALF), 0)
        working = channel < live

        def tapered(k, begin, end):
            product = series[:, begin:end].astype(jnp.float32) * tapers[k : k + 1, begin:end]
            if end - begin < HALF:
                product = jnp.concatenate(
                    [product, jnp.zeros((rows, HALF - (end - begin)), jnp.float32)], axis=1
                )
            product = jnp.where(working, product, 0.0)
            return product.astype(jnp.bfloat16).astype(jnp.float32)

        for k in range(K):
            ends = tapered(k, 0, HALF) + tapered(k, 2 * HALF, samples)
            middle = tapered(k, HALF, 2 * HALF)
            even[k * rows : (k + 1) * rows, :] = (ends + middle).astype(jnp.bfloat16)
            odd[k * rows : (k + 1) * rows, :] = (ends - middle).astype(jnp.bfloat16)

    for parity, folded in enumerate((even, odd)):
        bins = jnp.dot(folded[...], table[0, parity], preferred_element_type=jnp.float32)
        bins = bins.astype(jnp.bfloat16)
        out[0, :, parity * BW : (parity + 1) * BW] = bins[:, :BW]
        out[1, :, parity * BW : (parity + 1) * BW] = bins[:, BW:]


def block_spectra(scalars, series, tapers, table):
    rows, samples = series.shape
    return pl.pallas_call(
        spectra_kernel,
        grid=(OWNERS // 2,),
        in_specs=[
            pl.BlockSpec(memory_space=pltpu.SMEM),
            pl.BlockSpec((rows, samples), lambda step: (0, 0)),
            pl.BlockSpec((K, samples), lambda step: (0, 0)),
            pl.BlockSpec((1, 2, HALF, 2 * BW), lambda step: (step, 0, 0, 0)),
        ],
        out_specs=pl.BlockSpec((2, K * rows, 2 * BW), lambda step: (step, 0, 0)),
        out_shape=jax.ShapeDtypeStruct((OWNERS, K * rows, 2 * BW), jnp.bfloat16),
        scratch_shapes=[
            pltpu.VMEM((K * rows, HALF), jnp.bfloat16),
            pltpu.VMEM((K * rows, HALF), jnp.bfloat16),
        ],
        compiler_params=pltpu.CompilerParams(vmem_limit_bytes=VMEM_LIMIT),
        cost_estimate=pl.CostEstimate(
            flops=2 * K * rows * HALF * 2 * NF, bytes_accessed=20_000_000, transcendentals=0
        ),
    )(scalars, series, tapers, table)


def pair_kernel(targets, held, scalars, *refs):
    outs = refs[-RING:]
    mine_refs, other_refs = refs[: (len(refs) - RING) // 2], refs[(len(refs) - RING) // 2 : -RING]
    y, core = scalars[0], scalars[1]
    rows = mine_refs[0].shape[1] // K

    def channels(group, at, k):
        source = group[0] if at < held else group[1]
        at = at if at < held else at - held
        piece = source[RING * at : RING * (at + 1), k * rows : (k + 1) * rows, :]
        return piece.reshape(RING * rows, 2 * BW)

    def rotated(spectrum):
        wide = spectrum.astype(jnp.float32)
        half = BW // 2
        parts = []
        for parity in range(2):
            at = parity * BW
            parts += [wide[:, at + half : at + BW], -wide[:, at : at + half]]
        return jnp.concatenate(parts, axis=1).astype(jnp.bfloat16)

    for target in targets:
        total = None
        for k in range(K):
            mine = channels(mine_refs, target, k)
            left = jnp.concatenate([mine, rotated(mine)], axis=0)
            later = [channels(other_refs, target + step, k) for step in range(3)]
            right = jnp.concatenate(
                [
                    channels(mine_refs, target, k),
                    jnp.where(core == 0, later[0], later[1]),
                    channels(mine_refs, target + 1, k),
                    jnp.where(core == 0, later[1], later[2]),
                    channels(mine_refs, target + 2, k),
                ],
                axis=0,
            )
            term = lax.dot_general(
                left, right, (((1,), (1,)), ((), ())), preferred_element_type=jnp.float32
            )
            total = term if total is None else total + term
        total = (total * (1.0 / (K * BW))).astype(jnp.bfloat16)
        distance = lax.rem(target - y + RING, RING)
        for step in range(RING):

            @pl.when(distance == step)
            def _():
                for offset in range(SLOTS):
                    piece = total[:, offset * BW : (offset + 1) * BW]
                    outs[step][offset, 0] = piece[:BW]
                    outs[step][offset, 1] = piece[BW:]


def pair_products(targets, scalars, mine, other):
    held = mine[0].shape[0] // RING
    whole = pl.BlockSpec(memory_space=pltpu.VMEM)
    return pl.pallas_call(
        functools.partial(pair_kernel, targets, held),
        in_specs=[pl.BlockSpec(memory_space=pltpu.SMEM)] + [whole] * (len(mine) + len(other)),
        out_specs=[whole] * RING,
        out_shape=[jax.ShapeDtypeStruct((SLOTS, 2, BW, BW), jnp.bfloat16)] * RING,
        compiler_params=pltpu.CompilerParams(vmem_limit_bytes=VMEM_LIMIT),
        cost_estimate=pl.CostEstimate(
            flops=2 * len(targets) * K * 2 * BW * 2 * BW * SLOTS * BW,
            bytes_accessed=4_000_000,
            transcendentals=0,
        ),
    )(scalars, *mine, *other)


def slots_kernel(scalars, *refs):
    out = refs[-1]
    early, late = refs[:RING], refs[RING : 2 * RING]
    y, count = scalars[0], scalars[1]

    def place(group):
        for distance in range(RING):
            band = lax.rem(y - distance + RING, RING)
            for slot in range(SLOTS):
                live = (slot < count).astype(jnp.float32)
                piece = group[distance][scalars[2 + slot]]
                out[slot, :, band] = piece.astype(jnp.float32) * live

    pl.when(y < RING // 2)(lambda: place(early))
    pl.when(y >= RING // 2)(lambda: place(late))


def slots_output(scalars, early, late):
    whole = pl.BlockSpec(memory_space=pltpu.VMEM)
    return pl.pallas_call(
        slots_kernel,
        in_specs=[pl.BlockSpec(memory_space=pltpu.SMEM)] + [whole] * (2 * RING),
        out_specs=whole,
        out_shape=jax.ShapeDtypeStruct((SLOTS, 2, RING, BW, BW), jnp.float32),
        compiler_params=pltpu.CompilerParams(vmem_limit_bytes=VMEM_LIMIT),
    )(scalars, *early, *late)


def sent_to(targets, pieces):
    moved = [pieces[0]]
    for distance in range(1, RING):
        routes = [((target - distance) % RING, target) for target in targets]
        moved.append(lax.ppermute(pieces[distance], "y", routes))
    return moved


def body(table, series, tapers, live_channels, pair_offset, pair_count):
    x, y, core = lax.axis_index("freq"), lax.axis_index("y"), lax.axis_index("core")
    rows = series.shape[1]
    first = jnp.stack([live_channels[0], x * rows]).astype(jnp.int32)
    spectra = block_spectra(first, series[0], tapers, table)
    mine = lax.all_to_all(spectra, ("y", "freq"), 0, 0)
    swap = [(0, 1), (1, 0)]
    next_plane = [(i, (i - 1) % RING) for i in range(RING)]
    ahead = lax.ppermute(mine[: OWNERS // 2], "z", next_plane)
    other = lax.ppermute(mine, "core", swap)
    place = jnp.stack([y, core]).astype(jnp.int32)
    early = pair_products((0, 1), place, [mine], [other])
    early = sent_to((0, 1), early)
    other_ahead = lax.ppermute(ahead, "core", swap)
    late = pair_products((2, 3), place, [mine, ahead], [other, other_ahead])
    late = sent_to((2, 3), late)
    last = jnp.concatenate([jnp.stack([y, pair_count[0]]), pair_offset[0]]).astype(jnp.int32)
    return slots_output(last, early, late)[None]


def solution(mesh):
    table = half_period_tables()
    grid = Mesh(
        mesh.devices.reshape(RING, RING, RING, 2), ("freq", "z", "y", "core")
    )
    blk = ("z", "y", "core")
    return jax.shard_map(
        functools.partial(body, table),
        mesh=grid,
        in_specs=(P(blk, "freq", None), P(), P(blk), P(blk, None), P(blk)),
        out_specs=P(blk, None, None, "freq", None, None),
        check_vma=False,
    )
```

time: 496 us -> 103 us (0.21)
  other arithmetic: 252 us -> 1.91 us
  local copies, waits for them, and re-layouts: 65.5 us -> 2.05 us
  matrix products: 52.9 us -> 0 us
  waiting for transfers between devices: 79.5 us -> 28.1 us
  Pallas kernels: 0 us -> 25.7 us
  between operations: 11.3 us -> 1.44 us
  starting transfers between devices: 9.77 us -> 16 us
  blocking collectives: 22.1 us -> 27.1 us
    another operation x5 -> x2, other arithmetic: 207 us -> 1.26 us  [the longest x1 0.67 us: body(): place = jnp.stack([y, core]).astype(jnp.int32)]
    dot_general x14 -> x0, matrix products: 52.9 us -> none  [the longest x4 35.4 us: body(): product = jnp.dot(flat_rows, table, preferred_element_type=jnp.float32)]
    ppermute x4 -> x9, waiting for transfers between devices: 79.5 us -> 28.1 us  [the longest x6 13.7 us: sent_to(): moved.append(lax.ppermute(pieces[distance], 'y', routes))]
    concatenate x5 -> x1, other arithmetic: 38.2 us -> 0.65 us  [body(): jnp.concatenate([jnp.stack([y, pair_count[0]]), pair_offset[0]])]
    pallas_call x0 -> x4, Pallas kernels: none -> 25.7 us  [the longest x1 11.4 us: block_spectra(): pl.pallas_call(spectra_kernel, grid=(OWNERS // 2,), in_specs=[pl.BlockSpe...]
    unnamed x78 -> x20, local copies, waits for them, and re-layouts: 27.3 us -> 2.01 us
    all_to_all x2 -> x0, local copies, waits for them, and re-layouts: 12.5 us -> none  [body(): lax.all_to_all(spectra_all, 'freq', split_axis=3, concat_axis=1, tiled=True)]
    dynamic_slice x6 -> x0, local copies, waits for them, and re-layouts: 10.4 us -> none  [body(): partner = lax.dynamic_index_in_dim(stacked, offset, 0, keepdims=False)]
  transfers between devices with their start and end apart: 4 -> 9, of which waited for: 2 -> 4; matrix products, arithmetic and copies ran while one was open for 1% -> 1% of each run, Pallas kernels for 0% -> 5%
where the time goes in v1:
time: 103 us; the launch traced here: 102 us
  waiting for transfers between devices  28.1 us (27%)
  blocking collectives  27.1 us (26%)
  Pallas kernels  25.7 us (25%)
  starting transfers between devices  16 us (16%)
  local copies, waits for them, and re-layouts  2.05 us (2%)
  other arithmetic  1.91 us (2%)
  between operations  1.44 us (1%)
    all_to_all x1, blocking collectives, body(): mine = lax.all_to_all(spectra, ('y', 'freq'), 0, 0)  27.1 us
    ppermute x6, waiting for transfers between devices, sent_to(): moved.append(lax.ppermute(pieces[distance], 'y', routes))  13.7 us
    ppermute x1, waiting for transfers between devices, body(): ahead = lax.ppermute(mine[:OWNERS // 2], 'z', next_plane)  12.9 us
    ppermute x6, starting transfers between devices, sent_to(): moved.append(lax.ppermute(pieces[distance], 'y', routes))  11.9 us
    pallas_call x1, Pallas kernels, block_spectra(): pl.pallas_call(spectra_kernel, grid=(OWNERS // 2,), in_specs=[pl.BlockSpe...  11.4 us
    pallas_call x2, Pallas kernels, pair_products(): pl.pallas_call(functools.partial(pair_kernel, targets, held), in_specs=[p...  10.9 us
    ppermute x1, starting transfers between devices, body(): ahead = lax.ppermute(mine[:OWNERS // 2], 'z', next_plane)  4.1 us
    pallas_call x1, Pallas kernels, slots_output(): pl.pallas_call(slots_kernel, in_specs=[pl.BlockSpec(memory_space=pltpu.SM...  3.35 us
  transfers between devices with their start and end apart: 9, of which 4 were waited for; matrix products, arithmetic and copies ran while one was open for 1% of the time, Pallas kernels for 5%

profile of v1, /device:TPU:0, one launch (start us, length us, event | category | flops | bytes accessed | tf_op | source)
XLA Modules:
  0.0 102.3 jit_solution(18210595706963409779)
XLA Ops:
  0.7 0.6 pad_add_fusion.2.scalars
  1.2 11.4 %shard_map.64 = bf16[16,160,256]{2,1,0:T(8,128)(2,1)} custom-call(s32[2]{0:T(128)} %pad_add_fusion.2.scalars, bf16[32,6000]{1,0:T(8,128)(2,1)} %bitcast.6, f32[5,6000]{1,0:T(8,128)} %tapers.1, bf16[8,2,2048,256]{3,2,1,0:T(8,128)(2,1)} %constant.16.clone.table), custom_call_target="tpu_custom_call" | custom-call | flops 2684354560 | bytes 20000000 | tf_op jit(solution)/shard_map/pallas_call | solution.py:75
  12.6 27.1 %all_to_all.5.refs_0_ = bf16[16,160,256]{2,1,0:T(8,128)(2,1)S(1)} all-to-all(bf16[16,160,256]{2,1,0:T(8,128)(2,1)} %shard_map.64), channel_id=1, replica_groups=mesh['freq'=4,'z'=4,'y'=4,'core'=2] {'y','freq'}, dimensions={0} | all-to-all | bytes 2621440 | tf_op jit(solution)/shard_map/all_to_all | solution.py:208
  39.8 4.1 %collective-permute-start.4 = (bf16[8,160,256]{2,1,0:T(8,128)(2,1)S(1)}, bf16[8,160,256]{2,1,0:T(8,128)(2,1)S(1)}, u32[]{:S(2)}, u32[]{:S(2)}) collective-permute-start(bf16[8,160,256]{2,1,0:T(8,128)(2,1)S(1)} %slice.4), channel_id=1, source_target_pairs={{0,24},{8,0},{16,8},{24,16},{1,25},{9,1},{17,9},{25,17},{2,26},{10... | collective-permute-start | bytes 1966088 | tf_op jit(solution)/shard_map/ppermute | solution.py:211
  43.9 12.9 %collective-permute-done.4.refs_1_ = bf16[8,160,256]{2,1,0:T(8,128)(2,1)S(1)} collective-permute-done((bf16[8,160,256]{2,1,0:T(8,128)(2,1)S(1)}, bf16[8,160,256]{2,1,0:T(8,128)(2,1)S(1)}, u32[]{:S(2)}, u32[]{:S(2)}) %collective-permute-start.4) | collective-permute-done | bytes 655392 | tf_op jit(solution)/shard_map/ppermute | solution.py:211
  56.7 0.7 pad_add_fusion.1.scalars
  57.4 1.6 %collective-permute-done.5.refs_3_ = bf16[8,160,256]{2,1,0:T(8,128)(2,1)} collective-permute-done((bf16[8,160,256]{2,1,0:T(8,128)(2,1)S(1)}, bf16[8,160,256]{2,1,0:T(8,128)(2,1)}, u32[]{:S(2)}, u32[]{:S(2)}) %collective-permute-start.5) | collective-permute-done | bytes 655392 | tf_op jit(solution)/shard_map/ppermute | solution.py:216
  59.0 1.1 %copy-done.1 = bf16[16,160,256]{2,1,0:T(8,128)(2,1)} copy-done((bf16[16,160,256]{2,1,0:T(8,128)(2,1)}, bf16[16,160,256]{2,1,0:T(8,128)(2,1)S(1)}, u32[]{:S(2)}) %copy-start.1) | copy-done | bytes 1310744
  60.1 5.6 %shard_map.66 = (bf16[5,2,128,128]{3,2,1,0:T(8,128)(2,1)}, bf16[5,2,128,128]{3,2,1,0:T(8,128)(2,1)}, bf16[5,2,128,128]{3,2,1,0:T(8,128)(2,1)}, bf16[5,2,128,128]{3,2,1,0:T(8,128)(2,1)}) custom-call(s32[2]{0:T(128)} %pad_add_fusion.1.scalars, bf16[16,160,256]{2,1,0:T(8,128)(2,1)} %copy-done, bf16[8,160,256]{2,1,0:T(8,128)(2,1)} %copy-done.2, ...), custom_call_target="tpu_custom_call" | custom-call | flops 838860800 | bytes 4000000 | tf_op jit(solution)/shard_map/pallas_call | solution.py:153
  65.7 0.7 collective-permute-start.6
  66.4 5.4 %collective-permute-start.7 = (bf16[5,2,128,128]{3,2,1,0:T(8,128)(2,1)}, bf16[5,2,128,128]{3,2,1,0:T(8,128)(2,1)S(1)}, u32[]{:S(2)}, u32[]{:S(2)}) collective-permute-start(bf16[5,2,128,128]{3,2,1,0:T(8,128)(2,1)} %get-tuple-element.19), channel_id=1, source_target_pairs={{0,4},{2,6},{1,5},{3,7},{8,12},{10,14},{9,13},{11,15},{16,20},{18,... | collective-permute-start | bytes 983048 | tf_op jit(solution)/shard_map/ppermute | solution.py:199
  71.8 0.0 copy-start.9
  71.8 1.3 %collective-permute-start.8 = (bf16[5,2,128,128]{3,2,1,0:T(8,128)(2,1)}, bf16[5,2,128,128]{3,2,1,0:T(8,128)(2,1)S(1)}, u32[]{:S(2)}, u32[]{:S(2)}) collective-permute-start(bf16[5,2,128,128]{3,2,1,0:T(8,128)(2,1)} %get-tuple-element.20), channel_id=1, source_target_pairs={{6,4},{0,6},{7,5},{1,7},{14,12},{8,14},{15,13},{9,15},{22,20},{16,... | collective-permute-start | bytes 983048 | tf_op jit(solution)/shard_map/ppermute | solution.py:199
  73.2 5.3 %shard_map.65 = (bf16[5,2,128,128]{3,2,1,0:T(8,128)(2,1)}, bf16[5,2,128,128]{3,2,1,0:T(8,128)(2,1)}, bf16[5,2,128,128]{3,2,1,0:T(8,128)(2,1)}, bf16[5,2,128,128]{3,2,1,0:T(8,128)(2,1)}) custom-call(s32[2]{0:T(128)} %pad_add_fusion.1.scalars, bf16[16,160,256]{2,1,0:T(8,128)(2,1)} %copy-done, bf16[16,160,256]{2,1,0:T(8,128)(2,1)} %copy-done.1), custom_call_target="tpu_custom_call" | custom-call | flops 838860800 | bytes 4000000 | tf_op jit(solution)/shard_map/pallas_call | solution.py:153
  78.5 1.9 %collective-permute-start.1 = (bf16[5,2,128,128]{3,2,1,0:T(8,128)(2,1)}, bf16[5,2,128,128]{3,2,1,0:T(8,128)(2,1)S(1)}, u32[]{:S(2)}, u32[]{:S(2)}) collective-permute-start(bf16[5,2,128,128]{3,2,1,0:T(8,128)(2,1)} %get-tuple-element.14), channel_id=1, source_target_pairs={{6,0},{0,2},{7,1},{1,3},{14,8},{8,10},{15,9},{9,11},{22,16},{16,18... | collective-permute-start | bytes 983048 | tf_op jit(solution)/shard_map/ppermute | solution.py:199
  80.4 1.3 %collective-permute-start.2 = (bf16[5,2,128,128]{3,2,1,0:T(8,128)(2,1)}, bf16[5,2,128,128]{3,2,1,0:T(8,128)(2,1)S(1)}, u32[]{:S(2)}, u32[]{:S(2)}) collective-permute-start(bf16[5,2,128,128]{3,2,1,0:T(8,128)(2,1)} %get-tuple-element.15), channel_id=1, source_target_pairs={{4,0},{6,2},{5,1},{7,3},{12,8},{14,10},{13,9},{15,11},{20,16},{22,... | collective-permute-start | bytes 983048 | tf_op jit(solution)/shard_map/ppermute | solution.py:199
  81.7 1.3 %collective-permute-start.3 = (bf16[5,2,128,128]{3,2,1,0:T(8,128)(2,1)}, bf16[5,2,128,128]{3,2,1,0:T(8,128)(2,1)S(1)}, u32[]{:S(2)}, u32[]{:S(2)}) collective-permute-start(bf16[5,2,128,128]{3,2,1,0:T(8,128)(2,1)} %get-tuple-element.16), channel_id=1, source_target_pairs={{2,0},{4,2},{3,1},{5,3},{10,8},{12,10},{11,9},{13,11},{18,16},{20,... | collective-permute-start | bytes 983048 | tf_op jit(solution)/shard_map/ppermute | solution.py:199
  83.7 0.7 pad_add_fusion.scalars
  84.3 0.3 collective-permute-done.8.refs_7_
  84.6 13.4 %collective-permute-done.1.refs_1_ = bf16[5,2,128,128]{3,2,1,0:T(8,128)(2,1)S(1)} collective-permute-done((bf16[5,2,128,128]{3,2,1,0:T(8,128)(2,1)}, bf16[5,2,128,128]{3,2,1,0:T(8,128)(2,1)S(1)}, u32[]{:S(2)}, u32[]{:S(2)}) %collective-permute-start.1) | collective-permute-done | bytes 327712 | tf_op jit(solution)/shard_map/ppermute | solution.py:199
  98.0 0.7 copy-done.6
  98.7 0.1 copy-done.7
  98.8 0.1 copy-done.8
  98.9 3.4 %shard_map.67 = f32[5,2,4,128,128]{4,3,2,1,0:T(8,128)} custom-call(s32[7]{0:T(128)} %pad_add_fusion.scalars, bf16[5,2,128,128]{3,2,1,0:T(8,128)(2,1)} %get-tuple-element.13.refs_0_, bf16[5,2,128,128]{3,2,1,0:T(8,128)(2,1)} %copy-done.6, bf16[5,2,128,128]{3,2,1,0:T(8,128)(2,1)} %copy-done.7, bf16[5,2,128,128]{3,2,1,0:T(8,128)(2,1)} %copy-done.8, ...), custom_call_target="tpu_custom_call" | custom-call | tf_op jit(solution)/shard_map/pallas_call | solution.py:186
  (23 shorter events, 0.1 us)
Async XLA Ops:
  39.7 19.3 %copy-start = (bf16[16,160,256]{2,1,0:T(8,128)(2,1)}, bf16[16,160,256]{2,1,0:T(8,128)(2,1)S(1)}, u32[]{:S(2)}) copy-start(bf16[16,160,256]{2,1,0:T(8,128)(2,1)S(1)} %all_to_all.5.refs_0_) | copy-start | bytes 3932164
  39.8 17.0 %collective-permute-start.4 = (bf16[8,160,256]{2,1,0:T(8,128)(2,1)S(1)}, bf16[8,160,256]{2,1,0:T(8,128)(2,1)S(1)}, u32[]{:S(2)}, u32[]{:S(2)}) collective-permute-start(bf16[8,160,256]{2,1,0:T(8,128)(2,1)S(1)} %slice.4), channel_id=1, source_target_pairs={{0,24},{8,0},{16,8},{24,16},{1,25},{9,1},{17,9},{25,17},{2,26},{10... | collective-permute-start | bytes 1966088 | tf_op jit(solution)/shard_map/ppermute | solution.py:211
  43.9 15.1 %collective-permute-start = (bf16[16,160,256]{2,1,0:T(8,128)(2,1)S(1)}, bf16[16,160,256]{2,1,0:T(8,128)(2,1)S(1)}, u32[]{:S(2)}, u32[]{:S(2)}) collective-permute-start(bf16[16,160,256]{2,1,0:T(8,128)(2,1)S(1)} %all_to_all.5.refs_0_), channel_id=1, source_target_pairs={{0,1},{1,0},{2,3},{3,2},{4,5},{5,4},{6,7},{7,6},{8,9},{9,8},{10,11... | collective-permute-start | bytes 3932168 | tf_op jit(solution)/shard_map/ppermute | solution.py:212
  56.7 2.2 %copy-start.2 = (bf16[8,160,256]{2,1,0:T(8,128)(2,1)}, bf16[8,160,256]{2,1,0:T(8,128)(2,1)S(1)}, u32[]{:S(2)}) copy-start(bf16[8,160,256]{2,1,0:T(8,128)(2,1)S(1)} %collective-permute-done.4.refs_1_) | copy-start | bytes 1966084
  56.7 2.2 %collective-permute-start.5 = (bf16[8,160,256]{2,1,0:T(8,128)(2,1)S(1)}, bf16[8,160,256]{2,1,0:T(8,128)(2,1)}, u32[]{:S(2)}, u32[]{:S(2)}) collective-permute-start(bf16[8,160,256]{2,1,0:T(8,128)(2,1)S(1)} %collective-permute-done.4.refs_1_), channel_id=1, source_target_pairs={{0,1},{1,0},{2,3},{3,2},{4,5},{5,4},{6,7},{7,6},{8,9},{9,8},{10,11... | collective-permute-start | bytes 1966088 | tf_op jit(solution)/shard_map/ppermute | solution.py:216
  59.0 1.1 %copy-start.1 = (bf16[16,160,256]{2,1,0:T(8,128)(2,1)}, bf16[16,160,256]{2,1,0:T(8,128)(2,1)S(1)}, u32[]{:S(2)}) copy-start(bf16[16,160,256]{2,1,0:T(8,128)(2,1)S(1)} %collective-permute-done.refs_1_.refs_2_) | copy-start | bytes 3932164
  65.7 16.0 %collective-permute-start.6 = (bf16[5,2,128,128]{3,2,1,0:T(8,128)(2,1)}, bf16[5,2,128,128]{3,2,1,0:T(8,128)(2,1)S(1)}, u32[]{:S(2)}, u32[]{:S(2)}) collective-permute-start(bf16[5,2,128,128]{3,2,1,0:T(8,128)(2,1)} %get-tuple-element.18), channel_id=1, source_target_pairs={{2,4},{4,6},{3,5},{5,7},{10,12},{12,14},{11,13},{13,15},{18,20},{2... | collective-permute-start | bytes 983048 | tf_op jit(solution)/shard_map/ppermute | solution.py:199
  66.4 17.9 %collective-permute-start.7 = (bf16[5,2,128,128]{3,2,1,0:T(8,128)(2,1)}, bf16[5,2,128,128]{3,2,1,0:T(8,128)(2,1)S(1)}, u32[]{:S(2)}, u32[]{:S(2)}) collective-permute-start(bf16[5,2,128,128]{3,2,1,0:T(8,128)(2,1)} %get-tuple-element.19), channel_id=1, source_target_pairs={{0,4},{2,6},{1,5},{3,7},{8,12},{10,14},{9,13},{11,15},{16,20},{18,... | collective-permute-start | bytes 983048 | tf_op jit(solution)/shard_map/ppermute | solution.py:199
  71.8 11.8 %copy-start.9 = (s32[1,5]{1,0:T(1,128)S(1)}, s32[1,5]{1,0:T(1,128)}, u32[]{:S(2)}) copy-start(s32[1,5]{1,0:T(1,128)} %param.9) | copy-start | bytes 64
  71.8 12.8 %collective-permute-start.8 = (bf16[5,2,128,128]{3,2,1,0:T(8,128)(2,1)}, bf16[5,2,128,128]{3,2,1,0:T(8,128)(2,1)S(1)}, u32[]{:S(2)}, u32[]{:S(2)}) collective-permute-start(bf16[5,2,128,128]{3,2,1,0:T(8,128)(2,1)} %get-tuple-element.20), channel_id=1, source_target_pairs={{6,4},{0,6},{7,5},{1,7},{14,12},{8,14},{15,13},{9,15},{22,20},{16,... | collective-permute-start | bytes 983048 | tf_op jit(solution)/shard_map/ppermute | solution.py:199
  78.5 19.5 %collective-permute-start.1 = (bf16[5,2,128,128]{3,2,1,0:T(8,128)(2,1)}, bf16[5,2,128,128]{3,2,1,0:T(8,128)(2,1)S(1)}, u32[]{:S(2)}, u32[]{:S(2)}) collective-permute-start(bf16[5,2,128,128]{3,2,1,0:T(8,128)(2,1)} %get-tuple-element.14), channel_id=1, source_target_pairs={{6,0},{0,2},{7,1},{1,3},{14,8},{8,10},{15,9},{9,11},{22,16},{16,18... | collective-permute-start | bytes 983048 | tf_op jit(solution)/shard_map/ppermute | solution.py:199
  80.4 17.6 %collective-permute-start.2 = (bf16[5,2,128,128]{3,2,1,0:T(8,128)(2,1)}, bf16[5,2,128,128]{3,2,1,0:T(8,128)(2,1)S(1)}, u32[]{:S(2)}, u32[]{:S(2)}) collective-permute-start(bf16[5,2,128,128]{3,2,1,0:T(8,128)(2,1)} %get-tuple-element.15), channel_id=1, source_target_pairs={{4,0},{6,2},{5,1},{7,3},{12,8},{14,10},{13,9},{15,11},{20,16},{22,... | collective-permute-start | bytes 983048 | tf_op jit(solution)/shard_map/ppermute | solution.py:199
  81.7 16.3 %copy-start.3 = (bf16[5,2,128,128]{3,2,1,0:T(8,128)(2,1)}, bf16[5,2,128,128]{3,2,1,0:T(8,128)(2,1)S(1)}, u32[]{:S(2)}) copy-start(bf16[5,2,128,128]{3,2,1,0:T(8,128)(2,1)S(1)} %collective-permute-done.6.refs_5_) | copy-start | bytes 983044
  81.7 16.3 %collective-permute-start.3 = (bf16[5,2,128,128]{3,2,1,0:T(8,128)(2,1)}, bf16[5,2,128,128]{3,2,1,0:T(8,128)(2,1)S(1)}, u32[]{:S(2)}, u32[]{:S(2)}) collective-permute-start(bf16[5,2,128,128]{3,2,1,0:T(8,128)(2,1)} %get-tuple-element.16), channel_id=1, source_target_pairs={{2,0},{4,2},{3,1},{5,3},{10,8},{12,10},{11,9},{13,11},{18,16},{20,... | collective-permute-start | bytes 983048 | tf_op jit(solution)/shard_map/ppermute | solution.py:199
  84.3 13.7 %copy-start.4 = (bf16[5,2,128,128]{3,2,1,0:T(8,128)(2,1)}, bf16[5,2,128,128]{3,2,1,0:T(8,128)(2,1)S(1)}, u32[]{:S(2)}) copy-start(bf16[5,2,128,128]{3,2,1,0:T(8,128)(2,1)S(1)} %collective-permute-done.7.refs_6_) | copy-start | bytes 983044
  84.6 13.4 %copy-start.5 = (bf16[5,2,128,128]{3,2,1,0:T(8,128)(2,1)}, bf16[5,2,128,128]{3,2,1,0:T(8,128)(2,1)S(1)}, u32[]{:S(2)}) copy-start(bf16[5,2,128,128]{3,2,1,0:T(8,128)(2,1)S(1)} %collective-permute-done.8.refs_7_) | copy-start | bytes 983044
  98.0 0.7 copy-start.6
  98.0 0.8 copy-start.7
  98.0 0.9 copy-start.8

commit v2 on v1

v2 whole, which is shorter than its diff:
```python
import functools

import jax
import jax.numpy as jnp
import ml_dtypes
import numpy as np
from jax import lax
from jax.experimental import pallas as pl
from jax.experimental.pallas import tpu as pltpu
from jax.sharding import Mesh
from jax.sharding import PartitionSpec as P

NF = 2048
K = 5
BW = 128
PERIOD = 2 * NF
HALF = PERIOD // 2
SLOTS = 5
RING = 4
OWNERS = RING * RING
VMEM_LIMIT = 24 * 1024 * 1024
STREAM_VMEM_LIMIT = 56 * 1024 * 1024


def half_period_tables():
    samples = np.arange(HALF, dtype=np.int64)
    bins = np.stack(
        [
            np.concatenate(
                [(RING * (owner % RING) + owner // RING) * BW + 2 * np.arange(BW // 2) + parity
                 for owner in range(OWNERS)]
            )
            for parity in range(2)
        ]
    )
    angle = ((samples[None, :, None] * bins[:, None, :]) % PERIOD) * (2.0 * np.pi / PERIOD)
    parts = np.stack([np.cos(angle), -np.sin(angle)], axis=2)
    parts = parts.reshape(2, HALF, 2, OWNERS, BW // 2).transpose(3, 0, 1, 2, 4)
    parts = parts.reshape(OWNERS // 2, 2, 2, HALF, BW).transpose(0, 2, 3, 1, 4)
    return parts.reshape(OWNERS // 2, 2, HALF, 2 * BW).astype(ml_dtypes.bfloat16)


def spectra_kernel(live_counts, series, tapers, table, out, even, odd):
    rows, samples = series.shape

    @pl.when(pl.program_id(0) == 0)
    def _():
        live, first = live_counts[0], lax.axis_index("freq") * rows
        channel = first + lax.broadcasted_iota(jnp.int32, (rows, HALF), 0)
        working = channel < live

        def tapered(k, begin, end):
            product = series[:, begin:end].astype(jnp.float32) * tapers[k : k + 1, begin:end]
            if end - begin < HALF:
                product = jnp.concatenate(
                    [product, jnp.zeros((rows, HALF - (end - begin)), jnp.float32)], axis=1
                )
            product = jnp.where(working, product, 0.0)
            return product.astype(jnp.bfloat16).astype(jnp.float32)

        for k in range(K):
            ends = tapered(k, 0, HALF) + tapered(k, 2 * HALF, samples)
            middle = tapered(k, HALF, 2 * HALF)
            even[k * rows : (k + 1) * rows, :] = (ends + middle).astype(jnp.bfloat16)
            odd[k * rows : (k + 1) * rows, :] = (ends - middle).astype(jnp.bfloat16)

    for parity, folded in enumerate((even, odd)):
        bins = jnp.dot(folded[...], table[0, parity], preferred_element_type=jnp.float32)
        bins = bins.astype(jnp.bfloat16)
        out[0, :, parity * BW : (parity + 1) * BW] = bins[:, :BW]
        out[1, :, parity * BW : (parity + 1) * BW] = bins[:, BW:]


def block_spectra(live_counts, series, tapers, table):
    rows, samples = series.shape
    return pl.pallas_call(
        spectra_kernel,
        grid=(OWNERS // 2,),
        in_specs=[
            pl.BlockSpec(memory_space=pltpu.SMEM),
            pl.BlockSpec((rows, samples), lambda step: (0, 0)),
            pl.BlockSpec((K, samples), lambda step: (0, 0)),
            pl.BlockSpec((1, 2, HALF, 2 * BW), lambda step: (step, 0, 0, 0)),
        ],
        out_specs=pl.BlockSpec((2, K * rows, 2 * BW), lambda step: (step, 0, 0)),
        out_shape=jax.ShapeDtypeStruct((OWNERS, K * rows, 2 * BW), jnp.bfloat16),
        scratch_shapes=[
            pltpu.VMEM((K * rows, HALF), jnp.bfloat16),
            pltpu.VMEM((K * rows, HALF), jnp.bfloat16),
        ],
        compiler_params=pltpu.CompilerParams(vmem_limit_bytes=STREAM_VMEM_LIMIT),
        cost_estimate=pl.CostEstimate(
            flops=2 * K * rows * HALF * 2 * NF, bytes_accessed=20_000_000, transcendentals=0
        ),
    )(live_counts, series, tapers, table)


def pair_kernel(wanted, *refs):
    later, mine_wide, other_wide = refs[-3:]
    outs = refs[-3 - RING : -3]
    inputs = refs[: -3 - RING]
    y, core = lax.axis_index("y"), lax.axis_index("core")
    rows = inputs[0].shape[1] // K
    half = BW // 2
    first = min(wanted)

    def channels(group, at, k):
        for source in group:
            if at < source.shape[0] // RING:
                piece = source[RING * at : RING * (at + 1), k * rows : (k + 1) * rows, :]
                return piece.reshape(RING * rows, 2 * BW)
            at -= source.shape[0] // RING

    def widened(group, wide, blocks):
        for block in blocks:
            to = (block - first) * BW
            for k in range(K):
                wide[to : to + BW, k * 2 * BW : (k + 1) * 2 * BW] = channels(group, block, k)

    same_of, crossed_of = {}, {}
    for target, offsets in wanted.items():
        same_of[target] = [target + offset // 2 for offset in offsets if offset % 2 == 0]
        crossed_of[target] = [target + offset // 2 for offset in offsets if offset % 2 == 1]
    same_blocks = set(wanted).union(*same_of.values())
    crossed_blocks = set().union(*crossed_of.values())
    widened(inputs[: len(inputs) // 2], mine_wide, sorted(same_blocks))
    widened(
        inputs[len(inputs) // 2 :],
        other_wide,
        sorted(crossed_blocks | {block + 1 for block in crossed_blocks}),
    )

    contract = (((1,), (1,)), ((), ()))
    for target, offsets in wanted.items():
        to = (target - first) * BW
        later[:BW, :] = mine_wide[to : to + BW, :]
        for part in range(2 * K):
            at = part * BW
            wide = mine_wide[to : to + BW, at : at + BW].astype(jnp.float32)
            turned = jnp.concatenate([wide[:, half:], -wide[:, :half]], axis=1)
            later[BW:, at : at + BW] = turned.astype(jnp.bfloat16)
        same, crossed = same_of[target], crossed_of[target]
        at = (same[0] - first) * BW
        partners = mine_wide[at : at + len(same) * BW, :]
        even = lax.dot_general(later[...], partners, contract, preferred_element_type=jnp.float32)
        even = (even * (1.0 / (K * BW))).astype(jnp.bfloat16)
        if crossed:
            at = pl.multiple_of((crossed[0] - first + core) * BW, BW)
            partners = other_wide[pl.ds(at, len(crossed) * BW), :]
            odd = lax.dot_general(
                later[...], partners, contract, preferred_element_type=jnp.float32
            )
            odd = (odd * (1.0 / (K * BW))).astype(jnp.bfloat16)
        distance = lax.rem(target - y + RING, RING)
        for step in range(RING):

            @pl.when(distance == step)
            def _():
                for at, offset in enumerate(offsets):
                    group, kind = (even, same) if offset % 2 == 0 else (odd, crossed)
                    column = kind.index(target + offset // 2) * BW
                    piece = group[:, column : column + BW]
                    outs[step][at, 0] = piece[:BW]
                    outs[step][at, 1] = piece[BW:]


def pair_products(wanted, mine, other):
    pairs = max(len(offsets) for offsets in wanted.values())
    reach = sum(block.shape[0] // RING for block in mine) - min(wanted)
    whole = pl.BlockSpec(memory_space=pltpu.VMEM)
    return pl.pallas_call(
        functools.partial(pair_kernel, wanted),
        in_specs=[whole] * (len(mine) + len(other)),
        out_specs=[whole] * RING,
        out_shape=[jax.ShapeDtypeStruct((pairs, 2, BW, BW), jnp.bfloat16)] * RING,
        scratch_shapes=[
            pltpu.VMEM((2 * BW, K * 2 * BW), jnp.bfloat16),
            pltpu.VMEM((reach * BW, K * 2 * BW), jnp.bfloat16),
            pltpu.VMEM((reach * BW, K * 2 * BW), jnp.bfloat16),
        ],
        compiler_params=pltpu.CompilerParams(vmem_limit_bytes=VMEM_LIMIT),
        cost_estimate=pl.CostEstimate(flops=1, bytes_accessed=1, transcendentals=0),
    )(*mine, *other)


PLANE = {0: (0, 1, 2), 1: (0, 1, 2), 2: (0, 1, 2), 3: (0,)}
NEAR = {0: (3, 4), 1: (3, 4), 2: (3, 4), 3: (1, 2)}
FAR = {3: (3, 4)}


def slots_kernel(offsets, counts, *refs):
    out = refs[-1]
    y, count = lax.axis_index("y"), counts[0]
    parts = [refs[at * RING : (at + 1) * RING] for at in range(3)]

    def place(target):
        for group, wanted in zip(parts, (PLANE, NEAR, FAR)):
            for at, offset in enumerate(wanted.get(target, ())):
                slot = 0
                for step in range(1, SLOTS):
                    slot += jnp.where(offsets[0, step] == offset, step, 0)
                live = (slot < count).astype(jnp.float32)
                for distance in range(RING):
                    band = (target - distance) % RING
                    out[slot, :, band] = group[distance][at].astype(jnp.float32) * live

    for target in range(RING):
        pl.when(y == target)(functools.partial(place, target))


def slots_output(offsets, counts, parts):
    whole = pl.BlockSpec(memory_space=pltpu.VMEM)
    return pl.pallas_call(
        slots_kernel,
        in_specs=[pl.BlockSpec(memory_space=pltpu.SMEM)] * 2 + [whole] * (3 * RING),
        out_specs=whole,
        out_shape=jax.ShapeDtypeStruct((SLOTS, 2, RING, BW, BW), jnp.float32),
        compiler_params=pltpu.CompilerParams(vmem_limit_bytes=VMEM_LIMIT),
    )(offsets, counts, *parts)


def sent_to(targets, pieces):
    moved = [pieces[0]]
    for distance in range(1, RING):
        routes = [((target - distance) % RING, target) for target in targets]
        moved.append(lax.ppermute(pieces[distance], "y", routes))
    return moved


def body(table, series, tapers, live_channels, pair_offset, pair_count):
    swap = [(0, 1), (1, 0)]
    next_plane = [(i, (i - 1) % RING) for i in range(RING)]
    spectra = block_spectra(live_channels, series[0], tapers, table)
    mine = lax.all_to_all(spectra, ("y", "freq"), 0, 0)
    near = lax.ppermute(mine[:RING], "z", next_plane)
    far = lax.ppermute(mine[RING : 2 * RING], "z", next_plane)
    other = lax.ppermute(mine, "core", swap)
    plane = pair_products(PLANE, [mine], [other])
    near, _ = lax.optimization_barrier((near, plane[0]))
    plane = sent_to(PLANE, plane)
    other_near = lax.ppermute(near, "core", swap)
    close = pair_products(NEAR, [mine, near], [other, other_near])
    far, _ = lax.optimization_barrier((far, close[0]))
    close, plane = lax.optimization_barrier((close, plane))
    close = sent_to(NEAR, close)
    other_far = lax.ppermute(far, "core", swap)
    last = pair_products(FAR, [mine, near, far], [other, other_near, other_far])
    last = sent_to(FAR, last)
    parts = plane + close + last
    return slots_output(pair_offset, pair_count, parts)[None]


def solution(mesh):
    table = half_period_tables()
    grid = Mesh(
        mesh.devices.reshape(RING, RING, RING, 2), ("freq", "z", "y", "core")
    )
    blk = ("z", "y", "core")
    return jax.shard_map(
        functools.partial(body, table),
        mesh=grid,
        in_specs=(P(blk, "freq", None), P(), P(blk), P(blk, None), P(blk)),
        out_specs=P(blk, None, None, "freq", None, None),
        check_vma=False,
    )
```

time: 103 us -> 84.7 us (0.82)
  waiting for transfers between devices: 28.1 us -> 15.9 us
  Pallas kernels: 25.7 us -> 19 us
  starting transfers between devices: 16 us -> 20.3 us
  local copies, waits for them, and re-layouts: 2.05 us -> 0.05 us
  other arithmetic: 1.91 us -> 0 us
    ppermute x2 -> x4, waiting for transfers between devices: 14.4 us -> 6.94 us  [the longest x1 5.17 us: body(): near = lax.ppermute(mine[:RING], 'z', next_plane)]
    pallas_call x2 -> x3, Pallas kernels: 10.9 us -> 5.42 us  [pair_products(): pl.pallas_call(functools.partial(pair_kernel, wanted), in_specs=[whole] *...]
    ppermute x6 -> x9, waiting for transfers between devices: 13.7 us -> 9.01 us  [sent_to(): moved.append(lax.ppermute(pieces[distance], 'y', routes))]
    ppermute x2 -> x4, starting transfers between devices: 4.11 us -> 7.8 us  [the longest x1 4.1 us: body(): near = lax.ppermute(mine[:RING], 'z', next_plane)]
    unnamed x20 -> x2, local copies, waits for them, and re-layouts: 2.01 us -> 0.01 us
    another operation x2 -> x0, other arithmetic: 1.26 us -> none  [the longest x1 0.67 us: body(): place = jnp.stack([y, core]).astype(jnp.int32)]
    pallas_call x1, Pallas kernels: 3.35 us -> 2.24 us  [slots_output(): pl.pallas_call(slots_kernel, in_specs=[pl.BlockSpec(memory_space=pltpu.SM...]
    ppermute x6 -> x9, starting transfers between devices: 11.9 us -> 12.5 us  [sent_to(): moved.append(lax.ppermute(pieces[distance], 'y', routes))]
  transfers between devices with their start and end apart: 9 -> 14, of which waited for: 4 -> 6; matrix products, arithmetic and copies ran while one was open for 1% -> 0% of each run, Pallas kernels for 5% -> 6%
where the time goes in v2:
time: 84.7 us; the launch traced here: 83.8 us
  blocking collectives  27.1 us (32%)
  starting transfers between devices  20.3 us (24%)
  Pallas kernels  19 us (22%)
  waiting for transfers between devices  15.9 us (19%)
  between operations  1.4 us (2%)
    all_to_all x1, blocking collectives, body(): mine = lax.all_to_all(spectra, ('y', 'freq'), 0, 0)  27.1 us
    ppermute x9, starting transfers between devices, sent_to(): moved.append(lax.ppermute(pieces[distance], 'y', routes))  12.5 us
    pallas_call x1, Pallas kernels, block_spectra(): pl.pallas_call(spectra_kernel, grid=(OWNERS // 2,), in_specs=[pl.BlockSpe...  11.3 us
    ppermute x9, waiting for transfers between devices, sent_to(): moved.append(lax.ppermute(pieces[distance], 'y', routes))  9.01 us
    pallas_call x3, Pallas kernels, pair_products(): pl.pallas_call(functools.partial(pair_kernel, wanted), in_specs=[whole] *...  5.42 us
    ppermute x1, waiting for transfers between devices, body(): near = lax.ppermute(mine[:RING], 'z', next_plane)  5.17 us
    ppermute x1, starting transfers between devices, body(): near = lax.ppermute(mine[:RING], 'z', next_plane)  4.1 us
    ppermute x1, starting transfers between devices, body(): far = lax.ppermute(mine[RING:2 * RING], 'z', next_plane)  3.69 us
  transfers between devices with their start and end apart: 14, of which 6 were waited for; matrix products, arithmetic and copies ran while one was open for 0% of the time, Pallas kernels for 6%

profile of v2, /device:TPU:0, one launch (start us, length us, event | category | flops | bytes accessed | tf_op | source)
XLA Modules:
  0.0 83.8 jit_solution(8118410065180983320)
XLA Ops:
  0.7 11.3 %shard_map.64 = bf16[16,160,256]{2,1,0:T(8,128)(2,1)} custom-call(s32[1]{0:T(128)S(6)} %copy.7.live_counts, bf16[32,6000]{1,0:T(8,128)(2,1)} %bitcast.2, f32[5,6000]{1,0:T(8,128)} %tapers.1, bf16[8,2,2048,256]{3,2,1,0:T(8,128)(2,1)} %constant.2.clone.table), custom_call_target="tpu_custom_call" | custom-call | flops 2684354560 | bytes 20000000 | tf_op jit(solution)/shard_map/pallas_call | solution.py:76
  12.0 27.1 %all_to_all.5.refs_0_ = bf16[16,160,256]{2,1,0:T(8,128)(2,1)S(1)} all-to-all(bf16[16,160,256]{2,1,0:T(8,128)(2,1)} %shard_map.64), channel_id=1, replica_groups=mesh['freq'=4,'z'=4,'y'=4,'core'=2] {'y','freq'}, dimensions={0} | all-to-all | bytes 2621440 | tf_op jit(solution)/shard_map/all_to_all | solution.py:234
  39.1 4.1 %collective-permute-start = (bf16[4,160,256]{2,1,0:T(8,128)(2,1)S(1)}, bf16[4,160,256]{2,1,0:T(8,128)(2,1)S(1)}, u32[]{:S(2)}, u32[]{:S(2)}) collective-permute-start(bf16[4,160,256]{2,1,0:T(8,128)(2,1)S(1)} %get-tuple-element.50), channel_id=1, source_target_pairs={{0,24},{8,0},{16,8},{24,16},{1,25},{9,1},{17,9},{25,17},{2,26},{10... | collective-permute-start | bytes 983048 | tf_op jit(solution)/shard_map/ppermute | solution.py:235
  43.2 2.5 %shard_map.65 = (bf16[3,2,128,128]{3,2,1,0:T(8,128)(2,1)S(1)}, bf16[3,2,128,128]{3,2,1,0:T(8,128)(2,1)S(1)}, bf16[3,2,128,128]{3,2,1,0:T(8,128)(2,1)S(1)}, bf16[3,2,128,128]{3,2,1,0:T(8,128)(2,1)S(1)}) custom-call(bf16[16,160,256]{2,1,0:T(8,128)(2,1)S(1)} %all_to_all.5.refs_0_, bf16[16,160,256]{2,1,0:T(8,128)(2,1)S(1)} %collective-permute-done.1.refs_1_.refs_2_.refs_3_), custom_call_target="tpu_custom_call" | custom-call | flops 1 | bytes 1 | tf_op jit(solution)/shard_map/pallas_call | solution.py:171
  45.7 5.2 %collective-permute-done.refs_1_ = bf16[4,160,256]{2,1,0:T(8,128)(2,1)S(1)} collective-permute-done((bf16[4,160,256]{2,1,0:T(8,128)(2,1)S(1)}, bf16[4,160,256]{2,1,0:T(8,128)(2,1)S(1)}, u32[]{:S(2)}, u32[]{:S(2)}) %collective-permute-start) | collective-permute-done | bytes 327712 | tf_op jit(solution)/shard_map/ppermute | solution.py:235
  50.9 0.0 collective-permute-start.2
  50.9 3.7 %collective-permute-start.9 = (bf16[4,160,256]{2,1,0:T(8,128)(2,1)S(1)}, bf16[4,160,256]{2,1,0:T(8,128)(2,1)S(1)}, u32[]{:S(2)}, u32[]{:S(2)}) collective-permute-start(bf16[4,160,256]{2,1,0:T(8,128)(2,1)S(1)} %get-tuple-element.49), channel_id=1, source_target_pairs={{0,24},{8,0},{16,8},{24,16},{1,25},{9,1},{17,9},{25,17},{2,26},{10... | collective-permute-start | bytes 983048 | tf_op jit(solution)/shard_map/ppermute | solution.py:236
  54.6 2.3 %collective-permute-start.4 = (bf16[3,2,128,128]{3,2,1,0:T(8,128)(2,1)S(1)}, bf16[3,2,128,128]{3,2,1,0:T(8,128)(2,1)S(1)}, u32[]{:S(2)}, u32[]{:S(2)}) collective-permute-start(bf16[3,2,128,128]{3,2,1,0:T(8,128)(2,1)S(1)} %get-tuple-element.34), channel_id=1, source_target_pairs={{4,0},{6,2},{0,4},{2,6},{5,1},{7,3},{1,5},{3,7},{12,8},{14,10},{8,... | collective-permute-start | bytes 589832 | tf_op jit(solution)/shard_map/ppermute | solution.py:226
  56.9 1.2 %collective-permute-start.5 = (bf16[3,2,128,128]{3,2,1,0:T(8,128)(2,1)S(1)}, bf16[3,2,128,128]{3,2,1,0:T(8,128)(2,1)S(1)}, u32[]{:S(2)}, u32[]{:S(2)}) collective-permute-start(bf16[3,2,128,128]{3,2,1,0:T(8,128)(2,1)S(1)} %get-tuple-element.35), channel_id=1, source_target_pairs={{2,0},{4,2},{6,4},{0,6},{3,1},{5,3},{7,5},{1,7},{10,8},{12,10},{14... | collective-permute-start | bytes 589832 | tf_op jit(solution)/shard_map/ppermute | solution.py:226
  58.1 0.0 collective-permute-done.2.refs_3_.refs_4_
  58.1 2.4 %shard_map.66 = (bf16[2,2,128,128]{3,2,1,0:T(8,128)(2,1)S(1)}, bf16[2,2,128,128]{3,2,1,0:T(8,128)(2,1)S(1)}, bf16[2,2,128,128]{3,2,1,0:T(8,128)(2,1)S(1)}, bf16[2,2,128,128]{3,2,1,0:T(8,128)(2,1)S(1)}) custom-call(bf16[16,160,256]{2,1,0:T(8,128)(2,1)S(1)} %all_to_all.5.refs_0_, bf16[4,160,256]{2,1,0:T(8,128)(2,1)S(1)} %collective-permute-done.refs_1_, ...), custom_call_target="tpu_custom_call" | custom-call | flops 1 | bytes 1 | tf_op jit(solution)/shard_map/pallas_call | solution.py:171
  60.5 1.8 %collective-permute-done.9.refs_2_ = bf16[4,160,256]{2,1,0:T(8,128)(2,1)S(1)} collective-permute-done((bf16[4,160,256]{2,1,0:T(8,128)(2,1)S(1)}, bf16[4,160,256]{2,1,0:T(8,128)(2,1)S(1)}, u32[]{:S(2)}, u32[]{:S(2)}) %collective-permute-start.9) | collective-permute-done | bytes 327712 | tf_op jit(solution)/shard_map/ppermute | solution.py:236
  62.2 4.8 %collective-permute-done.3.refs_1_ = bf16[3,2,128,128]{3,2,1,0:T(8,128)(2,1)S(1)} collective-permute-done((bf16[3,2,128,128]{3,2,1,0:T(8,128)(2,1)S(1)}, bf16[3,2,128,128]{3,2,1,0:T(8,128)(2,1)S(1)}, u32[]{:S(2)}, u32[]{:S(2)}) %collective-permute-start.3) | collective-permute-done | bytes 196640 | tf_op jit(solution)/shard_map/ppermute | solution.py:226
  67.0 0.6 collective-permute-done.5.refs_3_
  67.6 0.2 collective-permute-start.6
  67.9 3.6 %collective-permute-start.7 = (bf16[2,2,128,128]{3,2,1,0:T(8,128)(2,1)S(1)}, bf16[2,2,128,128]{3,2,1,0:T(8,128)(2,1)S(1)}, u32[]{:S(2)}, u32[]{:S(2)}) collective-permute-start(bf16[2,2,128,128]{3,2,1,0:T(8,128)(2,1)S(1)} %get-tuple-element.42), channel_id=1, source_target_pairs={{4,0},{6,2},{0,4},{2,6},{5,1},{7,3},{1,5},{3,7},{12,8},{14,10},{8,... | collective-permute-start | bytes 393224 | tf_op jit(solution)/shard_map/ppermute | solution.py:226
  71.5 0.0 collective-permute-start.8
  71.5 0.6 shard_map.67
  72.0 0.7 collective-permute-start.11
  72.7 0.7 collective-permute-start.12
  73.4 1.0 %collective-permute-done.6.refs_5_ = bf16[2,2,128,128]{3,2,1,0:T(8,128)(2,1)S(1)} collective-permute-done((bf16[2,2,128,128]{3,2,1,0:T(8,128)(2,1)S(1)}, bf16[2,2,128,128]{3,2,1,0:T(8,128)(2,1)S(1)}, u32[]{:S(2)}, u32[]{:S(2)}) %collective-permute-start.6) | collective-permute-done | bytes 131104 | tf_op jit(solution)/shard_map/ppermute | solution.py:226
  74.4 3.9 %collective-permute-start.13 = (bf16[2,2,128,128]{3,2,1,0:T(8,128)(2,1)S(1)}, bf16[2,2,128,128]{3,2,1,0:T(8,128)(2,1)S(1)}, u32[]{:S(2)}, u32[]{:S(2)}) collective-permute-start(bf16[2,2,128,128]{3,2,1,0:T(8,128)(2,1)S(1)} %get-tuple-element.48), channel_id=1, source_target_pairs={{0,6},{1,7},{8,14},{9,15},{16,22},{17,23},{24,30},{25,31},{32,38},... | collective-permute-start | bytes 393224 | tf_op jit(solution)/shard_map/ppermute | solution.py:226
  79.0 2.5 %collective-permute-done.13.refs_11_ = bf16[2,2,128,128]{3,2,1,0:T(8,128)(2,1)S(1)} collective-permute-done((bf16[2,2,128,128]{3,2,1,0:T(8,128)(2,1)S(1)}, bf16[2,2,128,128]{3,2,1,0:T(8,128)(2,1)S(1)}, u32[]{:S(2)}, u32[]{:S(2)}) %collective-permute-start.13) | collective-permute-done | bytes 131104 | tf_op jit(solution)/shard_map/ppermute | solution.py:226
  81.5 2.2 %shard_map.68 = f32[5,2,4,128,128]{4,3,2,1,0:T(8,128)} custom-call(s32[1,5]{1,0:T(1,128)S(1)} %copy-done, s32[1]{0:T(128)S(6)} %copy.8.counts, bf16[3,2,128,128]{3,2,1,0:T(8,128)(2,1)S(1)} %get-tuple-element.36.refs_0_, bf16[3,2,128,128]{3,2,1,0:T(8,128)(2,1)S(1)} %collective-permute-done.3.refs_1_, ...), custom_call_target="tpu_custom_call" | custom-call | tf_op jit(solution)/shard_map/pallas_call | solution.py:213
  (13 shorter events, 0.1 us)
Async XLA Ops:
  39.1 4.2 %collective-permute-start.1 = (bf16[16,160,256]{2,1,0:T(8,128)(2,1)S(1)}, bf16[16,160,256]{2,1,0:T(8,128)(2,1)S(1)}, u32[]{:S(2)}, u32[]{:S(2)}) collective-permute-start(bf16[16,160,256]{2,1,0:T(8,128)(2,1)S(1)} %all_to_all.5.refs_0_), channel_id=1, source_target_pairs={{0,1},{1,0},{2,3},{3,2},{4,5},{5,4},{6,7},{7,6},{8,9},{9,8},{10,11... | collective-permute-start | bytes 3932168 | tf_op jit(solution)/shard_map/ppermute | solution.py:237
  39.1 11.7 %collective-permute-start = (bf16[4,160,256]{2,1,0:T(8,128)(2,1)S(1)}, bf16[4,160,256]{2,1,0:T(8,128)(2,1)S(1)}, u32[]{:S(2)}, u32[]{:S(2)}) collective-permute-start(bf16[4,160,256]{2,1,0:T(8,128)(2,1)S(1)} %get-tuple-element.50), channel_id=1, source_target_pairs={{0,24},{8,0},{16,8},{24,16},{1,25},{9,1},{17,9},{25,17},{2,26},{10... | collective-permute-start | bytes 983048 | tf_op jit(solution)/shard_map/ppermute | solution.py:235
  50.9 7.2 %collective-permute-start.2 = (bf16[4,160,256]{2,1,0:T(8,128)(2,1)S(1)}, bf16[4,160,256]{2,1,0:T(8,128)(2,1)S(1)}, u32[]{:S(2)}, u32[]{:S(2)}) collective-permute-start(bf16[4,160,256]{2,1,0:T(8,128)(2,1)S(1)} %collective-permute-done.refs_1_), channel_id=1, source_target_pairs={{0,1},{1,0},{2,3},{3,2},{4,5},{5,4},{6,7},{7,6},{8,9},{9,8},{10,11... | collective-permute-start | bytes 983048 | tf_op jit(solution)/shard_map/ppermute | solution.py:241
  50.9 11.3 %collective-permute-start.9 = (bf16[4,160,256]{2,1,0:T(8,128)(2,1)S(1)}, bf16[4,160,256]{2,1,0:T(8,128)(2,1)S(1)}, u32[]{:S(2)}, u32[]{:S(2)}) collective-permute-start(bf16[4,160,256]{2,1,0:T(8,128)(2,1)S(1)} %get-tuple-element.49), channel_id=1, source_target_pairs={{0,24},{8,0},{16,8},{24,16},{1,25},{9,1},{17,9},{25,17},{2,26},{10... | collective-permute-start | bytes 983048 | tf_op jit(solution)/shard_map/ppermute | solution.py:236
  54.6 12.5 %collective-permute-start.3 = (bf16[3,2,128,128]{3,2,1,0:T(8,128)(2,1)S(1)}, bf16[3,2,128,128]{3,2,1,0:T(8,128)(2,1)S(1)}, u32[]{:S(2)}, u32[]{:S(2)}) collective-permute-start(bf16[3,2,128,128]{3,2,1,0:T(8,128)(2,1)S(1)} %get-tuple-element.33), channel_id=1, source_target_pairs={{6,0},{0,2},{2,4},{4,6},{7,1},{1,3},{3,5},{5,7},{14,8},{8,10},{10,... | collective-permute-start | bytes 589832 | tf_op jit(solution)/shard_map/ppermute | solution.py:226
  54.6 12.5 %collective-permute-start.4 = (bf16[3,2,128,128]{3,2,1,0:T(8,128)(2,1)S(1)}, bf16[3,2,128,128]{3,2,1,0:T(8,128)(2,1)S(1)}, u32[]{:S(2)}, u32[]{:S(2)}) collective-permute-start(bf16[3,2,128,128]{3,2,1,0:T(8,128)(2,1)S(1)} %get-tuple-element.34), channel_id=1, source_target_pairs={{4,0},{6,2},{0,4},{2,6},{5,1},{7,3},{1,5},{3,7},{12,8},{14,10},{8,... | collective-permute-start | bytes 589832 | tf_op jit(solution)/shard_map/ppermute | solution.py:226
  56.9 10.8 %collective-permute-start.5 = (bf16[3,2,128,128]{3,2,1,0:T(8,128)(2,1)S(1)}, bf16[3,2,128,128]{3,2,1,0:T(8,128)(2,1)S(1)}, u32[]{:S(2)}, u32[]{:S(2)}) collective-permute-start(bf16[3,2,128,128]{3,2,1,0:T(8,128)(2,1)S(1)} %get-tuple-element.35), channel_id=1, source_target_pairs={{2,0},{4,2},{6,4},{0,6},{3,1},{5,3},{7,5},{1,7},{10,8},{12,10},{14... | collective-permute-start | bytes 589832 | tf_op jit(solution)/shard_map/ppermute | solution.py:226
  62.2 9.2 %collective-permute-start.10 = (bf16[4,160,256]{2,1,0:T(8,128)(2,1)S(1)}, bf16[4,160,256]{2,1,0:T(8,128)(2,1)S(1)}, u32[]{:S(2)}, u32[]{:S(2)}) collective-permute-start(bf16[4,160,256]{2,1,0:T(8,128)(2,1)S(1)} %collective-permute-done.9.refs_2_), channel_id=1, source_target_pairs={{0,1},{1,0},{2,3},{3,2},{4,5},{5,4},{6,7},{7,6},{8,9},{9,8},{10,11... | collective-permute-start | bytes 983048 | tf_op jit(solution)/shard_map/ppermute | solution.py:246
  67.6 13.9 %copy-start = (s32[1,5]{1,0:T(1,128)S(1)}, s32[1,5]{1,0:T(1,128)}, u32[]{:S(2)}) copy-start(s32[1,5]{1,0:T(1,128)} %offsets.1) | copy-start | bytes 64
  67.6 6.8 %collective-permute-start.6 = (bf16[2,2,128,128]{3,2,1,0:T(8,128)(2,1)S(1)}, bf16[2,2,128,128]{3,2,1,0:T(8,128)(2,1)S(1)}, u32[]{:S(2)}, u32[]{:S(2)}) collective-permute-start(bf16[2,2,128,128]{3,2,1,0:T(8,128)(2,1)S(1)} %get-tuple-element.41), channel_id=1, source_target_pairs={{6,0},{0,2},{2,4},{4,6},{7,1},{1,3},{3,5},{5,7},{14,8},{8,10},{10,... | collective-permute-start | bytes 393224 | tf_op jit(solution)/shard_map/ppermute | solution.py:226
  67.9 11.1 %collective-permute-start.7 = (bf16[2,2,128,128]{3,2,1,0:T(8,128)(2,1)S(1)}, bf16[2,2,128,128]{3,2,1,0:T(8,128)(2,1)S(1)}, u32[]{:S(2)}, u32[]{:S(2)}) collective-permute-start(bf16[2,2,128,128]{3,2,1,0:T(8,128)(2,1)S(1)} %get-tuple-element.42), channel_id=1, source_target_pairs={{4,0},{6,2},{0,4},{2,6},{5,1},{7,3},{1,5},{3,7},{12,8},{14,10},{8,... | collective-permute-start | bytes 393224 | tf_op jit(solution)/shard_map/ppermute | solution.py:226
  71.5 7.5 %collective-permute-start.8 = (bf16[2,2,128,128]{3,2,1,0:T(8,128)(2,1)S(1)}, bf16[2,2,128,128]{3,2,1,0:T(8,128)(2,1)S(1)}, u32[]{:S(2)}, u32[]{:S(2)}) collective-permute-start(bf16[2,2,128,128]{3,2,1,0:T(8,128)(2,1)S(1)} %get-tuple-element.43), channel_id=1, source_target_pairs={{2,0},{4,2},{6,4},{0,6},{3,1},{5,3},{7,5},{1,7},{10,8},{12,10},{14... | collective-permute-start | bytes 393224 | tf_op jit(solution)/shard_map/ppermute | solution.py:226
  72.0 6.9 %collective-permute-start.11 = (bf16[2,2,128,128]{3,2,1,0:T(8,128)(2,1)S(1)}, bf16[2,2,128,128]{3,2,1,0:T(8,128)(2,1)S(1)}, u32[]{:S(2)}, u32[]{:S(2)}) collective-permute-start(bf16[2,2,128,128]{3,2,1,0:T(8,128)(2,1)S(1)} %get-tuple-element.46), channel_id=1, source_target_pairs={{4,6},{5,7},{12,14},{13,15},{20,22},{21,23},{28,30},{29,31},{36,38... | collective-permute-start | bytes 393224 | tf_op jit(solution)/shard_map/ppermute | solution.py:226
  72.7 6.3 %collective-permute-start.12 = (bf16[2,2,128,128]{3,2,1,0:T(8,128)(2,1)S(1)}, bf16[2,2,128,128]{3,2,1,0:T(8,128)(2,1)S(1)}, u32[]{:S(2)}, u32[]{:S(2)}) collective-permute-start(bf16[2,2,128,128]{3,2,1,0:T(8,128)(2,1)S(1)} %get-tuple-element.47), channel_id=1, source_target_pairs={{2,6},{3,7},{10,14},{11,15},{18,22},{19,23},{26,30},{27,31},{34,38... | collective-permute-start | bytes 393224 | tf_op jit(solution)/shard_map/ppermute | solution.py:226
  74.4 7.1 %collective-permute-start.13 = (bf16[2,2,128,128]{3,2,1,0:T(8,128)(2,1)S(1)}, bf16[2,2,128,128]{3,2,1,0:T(8,128)(2,1)S(1)}, u32[]{:S(2)}, u32[]{:S(2)}) collective-permute-start(bf16[2,2,128,128]{3,2,1,0:T(8,128)(2,1)S(1)} %get-tuple-element.48), channel_id=1, source_target_pairs={{0,6},{1,7},{8,14},{9,15},{16,22},{17,23},{24,30},{25,31},{32,38},... | collective-permute-start | bytes 393224 | tf_op jit(solution)/shard_map/ppermute | solution.py:226

commit v3 on v2

--- a/solution.py
+++ b/solution.py
@@ -14,85 +14,97 @@
 K = 5
 BW = 128
 PERIOD = 2 * NF
-HALF = PERIOD // 2
+QUARTER = PERIOD // 4
+GROUP = BW // 4
 SLOTS = 5
 RING = 4
 OWNERS = RING * RING
+WIDTH = 512
 VMEM_LIMIT = 24 * 1024 * 1024
 STREAM_VMEM_LIMIT = 56 * 1024 * 1024
 
 
-def half_period_tables():
-    samples = np.arange(HALF, dtype=np.int64)
-    bins = np.stack(
-        [
-            np.concatenate(
-                [(RING * (owner % RING) + owner // RING) * BW + 2 * np.arange(BW // 2) + parity
-                 for owner in range(OWNERS)]
-            )
-            for parity in range(2)
-        ]
-    )
-    angle = ((samples[None, :, None] * bins[:, None, :]) % PERIOD) * (2.0 * np.pi / PERIOD)
-    parts = np.stack([np.cos(angle), -np.sin(angle)], axis=2)
-    parts = parts.reshape(2, HALF, 2, OWNERS, BW // 2).transpose(3, 0, 1, 2, 4)
-    parts = parts.reshape(OWNERS // 2, 2, 2, HALF, BW).transpose(0, 2, 3, 1, 4)
-    return parts.reshape(OWNERS // 2, 2, HALF, 2 * BW).astype(ml_dtypes.bfloat16)
-
-
-def spectra_kernel(live_counts, series, tapers, table, out, even, odd):
+def quarter_period_tables():
+    samples = np.arange(QUARTER, dtype=np.int64)
+    owner = np.arange(OWNERS)
+    bins = (RING * (owner % RING) + owner // RING)[:, None] * GROUP + np.arange(GROUP)
+    angle = (samples[:, None, None] * bins % QUARTER) * (2.0 * np.pi / QUARTER)
+    cos, sin = np.cos(angle), np.sin(angle)
+    table = np.stack([np.stack([cos, -sin], axis=2), np.stack([sin, cos], axis=2)])
+    table = table.reshape(2 * QUARTER, OWNERS * 2 * GROUP).astype(ml_dtypes.bfloat16)
+    turn = np.arange(1, 4)[:, None] * samples * (2.0 * np.pi / PERIOD)
+    turns = np.stack([np.cos(turn), np.sin(turn)], axis=1).reshape(6, QUARTER)
+    return turns.astype(np.float32), table
+
+
+def spectra_kernel(live_counts, series, tapers, turns, table, out, plain, turned):
     rows, samples = series.shape
+    total = K * rows
 
     @pl.when(pl.program_id(0) == 0)
     def _():
-        live, first = live_counts[0], lax.axis_index("freq") * rows
-        channel = first + lax.broadcasted_iota(jnp.int32, (rows, HALF), 0)
-        working = channel < live
-
-        def tapered(k, begin, end):
-            product = series[:, begin:end].astype(jnp.float32) * tapers[k : k + 1, begin:end]
-            if end - begin < HALF:
+        first = lax.axis_index("freq") * rows
+        channel = first + lax.broadcasted_iota(jnp.int32, (rows, QUARTER), 0)
+        working = channel < live_counts[0]
+
+        def tapered(k, quarter):
+            lanes = slice(quarter * QUARTER, min((quarter + 1) * QUARTER, samples))
+            product = series[:, lanes].astype(jnp.float32) * tapers[k : k + 1, lanes]
+            short = QUARTER - product.shape[1]
+            if short:
                 product = jnp.concatenate(
-                    [product, jnp.zeros((rows, HALF - (end - begin)), jnp.float32)], axis=1
+                    [product, jnp.zeros((rows, short), jnp.float32)], axis=1
                 )
             product = jnp.where(working, product, 0.0)
             return product.astype(jnp.bfloat16).astype(jnp.float32)
 
         for k in range(K):
-            ends = tapered(k, 0, HALF) + tapered(k, 2 * HALF, samples)
-            middle = tapered(k, HALF, 2 * HALF)
-            even[k * rows : (k + 1) * rows, :] = (ends + middle).astype(jnp.bfloat16)
-            odd[k * rows : (k + 1) * rows, :] = (ends - middle).astype(jnp.bfloat16)
-
-    for parity, folded in enumerate((even, odd)):
-        bins = jnp.dot(folded[...], table[0, parity], preferred_element_type=jnp.float32)
-        bins = bins.astype(jnp.bfloat16)
-        out[0, :, parity * BW : (parity + 1) * BW] = bins[:, :BW]
-        out[1, :, parity * BW : (parity + 1) * BW] = bins[:, BW:]
-
-
-def block_spectra(live_counts, series, tapers, table):
+            quarters = [tapered(k, 0) + tapered(k, 4), tapered(k, 1) + tapered(k, 5)]
+            quarters += [tapered(k, 2), tapered(k, 3)]
+            even, odd = quarters[0] + quarters[2], quarters[1] + quarters[3]
+            real, imag = quarters[0] - quarters[2], quarters[1] - quarters[3]
+            plain[k * rows : (k + 1) * rows, :] = (even + odd).astype(jnp.bfloat16)
+            for r, (p, q) in enumerate(((real, -imag), (even - odd, None), (real, imag))):
+                cos, sin = turns[2 * r : 2 * r + 1, :], turns[2 * r + 1 : 2 * r + 2, :]
+                at = r * total + k * rows
+                left, right = p * cos, -p * sin
+                if q is not None:
+                    left, right = left + q * sin, right + q * cos
+                turned[at : at + rows, :QUARTER] = left.astype(jnp.bfloat16)
+                turned[at : at + rows, QUARTER:] = right.astype(jnp.bfloat16)
+
+    groups = [jnp.dot(plain[...], table[:QUARTER, :], preferred_element_type=jnp.float32)]
+    others = jnp.dot(turned[...], table[...], preferred_element_type=jnp.float32)
+    groups += [others[r * total : (r + 1) * total] for r in range(3)]
+    for owner in range(WIDTH // (2 * GROUP)):
+        lanes = slice(owner * 2 * GROUP, (owner + 1) * 2 * GROUP)
+        for pair in range(2):
+            bins = jnp.concatenate([group[:, lanes] for group in groups[2 * pair :][:2]], axis=1)
+            out[owner, :, pair * BW : (pair + 1) * BW] = bins.astype(jnp.bfloat16)
+
+
+def block_spectra(live_counts, series, tapers, turns, table):
     rows, samples = series.shape
     return pl.pallas_call(
         spectra_kernel,
-        grid=(OWNERS // 2,),
+        grid=(OWNERS * 2 * GROUP // WIDTH,),
         in_specs=[
             pl.BlockSpec(memory_space=pltpu.SMEM),
             pl.BlockSpec((rows, samples), lambda step: (0, 0)),
             pl.BlockSpec((K, samples), lambda step: (0, 0)),
-            pl.BlockSpec((1, 2, HALF, 2 * BW), lambda step: (step, 0, 0, 0)),
+            pl.BlockSpec((6, QUARTER), lambda step: (0, 0)),
+            pl.BlockSpec((2 * QUARTER, WIDTH), lambda step: (0, step)),
         ],
-        out_specs=pl.BlockSpec((2, K * rows, 2 * BW), lambda step: (step, 0, 0)),
+        out_specs=pl.BlockSpec(
+            (WIDTH // (2 * GROUP), K * rows, 2 * BW), lambda step: (step, 0, 0)
+        ),
         out_shape=jax.ShapeDtypeStruct((OWNERS, K * rows, 2 * BW), jnp.bfloat16),
         scratch_shapes=[
-            pltpu.VMEM((K * rows, HALF), jnp.bfloat16),
-            pltpu.VMEM((K * rows, HALF), jnp.bfloat16),
+            pltpu.VMEM((K * rows, QUARTER), jnp.bfloat16),
+            pltpu.VMEM((3 * K * rows, 2 * QUARTER), jnp.bfloat16),
         ],
         compiler_params=pltpu.CompilerParams(vmem_limit_bytes=STREAM_VMEM_LIMIT),
-        cost_estimate=pl.CostEstimate(
-            flops=2 * K * rows * HALF * 2 * NF, bytes_accessed=20_000_000, transcendentals=0
-        ),
-    )(live_counts, series, tapers, table)
+    )(live_counts, series, tapers, turns, table)
 
 
 def pair_kernel(wanted, *refs):
@@ -101,7 +113,8 @@
     inputs = refs[: -3 - RING]
     y, core = lax.axis_index("y"), lax.axis_index("core")
     rows = inputs[0].shape[1] // K
-    half = BW // 2
+    lane = lax.broadcasted_iota(jnp.int32, (BW, BW), 1)
+    is_real = lane % (2 * GROUP) < GROUP
     first = min(wanted)
 
     def channels(group, at, k):
@@ -137,7 +150,9 @@
         for part in range(2 * K):
             at = part * BW
             wide = mine_wide[to : to + BW, at : at + BW].astype(jnp.float32)
-            turned = jnp.concatenate([wide[:, half:], -wide[:, :half]], axis=1)
+            turned = jnp.where(
+                is_real, pltpu.roll(wide, BW - GROUP, 1), -pltpu.roll(wide, GROUP, 1)
+            )
             later[BW:, at : at + BW] = turned.astype(jnp.bfloat16)
         same, crossed = same_of[target], crossed_of[target]
         at = (same[0] - first) * BW
@@ -227,10 +242,10 @@
     return moved
 
 
-def body(table, series, tapers, live_channels, pair_offset, pair_count):
+def body(turns, table, series, tapers, live_channels, pair_offset, pair_count):
     swap = [(0, 1), (1, 0)]
     next_plane = [(i, (i - 1) % RING) for i in range(RING)]
-    spectra = block_spectra(live_channels, series[0], tapers, table)
+    spectra = block_spectra(live_channels, series[0], tapers, turns, table)
     mine = lax.all_to_all(spectra, ("y", "freq"), 0, 0)
     near = lax.ppermute(mine[:RING], "z", next_plane)
     far = lax.ppermute(mine[RING : 2 * RING], "z", next_plane)
@@ -251,13 +266,13 @@
 
 
 def solution(mesh):
-    table = half_period_tables()
+    turns, table = quarter_period_tables()
     grid = Mesh(
         mesh.devices.reshape(RING, RING, RING, 2), ("freq", "z", "y", "core")
     )
     blk = ("z", "y", "core")
     return jax.shard_map(
-        functools.partial(body, table),
+        functools.partial(body, turns, table),
         mesh=grid,
         in_specs=(P(blk, "freq", None), P(), P(blk), P(blk, None), P(blk)),
         out_specs=P(blk, None, None, "freq", None, None),

time: 84.7 us -> 80 us (0.945)
  Pallas kernels: 19 us -> 14.4 us
    pallas_call x1, Pallas kernels: 11.3 us -> 6.74 us  [block_spectra(): pl.pallas_call(spectra_kernel, grid=(OWNERS * 2 * GROUP // WIDTH,), in_sp...]
  transfers between devices with their start and end apart: 14 -> 14, of which waited for: 6 -> 6; matrix products, arithmetic and copies ran while one was open for 0% -> 0% of each run, Pallas kernels for 6% -> 7%
where the time goes in v3:
time: 80 us; the launch traced here: 79.2 us
  blocking collectives  27.1 us (34%)
  starting transfers between devices  20.3 us (25%)
  waiting for transfers between devices  15.9 us (20%)
  Pallas kernels  14.4 us (18%)
  between operations  1.4 us (2%)
    all_to_all x1, blocking collectives, body(): mine = lax.all_to_all(spectra, ('y', 'freq'), 0, 0)  27.1 us
    ppermute x9, starting transfers between devices, sent_to(): moved.append(lax.ppermute(pieces[distance], 'y', routes))  12.5 us
    ppermute x9, waiting for transfers between devices, sent_to(): moved.append(lax.ppermute(pieces[distance], 'y', routes))  9.01 us
    pallas_call x1, Pallas kernels, block_spectra(): pl.pallas_call(spectra_kernel, grid=(OWNERS * 2 * GROUP // WIDTH,), in_sp...  6.74 us
    pallas_call x3, Pallas kernels, pair_products(): pl.pallas_call(functools.partial(pair_kernel, wanted), in_specs=[whole] *...  5.47 us
    ppermute x1, waiting for transfers between devices, body(): near = lax.ppermute(mine[:RING], 'z', next_plane)  5.18 us
    ppermute x1, starting transfers between devices, body(): near = lax.ppermute(mine[:RING], 'z', next_plane)  4.11 us
    ppermute x1, starting transfers between devices, body(): far = lax.ppermute(mine[RING:2 * RING], 'z', next_plane)  3.69 us
  transfers between devices with their start and end apart: 14, of which 6 were waited for; matrix products, arithmetic and copies ran while one was open for 0% of the time, Pallas kernels for 7%

profile of v3, /device:TPU:0, one launch (start us, length us, event | category | flops | bytes accessed | tf_op | source)
XLA Modules:
  0.0 79.2 jit_solution(9374912226939823511)
XLA Ops:
  0.7 6.7 %shard_map.73 = bf16[16,160,256]{2,1,0:T(8,128)(2,1)} custom-call(s32[1]{0:T(128)S(6)} %copy.8.live_counts, bf16[32,6000]{1,0:T(8,128)(2,1)} %bitcast.2, f32[5,6000]{1,0:T(8,128)} %tapers.1, f32[6,1024]{1,0:T(8,128)} %constant.4.clone.turns, bf16[2048,1024]{1,0:T(8,128)(2,1)} %constant.5.clone.table), custom_call_target="tpu_custom_call" | custom-call | tf_op jit(solution)/shard_map/pallas_call | solution.py:88
  7.4 27.1 %all_to_all.5.refs_0_ = bf16[16,160,256]{2,1,0:T(8,128)(2,1)S(1)} all-to-all(bf16[16,160,256]{2,1,0:T(8,128)(2,1)} %shard_map.73), channel_id=1, replica_groups=mesh['freq'=4,'z'=4,'y'=4,'core'=2] {'y','freq'}, dimensions={0} | all-to-all | bytes 2621440 | tf_op jit(solution)/shard_map/all_to_all | solution.py:249
  34.5 0.0 collective-permute-start.1
  34.5 4.1 %collective-permute-start = (bf16[4,160,256]{2,1,0:T(8,128)(2,1)S(1)}, bf16[4,160,256]{2,1,0:T(8,128)(2,1)S(1)}, u32[]{:S(2)}, u32[]{:S(2)}) collective-permute-start(bf16[4,160,256]{2,1,0:T(8,128)(2,1)S(1)} %get-tuple-element.50), channel_id=1, source_target_pairs={{0,24},{8,0},{16,8},{24,16},{1,25},{9,1},{17,9},{25,17},{2,26},{10... | collective-permute-start | bytes 983048 | tf_op jit(solution)/shard_map/ppermute | solution.py:250
  38.6 2.5 %shard_map.74 = (bf16[3,2,128,128]{3,2,1,0:T(8,128)(2,1)S(1)}, bf16[3,2,128,128]{3,2,1,0:T(8,128)(2,1)S(1)}, bf16[3,2,128,128]{3,2,1,0:T(8,128)(2,1)S(1)}, bf16[3,2,128,128]{3,2,1,0:T(8,128)(2,1)S(1)}) custom-call(bf16[16,160,256]{2,1,0:T(8,128)(2,1)S(1)} %all_to_all.5.refs_0_, bf16[16,160,256]{2,1,0:T(8,128)(2,1)S(1)} %collective-permute-done.1.refs_1_.refs_2_.refs_3_), custom_call_target="tpu_custom_call" | custom-call | flops 1 | bytes 1 | tf_op jit(solution)/shard_map/pallas_call | solution.py:186
  41.1 5.2 %collective-permute-done.refs_1_ = bf16[4,160,256]{2,1,0:T(8,128)(2,1)S(1)} collective-permute-done((bf16[4,160,256]{2,1,0:T(8,128)(2,1)S(1)}, bf16[4,160,256]{2,1,0:T(8,128)(2,1)S(1)}, u32[]{:S(2)}, u32[]{:S(2)}) %collective-permute-start) | collective-permute-done | bytes 327712 | tf_op jit(solution)/shard_map/ppermute | solution.py:250
  46.3 0.0 collective-permute-start.2
  46.3 3.7 %collective-permute-start.9 = (bf16[4,160,256]{2,1,0:T(8,128)(2,1)S(1)}, bf16[4,160,256]{2,1,0:T(8,128)(2,1)S(1)}, u32[]{:S(2)}, u32[]{:S(2)}) collective-permute-start(bf16[4,160,256]{2,1,0:T(8,128)(2,1)S(1)} %get-tuple-element.49), channel_id=1, source_target_pairs={{0,24},{8,0},{16,8},{24,16},{1,25},{9,1},{17,9},{25,17},{2,26},{10... | collective-permute-start | bytes 983048 | tf_op jit(solution)/shard_map/ppermute | solution.py:251
  50.0 2.3 %collective-permute-start.4 = (bf16[3,2,128,128]{3,2,1,0:T(8,128)(2,1)S(1)}, bf16[3,2,128,128]{3,2,1,0:T(8,128)(2,1)S(1)}, u32[]{:S(2)}, u32[]{:S(2)}) collective-permute-start(bf16[3,2,128,128]{3,2,1,0:T(8,128)(2,1)S(1)} %get-tuple-element.34), channel_id=1, source_target_pairs={{4,0},{6,2},{0,4},{2,6},{5,1},{7,3},{1,5},{3,7},{12,8},{14,10},{8,... | collective-permute-start | bytes 589832 | tf_op jit(solution)/shard_map/ppermute | solution.py:241
  52.3 1.2 %collective-permute-start.5 = (bf16[3,2,128,128]{3,2,1,0:T(8,128)(2,1)S(1)}, bf16[3,2,128,128]{3,2,1,0:T(8,128)(2,1)S(1)}, u32[]{:S(2)}, u32[]{:S(2)}) collective-permute-start(bf16[3,2,128,128]{3,2,1,0:T(8,128)(2,1)S(1)} %get-tuple-element.35), channel_id=1, source_target_pairs={{2,0},{4,2},{6,4},{0,6},{3,1},{5,3},{7,5},{1,7},{10,8},{12,10},{14... | collective-permute-start | bytes 589832 | tf_op jit(solution)/shard_map/ppermute | solution.py:241
  53.4 0.0 collective-permute-done.2.refs_3_.refs_4_
  53.4 2.4 %shard_map.75 = (bf16[2,2,128,128]{3,2,1,0:T(8,128)(2,1)S(1)}, bf16[2,2,128,128]{3,2,1,0:T(8,128)(2,1)S(1)}, bf16[2,2,128,128]{3,2,1,0:T(8,128)(2,1)S(1)}, bf16[2,2,128,128]{3,2,1,0:T(8,128)(2,1)S(1)}) custom-call(bf16[16,160,256]{2,1,0:T(8,128)(2,1)S(1)} %all_to_all.5.refs_0_, bf16[4,160,256]{2,1,0:T(8,128)(2,1)S(1)} %collective-permute-done.refs_1_, ...), custom_call_target="tpu_custom_call" | custom-call | flops 1 | bytes 1 | tf_op jit(solution)/shard_map/pallas_call | solution.py:186
  55.9 1.7 %collective-permute-done.9.refs_2_ = bf16[4,160,256]{2,1,0:T(8,128)(2,1)S(1)} collective-permute-done((bf16[4,160,256]{2,1,0:T(8,128)(2,1)S(1)}, bf16[4,160,256]{2,1,0:T(8,128)(2,1)S(1)}, u32[]{:S(2)}, u32[]{:S(2)}) %collective-permute-start.9) | collective-permute-done | bytes 327712 | tf_op jit(solution)/shard_map/ppermute | solution.py:251
  57.6 4.8 %collective-permute-done.3.refs_1_ = bf16[3,2,128,128]{3,2,1,0:T(8,128)(2,1)S(1)} collective-permute-done((bf16[3,2,128,128]{3,2,1,0:T(8,128)(2,1)S(1)}, bf16[3,2,128,128]{3,2,1,0:T(8,128)(2,1)S(1)}, u32[]{:S(2)}, u32[]{:S(2)}) %collective-permute-start.3) | collective-permute-done | bytes 196640 | tf_op jit(solution)/shard_map/ppermute | solution.py:241
  62.4 0.6 collective-permute-done.5.refs_3_
  63.0 0.2 collective-permute-start.6
  63.3 3.6 %collective-permute-start.7 = (bf16[2,2,128,128]{3,2,1,0:T(8,128)(2,1)S(1)}, bf16[2,2,128,128]{3,2,1,0:T(8,128)(2,1)S(1)}, u32[]{:S(2)}, u32[]{:S(2)}) collective-permute-start(bf16[2,2,128,128]{3,2,1,0:T(8,128)(2,1)S(1)} %get-tuple-element.42), channel_id=1, source_target_pairs={{4,0},{6,2},{0,4},{2,6},{5,1},{7,3},{1,5},{3,7},{12,8},{14,10},{8,... | collective-permute-start | bytes 393224 | tf_op jit(solution)/shard_map/ppermute | solution.py:241
  66.8 0.6 shard_map.76
  67.4 0.7 collective-permute-start.11
  68.1 0.7 collective-permute-start.12
  68.8 1.0 %collective-permute-done.6.refs_5_ = bf16[2,2,128,128]{3,2,1,0:T(8,128)(2,1)S(1)} collective-permute-done((bf16[2,2,128,128]{3,2,1,0:T(8,128)(2,1)S(1)}, bf16[2,2,128,128]{3,2,1,0:T(8,128)(2,1)S(1)}, u32[]{:S(2)}, u32[]{:S(2)}) %collective-permute-start.6) | collective-permute-done | bytes 131104 | tf_op jit(solution)/shard_map/ppermute | solution.py:241
  69.8 3.9 %collective-permute-start.13 = (bf16[2,2,128,128]{3,2,1,0:T(8,128)(2,1)S(1)}, bf16[2,2,128,128]{3,2,1,0:T(8,128)(2,1)S(1)}, u32[]{:S(2)}, u32[]{:S(2)}) collective-permute-start(bf16[2,2,128,128]{3,2,1,0:T(8,128)(2,1)S(1)} %get-tuple-element.48), channel_id=1, source_target_pairs={{0,6},{1,7},{8,14},{9,15},{16,22},{17,23},{24,30},{25,31},{32,38},... | collective-permute-start | bytes 393224 | tf_op jit(solution)/shard_map/ppermute | solution.py:241
  74.4 2.5 %collective-permute-done.13.refs_11_ = bf16[2,2,128,128]{3,2,1,0:T(8,128)(2,1)S(1)} collective-permute-done((bf16[2,2,128,128]{3,2,1,0:T(8,128)(2,1)S(1)}, bf16[2,2,128,128]{3,2,1,0:T(8,128)(2,1)S(1)}, u32[]{:S(2)}, u32[]{:S(2)}) %collective-permute-start.13) | collective-permute-done | bytes 131104 | tf_op jit(solution)/shard_map/ppermute | solution.py:241
  76.9 2.2 %shard_map.77 = f32[5,2,4,128,128]{4,3,2,1,0:T(8,128)} custom-call(s32[1,5]{1,0:T(1,128)S(1)} %copy-done, s32[1]{0:T(128)S(6)} %copy.9.counts, bf16[3,2,128,128]{3,2,1,0:T(8,128)(2,1)S(1)} %get-tuple-element.36.refs_0_, bf16[3,2,128,128]{3,2,1,0:T(8,128)(2,1)S(1)} %collective-permute-done.3.refs_1_, ...), custom_call_target="tpu_custom_call" | custom-call | tf_op jit(solution)/shard_map/pallas_call | solution.py:228
  (13 shorter events, 0.1 us)
Async XLA Ops:
  34.5 4.2 %collective-permute-start.1 = (bf16[16,160,256]{2,1,0:T(8,128)(2,1)S(1)}, bf16[16,160,256]{2,1,0:T(8,128)(2,1)S(1)}, u32[]{:S(2)}, u32[]{:S(2)}) collective-permute-start(bf16[16,160,256]{2,1,0:T(8,128)(2,1)S(1)} %all_to_all.5.refs_0_), channel_id=1, source_target_pairs={{0,1},{1,0},{2,3},{3,2},{4,5},{5,4},{6,7},{7,6},{8,9},{9,8},{10,11... | collective-permute-start | bytes 3932168 | tf_op jit(solution)/shard_map/ppermute | solution.py:252
  34.5 11.7 %collective-permute-start = (bf16[4,160,256]{2,1,0:T(8,128)(2,1)S(1)}, bf16[4,160,256]{2,1,0:T(8,128)(2,1)S(1)}, u32[]{:S(2)}, u32[]{:S(2)}) collective-permute-start(bf16[4,160,256]{2,1,0:T(8,128)(2,1)S(1)} %get-tuple-element.50), channel_id=1, source_target_pairs={{0,24},{8,0},{16,8},{24,16},{1,25},{9,1},{17,9},{25,17},{2,26},{10... | collective-permute-start | bytes 983048 | tf_op jit(solution)/shard_map/ppermute | solution.py:250
  46.3 7.2 %collective-permute-start.2 = (bf16[4,160,256]{2,1,0:T(8,128)(2,1)S(1)}, bf16[4,160,256]{2,1,0:T(8,128)(2,1)S(1)}, u32[]{:S(2)}, u32[]{:S(2)}) collective-permute-start(bf16[4,160,256]{2,1,0:T(8,128)(2,1)S(1)} %collective-permute-done.refs_1_), channel_id=1, source_target_pairs={{0,1},{1,0},{2,3},{3,2},{4,5},{5,4},{6,7},{7,6},{8,9},{9,8},{10,11... | collective-permute-start | bytes 983048 | tf_op jit(solution)/shard_map/ppermute | solution.py:256
  46.3 11.3 %collective-permute-start.9 = (bf16[4,160,256]{2,1,0:T(8,128)(2,1)S(1)}, bf16[4,160,256]{2,1,0:T(8,128)(2,1)S(1)}, u32[]{:S(2)}, u32[]{:S(2)}) collective-permute-start(bf16[4,160,256]{2,1,0:T(8,128)(2,1)S(1)} %get-tuple-element.49), channel_id=1, source_target_pairs={{0,24},{8,0},{16,8},{24,16},{1,25},{9,1},{17,9},{25,17},{2,26},{10... | collective-permute-start | bytes 983048 | tf_op jit(solution)/shard_map/ppermute | solution.py:251
  50.0 12.5 %collective-permute-start.3 = (bf16[3,2,128,128]{3,2,1,0:T(8,128)(2,1)S(1)}, bf16[3,2,128,128]{3,2,1,0:T(8,128)(2,1)S(1)}, u32[]{:S(2)}, u32[]{:S(2)}) collective-permute-start(bf16[3,2,128,128]{3,2,1,0:T(8,128)(2,1)S(1)} %get-tuple-element.33), channel_id=1, source_target_pairs={{6,0},{0,2},{2,4},{4,6},{7,1},{1,3},{3,5},{5,7},{14,8},{8,10},{10,... | collective-permute-start | bytes 589832 | tf_op jit(solution)/shard_map/ppermute | solution.py:241
  50.0 12.5 %collective-permute-start.4 = (bf16[3,2,128,128]{3,2,1,0:T(8,128)(2,1)S(1)}, bf16[3,2,128,128]{3,2,1,0:T(8,128)(2,1)S(1)}, u32[]{:S(2)}, u32[]{:S(2)}) collective-permute-start(bf16[3,2,128,128]{3,2,1,0:T(8,128)(2,1)S(1)} %get-tuple-element.34), channel_id=1, source_target_pairs={{4,0},{6,2},{0,4},{2,6},{5,1},{7,3},{1,5},{3,7},{12,8},{14,10},{8,... | collective-permute-start | bytes 589832 | tf_op jit(solution)/shard_map/ppermute | solution.py:241
  52.3 10.8 %collective-permute-start.5 = (bf16[3,2,128,128]{3,2,1,0:T(8,128)(2,1)S(1)}, bf16[3,2,128,128]{3,2,1,0:T(8,128)(2,1)S(1)}, u32[]{:S(2)}, u32[]{:S(2)}) collective-permute-start(bf16[3,2,128,128]{3,2,1,0:T(8,128)(2,1)S(1)} %get-tuple-element.35), channel_id=1, source_target_pairs={{2,0},{4,2},{6,4},{0,6},{3,1},{5,3},{7,5},{1,7},{10,8},{12,10},{14... | collective-permute-start | bytes 589832 | tf_op jit(solution)/shard_map/ppermute | solution.py:241
  57.6 9.2 %collective-permute-start.10 = (bf16[4,160,256]{2,1,0:T(8,128)(2,1)S(1)}, bf16[4,160,256]{2,1,0:T(8,128)(2,1)S(1)}, u32[]{:S(2)}, u32[]{:S(2)}) collective-permute-start(bf16[4,160,256]{2,1,0:T(8,128)(2,1)S(1)} %collective-permute-done.9.refs_2_), channel_id=1, source_target_pairs={{0,1},{1,0},{2,3},{3,2},{4,5},{5,4},{6,7},{7,6},{8,9},{9,8},{10,11... | collective-permute-start | bytes 983048 | tf_op jit(solution)/shard_map/ppermute | solution.py:261
  63.0 13.9 %copy-start = (s32[1,5]{1,0:T(1,128)S(1)}, s32[1,5]{1,0:T(1,128)}, u32[]{:S(2)}) copy-start(s32[1,5]{1,0:T(1,128)} %offsets.1) | copy-start | bytes 64
  63.0 6.8 %collective-permute-start.6 = (bf16[2,2,128,128]{3,2,1,0:T(8,128)(2,1)S(1)}, bf16[2,2,128,128]{3,2,1,0:T(8,128)(2,1)S(1)}, u32[]{:S(2)}, u32[]{:S(2)}) collective-permute-start(bf16[2,2,128,128]{3,2,1,0:T(8,128)(2,1)S(1)} %get-tuple-element.41), channel_id=1, source_target_pairs={{6,0},{0,2},{2,4},{4,6},{7,1},{1,3},{3,5},{5,7},{14,8},{8,10},{10,... | collective-permute-start | bytes 393224 | tf_op jit(solution)/shard_map/ppermute | solution.py:241
  63.3 11.1 %collective-permute-start.7 = (bf16[2,2,128,128]{3,2,1,0:T(8,128)(2,1)S(1)}, bf16[2,2,128,128]{3,2,1,0:T(8,128)(2,1)S(1)}, u32[]{:S(2)}, u32[]{:S(2)}) collective-permute-start(bf16[2,2,128,128]{3,2,1,0:T(8,128)(2,1)S(1)} %get-tuple-element.42), channel_id=1, source_target_pairs={{4,0},{6,2},{0,4},{2,6},{5,1},{7,3},{1,5},{3,7},{12,8},{14,10},{8,... | collective-permute-start | bytes 393224 | tf_op jit(solution)/shard_map/ppermute | solution.py:241
  66.8 7.5 %collective-permute-start.8 = (bf16[2,2,128,128]{3,2,1,0:T(8,128)(2,1)S(1)}, bf16[2,2,128,128]{3,2,1,0:T(8,128)(2,1)S(1)}, u32[]{:S(2)}, u32[]{:S(2)}) collective-permute-start(bf16[2,2,128,128]{3,2,1,0:T(8,128)(2,1)S(1)} %get-tuple-element.43), channel_id=1, source_target_pairs={{2,0},{4,2},{6,4},{0,6},{3,1},{5,3},{7,5},{1,7},{10,8},{12,10},{14... | collective-permute-start | bytes 393224 | tf_op jit(solution)/shard_map/ppermute | solution.py:241
  67.4 6.9 %collective-permute-start.11 = (bf16[2,2,128,128]{3,2,1,0:T(8,128)(2,1)S(1)}, bf16[2,2,128,128]{3,2,1,0:T(8,128)(2,1)S(1)}, u32[]{:S(2)}, u32[]{:S(2)}) collective-permute-start(bf16[2,2,128,128]{3,2,1,0:T(8,128)(2,1)S(1)} %get-tuple-element.46), channel_id=1, source_target_pairs={{4,6},{5,7},{12,14},{13,15},{20,22},{21,23},{28,30},{29,31},{36,38... | collective-permute-start | bytes 393224 | tf_op jit(solution)/shard_map/ppermute | solution.py:241
  68.1 6.3 %collective-permute-start.12 = (bf16[2,2,128,128]{3,2,1,0:T(8,128)(2,1)S(1)}, bf16[2,2,128,128]{3,2,1,0:T(8,128)(2,1)S(1)}, u32[]{:S(2)}, u32[]{:S(2)}) collective-permute-start(bf16[2,2,128,128]{3,2,1,0:T(8,128)(2,1)S(1)} %get-tuple-element.47), channel_id=1, source_target_pairs={{2,6},{3,7},{10,14},{11,15},{18,22},{19,23},{26,30},{27,31},{34,38... | collective-permute-start | bytes 393224 | tf_op jit(solution)/shard_map/ppermute | solution.py:241
  69.8 7.1 %collective-permute-start.13 = (bf16[2,2,128,128]{3,2,1,0:T(8,128)(2,1)S(1)}, bf16[2,2,128,128]{3,2,1,0:T(8,128)(2,1)S(1)}, u32[]{:S(2)}, u32[]{:S(2)}) collective-permute-start(bf16[2,2,128,128]{3,2,1,0:T(8,128)(2,1)S(1)} %get-tuple-element.48), channel_id=1, source_target_pairs={{0,6},{1,7},{8,14},{9,15},{16,22},{17,23},{24,30},{25,31},{32,38},... | collective-permute-start | bytes 393224 | tf_op jit(solution)/shard_map/ppermute | solution.py:241

commit v4 on v3

--- a/solution.py
+++ b/solution.py
@@ -107,10 +107,10 @@
     )(live_counts, series, tapers, turns, table)
 
 
-def pair_kernel(wanted, *refs):
+def pair_kernel(wanted, kept, *refs):
     later, mine_wide, other_wide = refs[-3:]
     outs = refs[-3 - RING : -3]
-    inputs = refs[: -3 - RING]
+    inputs = refs[: -3 - RING - kept]
     y, core = lax.axis_index("y"), lax.axis_index("core")
     rows = inputs[0].shape[1] // K
     lane = lax.broadcasted_iota(jnp.int32, (BW, BW), 1)
@@ -179,13 +179,13 @@
                     outs[step][at, 1] = piece[BW:]
 
 
-def pair_products(wanted, mine, other):
-    pairs = max(len(offsets) for offsets in wanted.values())
+def pair_products(wanted, pairs, mine, other, filled=()):
     reach = sum(block.shape[0] // RING for block in mine) - min(wanted)
     whole = pl.BlockSpec(memory_space=pltpu.VMEM)
+    inputs = len(mine) + len(other)
     return pl.pallas_call(
-        functools.partial(pair_kernel, wanted),
-        in_specs=[whole] * (len(mine) + len(other)),
+        functools.partial(pair_kernel, wanted, len(filled)),
+        in_specs=[whole] * (inputs + len(filled)),
         out_specs=[whole] * RING,
         out_shape=[jax.ShapeDtypeStruct((pairs, 2, BW, BW), jnp.bfloat16)] * RING,
         scratch_shapes=[
@@ -193,23 +193,24 @@
             pltpu.VMEM((reach * BW, K * 2 * BW), jnp.bfloat16),
             pltpu.VMEM((reach * BW, K * 2 * BW), jnp.bfloat16),
         ],
+        input_output_aliases={inputs + at: at for at in range(len(filled))},
         compiler_params=pltpu.CompilerParams(vmem_limit_bytes=VMEM_LIMIT),
         cost_estimate=pl.CostEstimate(flops=1, bytes_accessed=1, transcendentals=0),
-    )(*mine, *other)
+    )(*mine, *other, *filled)
 
 
 PLANE = {0: (0, 1, 2), 1: (0, 1, 2), 2: (0, 1, 2), 3: (0,)}
-NEAR = {0: (3, 4), 1: (3, 4), 2: (3, 4), 3: (1, 2)}
-FAR = {3: (3, 4)}
+REST = {0: (3, 4), 1: (3, 4)}
+AHEAD = {2: (3, 4), 3: (1, 2, 3, 4)}
 
 
 def slots_kernel(offsets, counts, *refs):
     out = refs[-1]
     y, count = lax.axis_index("y"), counts[0]
-    parts = [refs[at * RING : (at + 1) * RING] for at in range(3)]
+    parts = [refs[at * RING : (at + 1) * RING] for at in range(2)]
 
     def place(target):
-        for group, wanted in zip(parts, (PLANE, NEAR, FAR)):
+        for group, wanted in zip(parts, (PLANE, REST | AHEAD)):
             for at, offset in enumerate(wanted.get(target, ())):
                 slot = 0
                 for step in range(1, SLOTS):
@@ -227,17 +228,17 @@
     whole = pl.BlockSpec(memory_space=pltpu.VMEM)
     return pl.pallas_call(
         slots_kernel,
-        in_specs=[pl.BlockSpec(memory_space=pltpu.SMEM)] * 2 + [whole] * (3 * RING),
+        in_specs=[pl.BlockSpec(memory_space=pltpu.SMEM)] * 2 + [whole] * (2 * RING),
         out_specs=whole,
         out_shape=jax.ShapeDtypeStruct((SLOTS, 2, RING, BW, BW), jnp.float32),
         compiler_params=pltpu.CompilerParams(vmem_limit_bytes=VMEM_LIMIT),
     )(offsets, counts, *parts)
 
 
-def sent_to(targets, pieces):
+def sent_along(pieces):
     moved = [pieces[0]]
     for distance in range(1, RING):
-        routes = [((target - distance) % RING, target) for target in targets]
+        routes = [(y, (y + distance) % RING) for y in range(RING)]
         moved.append(lax.ppermute(pieces[distance], "y", routes))
     return moved
 
@@ -247,21 +248,15 @@
     next_plane = [(i, (i - 1) % RING) for i in range(RING)]
     spectra = block_spectra(live_channels, series[0], tapers, turns, table)
     mine = lax.all_to_all(spectra, ("y", "freq"), 0, 0)
-    near = lax.ppermute(mine[:RING], "z", next_plane)
-    far = lax.ppermute(mine[RING : 2 * RING], "z", next_plane)
+    ahead = lax.ppermute(mine[: 2 * RING], "z", next_plane)
     other = lax.ppermute(mine, "core", swap)
-    plane = pair_products(PLANE, [mine], [other])
-    near, _ = lax.optimization_barrier((near, plane[0]))
-    plane = sent_to(PLANE, plane)
-    other_near = lax.ppermute(near, "core", swap)
-    close = pair_products(NEAR, [mine, near], [other, other_near])
-    far, _ = lax.optimization_barrier((far, close[0]))
-    close, plane = lax.optimization_barrier((close, plane))
-    close = sent_to(NEAR, close)
-    other_far = lax.ppermute(far, "core", swap)
-    last = pair_products(FAR, [mine, near, far], [other, other_near, other_far])
-    last = sent_to(FAR, last)
-    parts = plane + close + last
+    plane = sent_along(pair_products(PLANE, 3, [mine], [other]))
+    rest = pair_products(REST, 4, [mine], [other])
+    ahead, *held = lax.optimization_barrier((ahead, *plane, *rest))
+    plane, rest = held[:RING], held[RING:]
+    other_ahead = lax.ppermute(ahead, "core", swap)
+    rest = pair_products(AHEAD, 4, [mine, ahead], [other, other_ahead], rest)
+    parts = plane + sent_along(rest)
     return slots_output(pair_offset, pair_count, parts)[None]
 
 

time: 80 us -> 76.1 us (0.951)
  starting transfers between devices: 20.3 us -> 11.5 us
  waiting for transfers between devices: 15.9 us -> 21.8 us
    ppermute x13 -> x8, starting transfers between devices: 20.3 us -> 11.5 us  [the longest x6 7.42 us: sent_along(): moved.append(lax.ppermute(pieces[distance], 'y', routes))]
    ppermute x13 -> x8, waiting for transfers between devices: 15.9 us -> 21.8 us  [the longest x6 12.3 us: sent_along(): moved.append(lax.ppermute(pieces[distance], 'y', routes))]
  transfers between devices with their start and end apart: 14 -> 9, of which waited for: 6 -> 7; matrix products, arithmetic and copies ran while one was open for 0% -> 0% of each run, Pallas kernels for 7% -> 5%
where the time goes in v4:
time: 76.1 us; the launch traced here: 75.7 us
  blocking collectives  27.1 us (36%)
  waiting for transfers between devices  21.8 us (29%)
  Pallas kernels  13.9 us (18%)
  starting transfers between devices  11.5 us (15%)
  between operations  1.35 us (2%)
    all_to_all x1, blocking collectives, body(): mine = lax.all_to_all(spectra, ('y', 'freq'), 0, 0)  27.1 us
    ppermute x6, waiting for transfers between devices, sent_along(): moved.append(lax.ppermute(pieces[distance], 'y', routes))  12.3 us
    ppermute x6, starting transfers between devices, sent_along(): moved.append(lax.ppermute(pieces[distance], 'y', routes))  7.42 us
    ppermute x1, waiting for transfers between devices, body(): ahead = lax.ppermute(mine[:2 * RING], 'z', next_plane)  7.41 us
    pallas_call x1, Pallas kernels, block_spectra(): pl.pallas_call(spectra_kernel, grid=(OWNERS * 2 * GROUP // WIDTH,), in_sp...  6.74 us
    pallas_call x3, Pallas kernels, pair_products(): pl.pallas_call(functools.partial(pair_kernel, wanted, len(filled)), in_sp...  4.94 us
    ppermute x1, starting transfers between devices, body(): ahead = lax.ppermute(mine[:2 * RING], 'z', next_plane)  4.11 us
    pallas_call x1, Pallas kernels, slots_output(): pl.pallas_call(slots_kernel, in_specs=[pl.BlockSpec(memory_space=pltpu.SM...  2.24 us
  transfers between devices with their start and end apart: 9, of which 7 were waited for; matrix products, arithmetic and copies ran while one was open for 0% of the time, Pallas kernels for 5%

profile of v4, /device:TPU:0, one launch (start us, length us, event | category | flops | bytes accessed | tf_op | source)
XLA Modules:
  0.0 75.7 jit_solution(15741441867821571799)
XLA Ops:
  0.7 6.7 %shard_map.73 = bf16[16,160,256]{2,1,0:T(8,128)(2,1)} custom-call(s32[1]{0:T(128)S(6)} %copy.16.live_counts, bf16[32,6000]{1,0:T(8,128)(2,1)} %bitcast.2, f32[5,6000]{1,0:T(8,128)} %tapers.1, f32[6,1024]{1,0:T(8,128)} %constant.4.clone.turns, bf16[2048,1024]{1,0:T(8,128)(2,1)} %constant.5.clone.table), custom_call_target="tpu_custom_call" | custom-call | tf_op jit(solution)/shard_map/pallas_call | solution.py:88
  7.4 27.1 %all_to_all.5.refs_0_ = bf16[16,160,256]{2,1,0:T(8,128)(2,1)S(1)} all-to-all(bf16[16,160,256]{2,1,0:T(8,128)(2,1)} %shard_map.73), channel_id=1, replica_groups=mesh['freq'=4,'z'=4,'y'=4,'core'=2] {'y','freq'}, dimensions={0} | all-to-all | bytes 2621440 | tf_op jit(solution)/shard_map/all_to_all | solution.py:250
  34.5 0.0 collective-permute-start.1
  34.5 4.1 %collective-permute-start = (bf16[8,160,256]{2,1,0:T(8,128)(2,1)S(1)}, bf16[8,160,256]{2,1,0:T(8,128)(2,1)S(1)}, u32[]{:S(2)}, u32[]{:S(2)}) collective-permute-start(bf16[8,160,256]{2,1,0:T(8,128)(2,1)S(1)} %slice.4), channel_id=1, source_target_pairs={{0,24},{8,0},{16,8},{24,16},{1,25},{9,1},{17,9},{25,17},{2,26},{10... | collective-permute-start | bytes 1966088 | tf_op jit(solution)/shard_map/ppermute | solution.py:251
  38.6 0.0 collective-permute-done.1.refs_1_.refs_2_
  38.6 2.5 %shard_map.74 = (bf16[3,2,128,128]{3,2,1,0:T(8,128)(2,1)S(1)}, bf16[3,2,128,128]{3,2,1,0:T(8,128)(2,1)S(1)}, bf16[3,2,128,128]{3,2,1,0:T(8,128)(2,1)S(1)}, bf16[3,2,128,128]{3,2,1,0:T(8,128)(2,1)S(1)}) custom-call(bf16[16,160,256]{2,1,0:T(8,128)(2,1)S(1)} %all_to_all.5.refs_0_, bf16[16,160,256]{2,1,0:T(8,128)(2,1)S(1)} %collective-permute-done.1.refs_1_.refs_2_), custom_call_target="tpu_custom_call" | custom-call | flops 1 | bytes 1 | tf_op jit(solution)/shard_map/pallas_call | solution.py:186
  41.1 0.1 collective-permute-start.2
  41.2 2.3 %collective-permute-start.3 = (bf16[3,2,128,128]{3,2,1,0:T(8,128)(2,1)S(1)}, bf16[3,2,128,128]{3,2,1,0:T(8,128)(2,1)S(1)}, u32[]{:S(2)}, u32[]{:S(2)}) collective-permute-start(bf16[3,2,128,128]{3,2,1,0:T(8,128)(2,1)S(1)} %get-tuple-element.28), channel_id=1, source_target_pairs={{0,4},{2,6},{4,0},{6,2},{1,5},{3,7},{5,1},{7,3},{8,12},{10,14},{12... | collective-permute-start | bytes 589832 | tf_op jit(solution)/shard_map/ppermute | solution.py:242
  43.5 1.2 %collective-permute-start.4 = (bf16[3,2,128,128]{3,2,1,0:T(8,128)(2,1)S(1)}, bf16[3,2,128,128]{3,2,1,0:T(8,128)(2,1)S(1)}, u32[]{:S(2)}, u32[]{:S(2)}) collective-permute-start(bf16[3,2,128,128]{3,2,1,0:T(8,128)(2,1)S(1)} %get-tuple-element.29), channel_id=1, source_target_pairs={{0,6},{2,0},{4,2},{6,4},{1,7},{3,1},{5,3},{7,5},{8,14},{10,8},{12,... | collective-permute-start | bytes 589832 | tf_op jit(solution)/shard_map/ppermute | solution.py:242
  44.6 1.2 %shard_map.75 = (bf16[4,2,128,128]{3,2,1,0:T(8,128)(2,1)S(1)}, bf16[4,2,128,128]{3,2,1,0:T(8,128)(2,1)S(1)}, bf16[4,2,128,128]{3,2,1,0:T(8,128)(2,1)S(1)}, bf16[4,2,128,128]{3,2,1,0:T(8,128)(2,1)S(1)}) custom-call(bf16[16,160,256]{2,1,0:T(8,128)(2,1)S(1)} %all_to_all.5.refs_0_, bf16[16,160,256]{2,1,0:T(8,128)(2,1)S(1)} %collective-permute-done.1.refs_1_.refs_2_), custom_call_target="tpu_custom_call" | custom-call | flops 1 | bytes 1 | tf_op jit(solution)/shard_map/pallas_call | solution.py:186
  45.9 7.4 %collective-permute-done.refs_1_ = bf16[8,160,256]{2,1,0:T(8,128)(2,1)S(1)} collective-permute-done((bf16[8,160,256]{2,1,0:T(8,128)(2,1)S(1)}, bf16[8,160,256]{2,1,0:T(8,128)(2,1)S(1)}, u32[]{:S(2)}, u32[]{:S(2)}) %collective-permute-start) | collective-permute-done | bytes 655392 | tf_op jit(solution)/shard_map/ppermute | solution.py:251
  53.3 0.3 collective-permute-done.2.refs_1_
  53.6 0.0 collective-permute-done.3.refs_2_
  53.6 0.6 collective-permute-done.4.refs_3_
  54.2 0.0 collective-permute-start.5
  54.2 2.1 %collective-permute-done.5.refs_3_ = bf16[8,160,256]{2,1,0:T(8,128)(2,1)S(1)} collective-permute-done((bf16[8,160,256]{2,1,0:T(8,128)(2,1)S(1)}, bf16[8,160,256]{2,1,0:T(8,128)(2,1)S(1)}, u32[]{:S(2)}, u32[]{:S(2)}) %collective-permute-start.5) | collective-permute-done | bytes 655392 | tf_op jit(solution)/shard_map/ppermute | solution.py:257
  56.3 1.3 %shard_map.76 = (bf16[4,2,128,128]{3,2,1,0:T(8,128)(2,1)S(1)}, bf16[4,2,128,128]{3,2,1,0:T(8,128)(2,1)S(1)}, bf16[4,2,128,128]{3,2,1,0:T(8,128)(2,1)S(1)}, bf16[4,2,128,128]{3,2,1,0:T(8,128)(2,1)S(1)}) custom-call(bf16[16,160,256]{2,1,0:T(8,128)(2,1)S(1)} %all_to_all.5.refs_0_, ...), custom_call_target="tpu_custom_call", output_to_operand_aliasing={{0}: (4, {}), {1}: (5, {}), {2}: (6, {}), {3}: (7, {})} | custom-call | flops 1 | bytes 1 | tf_op jit(solution)/shard_map/pallas_call | solution.py:186
  57.6 0.3 collective-permute-start.6
  57.9 3.6 %collective-permute-start.7 = (bf16[4,2,128,128]{3,2,1,0:T(8,128)(2,1)S(1)}, bf16[4,2,128,128]{3,2,1,0:T(8,128)(2,1)S(1)}, u32[]{:S(2)}, u32[]{:S(2)}) collective-permute-start(bf16[4,2,128,128]{3,2,1,0:T(8,128)(2,1)S(1)} %get-tuple-element.45), channel_id=1, source_target_pairs={{0,4},{2,6},{4,0},{6,2},{1,5},{3,7},{5,1},{7,3},{8,12},{10,14},{12... | collective-permute-start | bytes 786440 | tf_op jit(solution)/shard_map/ppermute | solution.py:242
  61.5 0.0 collective-permute-start.8
  62.1 5.3 %collective-permute-done.6.refs_5_ = bf16[4,2,128,128]{3,2,1,0:T(8,128)(2,1)S(1)} collective-permute-done((bf16[4,2,128,128]{3,2,1,0:T(8,128)(2,1)S(1)}, bf16[4,2,128,128]{3,2,1,0:T(8,128)(2,1)S(1)}, u32[]{:S(2)}, u32[]{:S(2)}) %collective-permute-start.6) | collective-permute-done | bytes 262176 | tf_op jit(solution)/shard_map/ppermute | solution.py:242
  67.5 6.0 %collective-permute-done.7.refs_6_ = bf16[4,2,128,128]{3,2,1,0:T(8,128)(2,1)S(1)} collective-permute-done((bf16[4,2,128,128]{3,2,1,0:T(8,128)(2,1)S(1)}, bf16[4,2,128,128]{3,2,1,0:T(8,128)(2,1)S(1)}, u32[]{:S(2)}, u32[]{:S(2)}) %collective-permute-start.7) | collective-permute-done | bytes 262176 | tf_op jit(solution)/shard_map/ppermute | solution.py:242
  73.4 0.1 collective-permute-done.8.refs_7_
  73.5 2.2 %shard_map.77 = f32[5,2,4,128,128]{4,3,2,1,0:T(8,128)} custom-call(s32[1,5]{1,0:T(1,128)S(1)} %copy-done, s32[1]{0:T(128)S(6)} %copy.17.counts, bf16[3,2,128,128]{3,2,1,0:T(8,128)(2,1)S(1)} %get-tuple-element.34.refs_0_, bf16[3,2,128,128]{3,2,1,0:T(8,128)(2,1)S(1)} %collective-permute-done.2.refs_1_, ...), custom_call_target="tpu_custom_call" | custom-call | tf_op jit(solution)/shard_map/pallas_call | solution.py:229
  (3 shorter events, 0.0 us)
Async XLA Ops:
  34.5 4.2 %collective-permute-start.1 = (bf16[16,160,256]{2,1,0:T(8,128)(2,1)S(1)}, bf16[16,160,256]{2,1,0:T(8,128)(2,1)S(1)}, u32[]{:S(2)}, u32[]{:S(2)}) collective-permute-start(bf16[16,160,256]{2,1,0:T(8,128)(2,1)S(1)} %all_to_all.5.refs_0_), channel_id=1, source_target_pairs={{0,1},{1,0},{2,3},{3,2},{4,5},{5,4},{6,7},{7,6},{8,9},{9,8},{10,11... | collective-permute-start | bytes 3932168 | tf_op jit(solution)/shard_map/ppermute | solution.py:252
  34.5 18.8 %collective-permute-start = (bf16[8,160,256]{2,1,0:T(8,128)(2,1)S(1)}, bf16[8,160,256]{2,1,0:T(8,128)(2,1)S(1)}, u32[]{:S(2)}, u32[]{:S(2)}) collective-permute-start(bf16[8,160,256]{2,1,0:T(8,128)(2,1)S(1)} %slice.4), channel_id=1, source_target_pairs={{0,24},{8,0},{16,8},{24,16},{1,25},{9,1},{17,9},{25,17},{2,26},{10... | collective-permute-start | bytes 1966088 | tf_op jit(solution)/shard_map/ppermute | solution.py:251
  41.1 12.5 %collective-permute-start.2 = (bf16[3,2,128,128]{3,2,1,0:T(8,128)(2,1)S(1)}, bf16[3,2,128,128]{3,2,1,0:T(8,128)(2,1)S(1)}, u32[]{:S(2)}, u32[]{:S(2)}) collective-permute-start(bf16[3,2,128,128]{3,2,1,0:T(8,128)(2,1)S(1)} %get-tuple-element.27), channel_id=1, source_target_pairs={{0,2},{2,4},{4,6},{6,0},{1,3},{3,5},{5,7},{7,1},{8,10},{10,12},{12... | collective-permute-start | bytes 589832 | tf_op jit(solution)/shard_map/ppermute | solution.py:242
  41.2 12.4 %collective-permute-start.3 = (bf16[3,2,128,128]{3,2,1,0:T(8,128)(2,1)S(1)}, bf16[3,2,128,128]{3,2,1,0:T(8,128)(2,1)S(1)}, u32[]{:S(2)}, u32[]{:S(2)}) collective-permute-start(bf16[3,2,128,128]{3,2,1,0:T(8,128)(2,1)S(1)} %get-tuple-element.28), channel_id=1, source_target_pairs={{0,4},{2,6},{4,0},{6,2},{1,5},{3,7},{5,1},{7,3},{8,12},{10,14},{12... | collective-permute-start | bytes 589832 | tf_op jit(solution)/shard_map/ppermute | solution.py:242
  43.5 10.8 %collective-permute-start.4 = (bf16[3,2,128,128]{3,2,1,0:T(8,128)(2,1)S(1)}, bf16[3,2,128,128]{3,2,1,0:T(8,128)(2,1)S(1)}, u32[]{:S(2)}, u32[]{:S(2)}) collective-permute-start(bf16[3,2,128,128]{3,2,1,0:T(8,128)(2,1)S(1)} %get-tuple-element.29), channel_id=1, source_target_pairs={{0,6},{2,0},{4,2},{6,4},{1,7},{3,1},{5,3},{7,5},{8,14},{10,8},{12,... | collective-permute-start | bytes 589832 | tf_op jit(solution)/shard_map/ppermute | solution.py:242
  54.2 19.2 %copy-start = (s32[1,5]{1,0:T(1,128)S(1)}, s32[1,5]{1,0:T(1,128)}, u32[]{:S(2)}) copy-start(s32[1,5]{1,0:T(1,128)} %offsets.1) | copy-start | bytes 64
  54.2 2.1 %collective-permute-start.5 = (bf16[8,160,256]{2,1,0:T(8,128)(2,1)S(1)}, bf16[8,160,256]{2,1,0:T(8,128)(2,1)S(1)}, u32[]{:S(2)}, u32[]{:S(2)}) collective-permute-start(bf16[8,160,256]{2,1,0:T(8,128)(2,1)S(1)} %collective-permute-done.refs_1_), channel_id=1, source_target_pairs={{0,1},{1,0},{2,3},{3,2},{4,5},{5,4},{6,7},{7,6},{8,9},{9,8},{10,11... | collective-permute-start | bytes 1966088 | tf_op jit(solution)/shard_map/ppermute | solution.py:257
  57.6 9.9 %collective-permute-start.6 = (bf16[4,2,128,128]{3,2,1,0:T(8,128)(2,1)S(1)}, bf16[4,2,128,128]{3,2,1,0:T(8,128)(2,1)S(1)}, u32[]{:S(2)}, u32[]{:S(2)}) collective-permute-start(bf16[4,2,128,128]{3,2,1,0:T(8,128)(2,1)S(1)} %get-tuple-element.44), channel_id=1, source_target_pairs={{0,2},{2,4},{4,6},{6,0},{1,3},{3,5},{5,7},{7,1},{8,10},{10,12},{12... | collective-permute-start | bytes 786440 | tf_op jit(solution)/shard_map/ppermute | solution.py:242
  57.9 15.5 %collective-permute-start.7 = (bf16[4,2,128,128]{3,2,1,0:T(8,128)(2,1)S(1)}, bf16[4,2,128,128]{3,2,1,0:T(8,128)(2,1)S(1)}, u32[]{:S(2)}, u32[]{:S(2)}) collective-permute-start(bf16[4,2,128,128]{3,2,1,0:T(8,128)(2,1)S(1)} %get-tuple-element.45), channel_id=1, source_target_pairs={{0,4},{2,6},{4,0},{6,2},{1,5},{3,7},{5,1},{7,3},{8,12},{10,14},{12... | collective-permute-start | bytes 786440 | tf_op jit(solution)/shard_map/ppermute | solution.py:242
  61.5 12.0 %collective-permute-start.8 = (bf16[4,2,128,128]{3,2,1,0:T(8,128)(2,1)S(1)}, bf16[4,2,128,128]{3,2,1,0:T(8,128)(2,1)S(1)}, u32[]{:S(2)}, u32[]{:S(2)}) collective-permute-start(bf16[4,2,128,128]{3,2,1,0:T(8,128)(2,1)S(1)} %get-tuple-element.46), channel_id=1, source_target_pairs={{0,6},{2,0},{4,2},{6,4},{1,7},{3,1},{5,3},{7,5},{8,14},{10,8},{12,... | collective-permute-start | bytes 786440 | tf_op jit(solution)/shard_map/ppermute | solution.py:242

commit v5 on v4

--- a/solution.py
+++ b/solution.py
@@ -37,71 +37,102 @@
     return turns.astype(np.float32), table
 
 
-def spectra_kernel(live_counts, series, tapers, turns, table, out, plain, turned):
+def spectra_kernel(*refs):
+    live_in, series_in, tapers_in, turns_in, table_in, out = refs[:6]
+    live, series, tapers, turns, table, spectra, plain, turned, arrived, sent = refs[6:]
     rows, samples = series.shape
     total = K * rows
-
-    @pl.when(pl.program_id(0) == 0)
-    def _():
-        first = lax.axis_index("freq") * rows
-        channel = first + lax.broadcasted_iota(jnp.int32, (rows, QUARTER), 0)
-        working = channel < live_counts[0]
-
-        def tapered(k, quarter):
-            lanes = slice(quarter * QUARTER, min((quarter + 1) * QUARTER, samples))
-            product = series[:, lanes].astype(jnp.float32) * tapers[k : k + 1, lanes]
-            short = QUARTER - product.shape[1]
-            if short:
-                product = jnp.concatenate(
-                    [product, jnp.zeros((rows, short), jnp.float32)], axis=1
+    owners = WIDTH // (2 * GROUP)
+    steps = OWNERS // owners
+    small = ((live_in, live), (series_in, series), (tapers_in, tapers), (turns_in, turns))
+    loads = [
+        pltpu.make_async_copy(source, to, arrived.at[at]) for at, (source, to) in enumerate(small)
+    ]
+    for step in range(steps):
+        columns = pl.ds(step * WIDTH, WIDTH)
+        loads.append(
+            pltpu.make_async_copy(
+                table_in.at[:, columns], table.at[:, columns], arrived.at[len(small) + step]
+            )
+        )
+    for load in loads[: len(small)]:
+        load.start()
+    for load in loads[: len(small)]:
+        load.wait()
+    for load in loads[len(small) :]:
+        load.start()
+
+    first = lax.axis_index("freq") * rows
+    channel = first + lax.broadcasted_iota(jnp.int32, (rows, QUARTER), 0)
+    working = channel < live[0]
+
+    def tapered(k, quarter):
+        lanes = slice(quarter * QUARTER, min((quarter + 1) * QUARTER, samples))
+        product = series[:, lanes].astype(jnp.float32) * tapers[k : k + 1, lanes]
+        short = QUARTER - product.shape[1]
+        if short:
+            product = jnp.concatenate([product, jnp.zeros((rows, short), jnp.float32)], axis=1)
+        product = jnp.where(working, product, 0.0)
+        return product.astype(jnp.bfloat16).astype(jnp.float32)
+
+    for k in range(K):
+        quarters = [tapered(k, 0) + tapered(k, 4), tapered(k, 1) + tapered(k, 5)]
+        quarters += [tapered(k, 2), tapered(k, 3)]
+        even, odd = quarters[0] + quarters[2], quarters[1] + quarters[3]
+        real, imag = quarters[0] - quarters[2], quarters[1] - quarters[3]
+        plain[k * rows : (k + 1) * rows, :] = (even + odd).astype(jnp.bfloat16)
+        for r, (p, q) in enumerate(((real, -imag), (even - odd, None), (real, imag))):
+            cos, sin = turns[2 * r : 2 * r + 1, :], turns[2 * r + 1 : 2 * r + 2, :]
+            at = r * total + k * rows
+            left, right = p * cos, -p * sin
+            if q is not None:
+                left, right = left + q * sin, right + q * cos
+            turned[at : at + rows, :QUARTER] = left.astype(jnp.bfloat16)
+            turned[at : at + rows, QUARTER:] = right.astype(jnp.bfloat16)
+
+    sends = []
+    for step in range(steps):
+        loads[len(small) + step].wait()
+        columns = slice(step * WIDTH, (step + 1) * WIDTH)
+        groups = [
+            jnp.dot(plain[...], table[:QUARTER, columns], preferred_element_type=jnp.float32)
+        ]
+        others = jnp.dot(turned[...], table[:, columns], preferred_element_type=jnp.float32)
+        groups += [others[r * total : (r + 1) * total] for r in range(3)]
+        for owner in range(owners):
+            lanes = slice(owner * 2 * GROUP, (owner + 1) * 2 * GROUP)
+            for pair in range(2):
+                bins = [group[:, lanes] for group in groups[2 * pair :][:2]]
+                spectra[step * owners + owner, :, pair * BW : (pair + 1) * BW] = (
+                    jnp.concatenate(bins, axis=1).astype(jnp.bfloat16)
                 )
-            product = jnp.where(working, product, 0.0)
-            return product.astype(jnp.bfloat16).astype(jnp.float32)
-
-        for k in range(K):
-            quarters = [tapered(k, 0) + tapered(k, 4), tapered(k, 1) + tapered(k, 5)]
-            quarters += [tapered(k, 2), tapered(k, 3)]
-            even, odd = quarters[0] + quarters[2], quarters[1] + quarters[3]
-            real, imag = quarters[0] - quarters[2], quarters[1] - quarters[3]
-            plain[k * rows : (k + 1) * rows, :] = (even + odd).astype(jnp.bfloat16)
-            for r, (p, q) in enumerate(((real, -imag), (even - odd, None), (real, imag))):
-                cos, sin = turns[2 * r : 2 * r + 1, :], turns[2 * r + 1 : 2 * r + 2, :]
-                at = r * total + k * rows
-                left, right = p * cos, -p * sin
-                if q is not None:
-                    left, right = left + q * sin, right + q * cos
-                turned[at : at + rows, :QUARTER] = left.astype(jnp.bfloat16)
-                turned[at : at + rows, QUARTER:] = right.astype(jnp.bfloat16)
-
-    groups = [jnp.dot(plain[...], table[:QUARTER, :], preferred_element_type=jnp.float32)]
-    others = jnp.dot(turned[...], table[...], preferred_element_type=jnp.float32)
-    groups += [others[r * total : (r + 1) * total] for r in range(3)]
-    for owner in range(WIDTH // (2 * GROUP)):
-        lanes = slice(owner * 2 * GROUP, (owner + 1) * 2 * GROUP)
-        for pair in range(2):
-            bins = jnp.concatenate([group[:, lanes] for group in groups[2 * pair :][:2]], axis=1)
-            out[owner, :, pair * BW : (pair + 1) * BW] = bins.astype(jnp.bfloat16)
+        done = pl.ds(step * owners, owners)
+        sends.append(pltpu.make_async_copy(spectra.at[done], out.at[done], sent.at[step]))
+        sends[-1].start()
+    for send in sends:
+        send.wait()
 
 
 def block_spectra(live_counts, series, tapers, turns, table):
-    rows, samples = series.shape
+    rows = series.shape[0]
+    shape = (OWNERS, K * rows, 2 * BW)
+    steps = OWNERS * 2 * GROUP // WIDTH
     return pl.pallas_call(
         spectra_kernel,
-        grid=(OWNERS * 2 * GROUP // WIDTH,),
-        in_specs=[
-            pl.BlockSpec(memory_space=pltpu.SMEM),
-            pl.BlockSpec((rows, samples), lambda step: (0, 0)),
-            pl.BlockSpec((K, samples), lambda step: (0, 0)),
-            pl.BlockSpec((6, QUARTER), lambda step: (0, 0)),
-            pl.BlockSpec((2 * QUARTER, WIDTH), lambda step: (0, step)),
-        ],
-        out_specs=pl.BlockSpec(
-            (WIDTH // (2 * GROUP), K * rows, 2 * BW), lambda step: (step, 0, 0)
-        ),
-        out_shape=jax.ShapeDtypeStruct((OWNERS, K * rows, 2 * BW), jnp.bfloat16),
+        in_specs=[pl.BlockSpec(memory_space=pl.ANY)] * 5,
+        out_specs=pl.BlockSpec(memory_space=pl.ANY),
+        out_shape=jax.ShapeDtypeStruct(shape, jnp.bfloat16),
         scratch_shapes=[
+            pltpu.SMEM(live_counts.shape, live_counts.dtype),
+            pltpu.VMEM(series.shape, series.dtype),
+            pltpu.VMEM(tapers.shape, tapers.dtype),
+            pltpu.VMEM(turns.shape, turns.dtype),
+            pltpu.VMEM(table.shape, table.dtype),
+            pltpu.VMEM(shape, jnp.bfloat16),
             pltpu.VMEM((K * rows, QUARTER), jnp.bfloat16),
             pltpu.VMEM((3 * K * rows, 2 * QUARTER), jnp.bfloat16),
+            pltpu.SemaphoreType.DMA((4 + steps,)),
+            pltpu.SemaphoreType.DMA((steps,)),
         ],
         compiler_params=pltpu.CompilerParams(vmem_limit_bytes=STREAM_VMEM_LIMIT),
     )(live_counts, series, tapers, turns, table)
@@ -204,35 +235,55 @@
 AHEAD = {2: (3, 4), 3: (1, 2, 3, 4)}
 
 
-def slots_kernel(offsets, counts, *refs):
-    out = refs[-1]
+def slots_kernel(sources, offsets, counts, *refs):
+    out, wide, done = refs[-3:]
     y, count = lax.axis_index("y"), counts[0]
-    parts = [refs[at * RING : (at + 1) * RING] for at in range(2)]
 
     def place(target):
-        for group, wanted in zip(parts, (PLANE, REST | AHEAD)):
-            for at, offset in enumerate(wanted.get(target, ())):
+        copies = []
+        for (distance, first_set), group in zip(sources, refs):
+            wanted = PLANE if first_set else REST | AHEAD
+            band = (target - distance) % RING
+            for at, offset in enumerate(wanted[target]):
                 slot = 0
                 for step in range(1, SLOTS):
                     slot += jnp.where(offsets[0, step] == offset, step, 0)
                 live = (slot < count).astype(jnp.float32)
-                for distance in range(RING):
-                    band = (target - distance) % RING
-                    out[slot, :, band] = group[distance][at].astype(jnp.float32) * live
+                piece = len(copies)
+                wide[piece] = group[at].astype(jnp.float32) * live
+                copies.append(
+                    pltpu.make_async_copy(wide.at[piece], out.at[slot, :, band], done.at[piece])
+                )
+                copies[-1].start()
+        for copy in copies:
+            copy.wait()
 
     for target in range(RING):
         pl.when(y == target)(functools.partial(place, target))
 
 
-def slots_output(offsets, counts, parts):
+def slots_output(offsets, counts, sources, groups, begun=None):
+    pieces = max(
+        sum(len((PLANE if first_set else REST | AHEAD)[target]) for _, first_set in sources)
+        for target in range(RING)
+    )
     whole = pl.BlockSpec(memory_space=pltpu.VMEM)
+    earlier = [] if begun is None else [begun]
     return pl.pallas_call(
-        slots_kernel,
-        in_specs=[pl.BlockSpec(memory_space=pltpu.SMEM)] * 2 + [whole] * (2 * RING),
-        out_specs=whole,
+        functools.partial(slots_kernel, sources),
+        in_specs=[pl.BlockSpec(memory_space=pltpu.SMEM)] * 2
+        + [whole] * len(groups)
+        + [pl.BlockSpec(memory_space=pl.ANY)] * len(earlier),
+        out_specs=pl.BlockSpec(memory_space=pl.ANY),
         out_shape=jax.ShapeDtypeStruct((SLOTS, 2, RING, BW, BW), jnp.float32),
+        scratch_shapes=[
+            pltpu.VMEM((pieces, 2, BW, BW), jnp.float32),
+            pltpu.SemaphoreType.DMA((pieces,)),
+        ],
+        input_output_aliases={2 + len(groups): 0} if earlier else {},
         compiler_params=pltpu.CompilerParams(vmem_limit_bytes=VMEM_LIMIT),
-    )(offsets, counts, *parts)
+        cost_estimate=pl.CostEstimate(flops=1, bytes_accessed=1, transcendentals=0),
+    )(offsets, counts, *groups, *earlier)
 
 
 def sent_along(pieces):
@@ -256,8 +307,11 @@
     plane, rest = held[:RING], held[RING:]
     other_ahead = lax.ppermute(ahead, "core", swap)
     rest = pair_products(AHEAD, 4, [mine, ahead], [other, other_ahead], rest)
-    parts = plane + sent_along(rest)
-    return slots_output(pair_offset, pair_count, parts)[None]
+    rest = sent_along(rest)
+    early = [(distance, True) for distance in range(RING)] + [(0, False)]
+    late = [(distance, False) for distance in range(1, RING)]
+    out = slots_output(pair_offset, pair_count, early, plane + rest[:1])
+    return slots_output(pair_offset, pair_count, late, rest[1:], out)[None]
 
 
 def solution(mesh):

time: 76.1 us -> 75.1 us (0.987)
  waiting for transfers between devices: 21.8 us -> 19.8 us
  Pallas kernels: 13.9 us -> 14.9 us
    ppermute x6, waiting for transfers between devices: 12.3 us -> 10.4 us  [sent_along(): moved.append(lax.ppermute(pieces[distance], 'y', routes))]
    pallas_call x2 -> x3, Pallas kernels: 8.98 us -> 9.88 us  [the longest x1 6.42 us: block_spectra(): pl.pallas_call(spectra_kernel, in_specs=[pl.BlockSpec(memory_space=pl.ANY...]
  transfers between devices with their start and end apart: 9 -> 9, of which waited for: 7 -> 7; matrix products, arithmetic and copies ran while one was open for 0% -> 0% of each run, Pallas kernels for 5% -> 8%
where the time goes in v5:
time: 75.1 us; the launch traced here: 74.8 us
  blocking collectives  27.1 us (36%)
  waiting for transfers between devices  19.8 us (26%)
  Pallas kernels  14.9 us (20%)
  starting transfers between devices  11.5 us (15%)
  between operations  1.38 us (2%)
    all_to_all x1, blocking collectives, body(): mine = lax.all_to_all(spectra, ('y', 'freq'), 0, 0)  27.1 us
    ppermute x6, waiting for transfers between devices, sent_along(): moved.append(lax.ppermute(pieces[distance], 'y', routes))  10.4 us
    ppermute x6, starting transfers between devices, sent_along(): moved.append(lax.ppermute(pieces[distance], 'y', routes))  7.42 us
    ppermute x1, waiting for transfers between devices, body(): ahead = lax.ppermute(mine[:2 * RING], 'z', next_plane)  7.35 us
    pallas_call x1, Pallas kernels, block_spectra(): pl.pallas_call(spectra_kernel, in_specs=[pl.BlockSpec(memory_space=pl.ANY...  6.42 us
    pallas_call x3, Pallas kernels, pair_products(): pl.pallas_call(functools.partial(pair_kernel, wanted, len(filled)), in_sp...  5 us
    ppermute x1, starting transfers between devices, body(): ahead = lax.ppermute(mine[:2 * RING], 'z', next_plane)  4.11 us
    pallas_call x2, Pallas kernels, slots_output(): pl.pallas_call(functools.partial(slots_kernel, sources), in_specs=[pl.Blo...  3.45 us
  transfers between devices with their start and end apart: 9, of which 7 were waited for; matrix products, arithmetic and copies ran while one was open for 0% of the time, Pallas kernels for 8%

profile of v5, /device:TPU:0, one launch (start us, length us, event | category | flops | bytes accessed | tf_op | source)
XLA Modules:
  0.0 74.8 jit_solution(13046514472904656610)
XLA Ops:
  0.7 6.4 %shard_map.73 = bf16[16,160,256]{2,1,0:T(8,128)(2,1)} custom-call(s32[1]{0:T(128)S(6)} %copy.18.refs_0_, bf16[32,6000]{1,0:T(8,128)(2,1)} %bitcast.2, f32[5,6000]{1,0:T(8,128)} %refs_2_.1, f32[6,1024]{1,0:T(8,128)} %constant.4.clone.refs_3_, bf16[2048,1024]{1,0:T(8,128)(2,1)} %constant.5.clone.refs_4_), custom_call_target="tpu_custom_call" | custom-call | tf_op jit(solution)/shard_map/pallas_call | solution.py:120
  7.1 27.1 %all_to_all.5.refs_0_ = bf16[16,160,256]{2,1,0:T(8,128)(2,1)S(1)} all-to-all(bf16[16,160,256]{2,1,0:T(8,128)(2,1)} %shard_map.73), channel_id=1, replica_groups=mesh['freq'=4,'z'=4,'y'=4,'core'=2] {'y','freq'}, dimensions={0} | all-to-all | bytes 2621440 | tf_op jit(solution)/shard_map/all_to_all | solution.py:301
  34.2 0.0 collective-permute-start.1
  34.2 4.1 %collective-permute-start = (bf16[8,160,256]{2,1,0:T(8,128)(2,1)S(1)}, bf16[8,160,256]{2,1,0:T(8,128)(2,1)S(1)}, u32[]{:S(2)}, u32[]{:S(2)}) collective-permute-start(bf16[8,160,256]{2,1,0:T(8,128)(2,1)S(1)} %slice.4), channel_id=1, source_target_pairs={{0,24},{8,0},{16,8},{24,16},{1,25},{9,1},{17,9},{25,17},{2,26},{10... | collective-permute-start | bytes 1966088 | tf_op jit(solution)/shard_map/ppermute | solution.py:302
  38.3 0.0 collective-permute-done.1.refs_1_.refs_2_
  38.3 2.5 %shard_map.74 = (bf16[3,2,128,128]{3,2,1,0:T(8,128)(2,1)S(1)}, bf16[3,2,128,128]{3,2,1,0:T(8,128)(2,1)S(1)}, bf16[3,2,128,128]{3,2,1,0:T(8,128)(2,1)S(1)}, bf16[3,2,128,128]{3,2,1,0:T(8,128)(2,1)S(1)}) custom-call(bf16[16,160,256]{2,1,0:T(8,128)(2,1)S(1)} %all_to_all.5.refs_0_, bf16[16,160,256]{2,1,0:T(8,128)(2,1)S(1)} %collective-permute-done.1.refs_1_.refs_2_), custom_call_target="tpu_custom_call" | custom-call | flops 1 | bytes 1 | tf_op jit(solution)/shard_map/pallas_call | solution.py:217
  40.8 0.1 collective-permute-start.2
  40.9 2.3 %collective-permute-start.3 = (bf16[3,2,128,128]{3,2,1,0:T(8,128)(2,1)S(1)}, bf16[3,2,128,128]{3,2,1,0:T(8,128)(2,1)S(1)}, u32[]{:S(2)}, u32[]{:S(2)}) collective-permute-start(bf16[3,2,128,128]{3,2,1,0:T(8,128)(2,1)S(1)} %get-tuple-element.28), channel_id=1, source_target_pairs={{0,4},{2,6},{4,0},{6,2},{1,5},{3,7},{5,1},{7,3},{8,12},{10,14},{12... | collective-permute-start | bytes 589832 | tf_op jit(solution)/shard_map/ppermute | solution.py:293
  43.2 1.2 %collective-permute-start.4 = (bf16[3,2,128,128]{3,2,1,0:T(8,128)(2,1)S(1)}, bf16[3,2,128,128]{3,2,1,0:T(8,128)(2,1)S(1)}, u32[]{:S(2)}, u32[]{:S(2)}) collective-permute-start(bf16[3,2,128,128]{3,2,1,0:T(8,128)(2,1)S(1)} %get-tuple-element.29), channel_id=1, source_target_pairs={{0,6},{2,0},{4,2},{6,4},{1,7},{3,1},{5,3},{7,5},{8,14},{10,8},{12,... | collective-permute-start | bytes 589832 | tf_op jit(solution)/shard_map/ppermute | solution.py:293
  44.4 1.3 %shard_map.75 = (bf16[4,2,128,128]{3,2,1,0:T(8,128)(2,1)S(1)}, bf16[4,2,128,128]{3,2,1,0:T(8,128)(2,1)S(1)}, bf16[4,2,128,128]{3,2,1,0:T(8,128)(2,1)S(1)}, bf16[4,2,128,128]{3,2,1,0:T(8,128)(2,1)S(1)}) custom-call(bf16[16,160,256]{2,1,0:T(8,128)(2,1)S(1)} %all_to_all.5.refs_0_, bf16[16,160,256]{2,1,0:T(8,128)(2,1)S(1)} %collective-permute-done.1.refs_1_.refs_2_), custom_call_target="tpu_custom_call" | custom-call | flops 1 | bytes 1 | tf_op jit(solution)/shard_map/pallas_call | solution.py:217
  45.6 0.0 copy-start
  45.6 7.3 %collective-permute-done.refs_1_ = bf16[8,160,256]{2,1,0:T(8,128)(2,1)S(1)} collective-permute-done((bf16[8,160,256]{2,1,0:T(8,128)(2,1)S(1)}, bf16[8,160,256]{2,1,0:T(8,128)(2,1)S(1)}, u32[]{:S(2)}, u32[]{:S(2)}) %collective-permute-start) | collective-permute-done | bytes 655392 | tf_op jit(solution)/shard_map/ppermute | solution.py:302
  53.0 0.3 collective-permute-done.2.refs_1_
  53.3 0.0 collective-permute-done.3.refs_2_
  53.3 0.6 collective-permute-done.4.refs_3_
  54.0 2.1 %collective-permute-done.5.refs_3_ = bf16[8,160,256]{2,1,0:T(8,128)(2,1)S(1)} collective-permute-done((bf16[8,160,256]{2,1,0:T(8,128)(2,1)S(1)}, bf16[8,160,256]{2,1,0:T(8,128)(2,1)S(1)}, u32[]{:S(2)}, u32[]{:S(2)}) %collective-permute-start.5) | collective-permute-done | bytes 655392 | tf_op jit(solution)/shard_map/ppermute | solution.py:308
  56.1 1.3 %shard_map.76 = (bf16[4,2,128,128]{3,2,1,0:T(8,128)(2,1)S(1)}, bf16[4,2,128,128]{3,2,1,0:T(8,128)(2,1)S(1)}, bf16[4,2,128,128]{3,2,1,0:T(8,128)(2,1)S(1)}, bf16[4,2,128,128]{3,2,1,0:T(8,128)(2,1)S(1)}) custom-call(bf16[16,160,256]{2,1,0:T(8,128)(2,1)S(1)} %all_to_all.5.refs_0_, ...), custom_call_target="tpu_custom_call", output_to_operand_aliasing={{0}: (4, {}), {1}: (5, {}), {2}: (6, {}), {3}: (7, {})} | custom-call | flops 1 | bytes 1 | tf_op jit(solution)/shard_map/pallas_call | solution.py:217
  57.3 0.3 collective-permute-start.6
  57.7 3.6 %collective-permute-start.7 = (bf16[4,2,128,128]{3,2,1,0:T(8,128)(2,1)S(1)}, bf16[4,2,128,128]{3,2,1,0:T(8,128)(2,1)S(1)}, u32[]{:S(2)}, u32[]{:S(2)}) collective-permute-start(bf16[4,2,128,128]{3,2,1,0:T(8,128)(2,1)S(1)} %get-tuple-element.40), channel_id=1, source_target_pairs={{0,4},{2,6},{4,0},{6,2},{1,5},{3,7},{5,1},{7,3},{8,12},{10,14},{12... | collective-permute-start | bytes 786440 | tf_op jit(solution)/shard_map/ppermute | solution.py:293
  61.9 1.9 %shard_map.77.refs_3_ = f32[5,2,4,128,128]{4,3,2,1,0:T(8,128)} custom-call(s32[1,5]{1,0:T(1,128)S(1)} %copy-done, s32[1]{0:T(128)S(6)} %copy.19.counts, bf16[3,2,128,128]{3,2,1,0:T(8,128)(2,1)S(1)} %get-tuple-element.42.refs_0_, bf16[3,2,128,128]{3,2,1,0:T(8,128)(2,1)S(1)} %collective-permute-done.2.refs_1_, ...), custom_call_target="tpu_custom_call" | custom-call | flops 1 | bytes 1 | tf_op jit(solution)/shard_map/pallas_call | solution.py:272
  63.8 3.4 %collective-permute-done.6.refs_0_ = bf16[4,2,128,128]{3,2,1,0:T(8,128)(2,1)S(1)} collective-permute-done((bf16[4,2,128,128]{3,2,1,0:T(8,128)(2,1)S(1)}, bf16[4,2,128,128]{3,2,1,0:T(8,128)(2,1)S(1)}, u32[]{:S(2)}, u32[]{:S(2)}) %collective-permute-start.6) | collective-permute-done | bytes 262176 | tf_op jit(solution)/shard_map/ppermute | solution.py:293
  67.2 6.0 %collective-permute-done.7.refs_1_ = bf16[4,2,128,128]{3,2,1,0:T(8,128)(2,1)S(1)} collective-permute-done((bf16[4,2,128,128]{3,2,1,0:T(8,128)(2,1)S(1)}, bf16[4,2,128,128]{3,2,1,0:T(8,128)(2,1)S(1)}, u32[]{:S(2)}, u32[]{:S(2)}) %collective-permute-start.7) | collective-permute-done | bytes 262176 | tf_op jit(solution)/shard_map/ppermute | solution.py:293
  73.2 0.1 collective-permute-done.8.refs_2_
  73.2 1.5 %shard_map.78 = f32[5,2,4,128,128]{4,3,2,1,0:T(8,128)} custom-call(s32[1,5]{1,0:T(1,128)S(1)} %copy-done, s32[1]{0:T(128)S(6)} %copy.19.counts, bf16[4,2,128,128]{3,2,1,0:T(8,128)(2,1)S(1)} %collective-permute-done.6.refs_0_, bf16[4,2,128,128]{3,2,1,0:T(8,128)(2,1)S(1)} %collective-permute-done.7.refs_1_, ...), custom_call_target="tpu_custom_call", output_to_operand_aliasing={{}: (5, {})} | custom-call | flops 1 | bytes 1 | tf_op jit(solution)/shard_map/pallas_call | solution.py:272
  (4 shorter events, 0.1 us)
Async XLA Ops:
  34.2 4.2 %collective-permute-start.1 = (bf16[16,160,256]{2,1,0:T(8,128)(2,1)S(1)}, bf16[16,160,256]{2,1,0:T(8,128)(2,1)S(1)}, u32[]{:S(2)}, u32[]{:S(2)}) collective-permute-start(bf16[16,160,256]{2,1,0:T(8,128)(2,1)S(1)} %all_to_all.5.refs_0_), channel_id=1, source_target_pairs={{0,1},{1,0},{2,3},{3,2},{4,5},{5,4},{6,7},{7,6},{8,9},{9,8},{10,11... | collective-permute-start | bytes 3932168 | tf_op jit(solution)/shard_map/ppermute | solution.py:303
  34.2 18.8 %collective-permute-start = (bf16[8,160,256]{2,1,0:T(8,128)(2,1)S(1)}, bf16[8,160,256]{2,1,0:T(8,128)(2,1)S(1)}, u32[]{:S(2)}, u32[]{:S(2)}) collective-permute-start(bf16[8,160,256]{2,1,0:T(8,128)(2,1)S(1)} %slice.4), channel_id=1, source_target_pairs={{0,24},{8,0},{16,8},{24,16},{1,25},{9,1},{17,9},{25,17},{2,26},{10... | collective-permute-start | bytes 1966088 | tf_op jit(solution)/shard_map/ppermute | solution.py:302
  40.8 12.5 %collective-permute-start.2 = (bf16[3,2,128,128]{3,2,1,0:T(8,128)(2,1)S(1)}, bf16[3,2,128,128]{3,2,1,0:T(8,128)(2,1)S(1)}, u32[]{:S(2)}, u32[]{:S(2)}) collective-permute-start(bf16[3,2,128,128]{3,2,1,0:T(8,128)(2,1)S(1)} %get-tuple-element.27), channel_id=1, source_target_pairs={{0,2},{2,4},{4,6},{6,0},{1,3},{3,5},{5,7},{7,1},{8,10},{10,12},{12... | collective-permute-start | bytes 589832 | tf_op jit(solution)/shard_map/ppermute | solution.py:293
  40.9 12.4 %collective-permute-start.3 = (bf16[3,2,128,128]{3,2,1,0:T(8,128)(2,1)S(1)}, bf16[3,2,128,128]{3,2,1,0:T(8,128)(2,1)S(1)}, u32[]{:S(2)}, u32[]{:S(2)}) collective-permute-start(bf16[3,2,128,128]{3,2,1,0:T(8,128)(2,1)S(1)} %get-tuple-element.28), channel_id=1, source_target_pairs={{0,4},{2,6},{4,0},{6,2},{1,5},{3,7},{5,1},{7,3},{8,12},{10,14},{12... | collective-permute-start | bytes 589832 | tf_op jit(solution)/shard_map/ppermute | solution.py:293
  43.2 10.8 %collective-permute-start.4 = (bf16[3,2,128,128]{3,2,1,0:T(8,128)(2,1)S(1)}, bf16[3,2,128,128]{3,2,1,0:T(8,128)(2,1)S(1)}, u32[]{:S(2)}, u32[]{:S(2)}) collective-permute-start(bf16[3,2,128,128]{3,2,1,0:T(8,128)(2,1)S(1)} %get-tuple-element.29), channel_id=1, source_target_pairs={{0,6},{2,0},{4,2},{6,4},{1,7},{3,1},{5,3},{7,5},{8,14},{10,8},{12,... | collective-permute-start | bytes 589832 | tf_op jit(solution)/shard_map/ppermute | solution.py:293
  45.6 16.2 %copy-start = (s32[1,5]{1,0:T(1,128)S(1)}, s32[1,5]{1,0:T(1,128)}, u32[]{:S(2)}) copy-start(s32[1,5]{1,0:T(1,128)} %offsets.3) | copy-start | bytes 64
  54.0 2.1 %collective-permute-start.5 = (bf16[8,160,256]{2,1,0:T(8,128)(2,1)S(1)}, bf16[8,160,256]{2,1,0:T(8,128)(2,1)S(1)}, u32[]{:S(2)}, u32[]{:S(2)}) collective-permute-start(bf16[8,160,256]{2,1,0:T(8,128)(2,1)S(1)} %collective-permute-done.refs_1_), channel_id=1, source_target_pairs={{0,1},{1,0},{2,3},{3,2},{4,5},{5,4},{6,7},{7,6},{8,9},{9,8},{10,11... | collective-permute-start | bytes 1966088 | tf_op jit(solution)/shard_map/ppermute | solution.py:308
  57.3 9.9 %collective-permute-start.6 = (bf16[4,2,128,128]{3,2,1,0:T(8,128)(2,1)S(1)}, bf16[4,2,128,128]{3,2,1,0:T(8,128)(2,1)S(1)}, u32[]{:S(2)}, u32[]{:S(2)}) collective-permute-start(bf16[4,2,128,128]{3,2,1,0:T(8,128)(2,1)S(1)} %get-tuple-element.39), channel_id=1, source_target_pairs={{0,2},{2,4},{4,6},{6,0},{1,3},{3,5},{5,7},{7,1},{8,10},{10,12},{12... | collective-permute-start | bytes 786440 | tf_op jit(solution)/shard_map/ppermute | solution.py:293
  57.7 15.5 %collective-permute-start.7 = (bf16[4,2,128,128]{3,2,1,0:T(8,128)(2,1)S(1)}, bf16[4,2,128,128]{3,2,1,0:T(8,128)(2,1)S(1)}, u32[]{:S(2)}, u32[]{:S(2)}) collective-permute-start(bf16[4,2,128,128]{3,2,1,0:T(8,128)(2,1)S(1)} %get-tuple-element.40), channel_id=1, source_target_pairs={{0,4},{2,6},{4,0},{6,2},{1,5},{3,7},{5,1},{7,3},{8,12},{10,14},{12... | collective-permute-start | bytes 786440 | tf_op jit(solution)/shard_map/ppermute | solution.py:293
  61.2 12.0 %collective-permute-start.8 = (bf16[4,2,128,128]{3,2,1,0:T(8,128)(2,1)S(1)}, bf16[4,2,128,128]{3,2,1,0:T(8,128)(2,1)S(1)}, u32[]{:S(2)}, u32[]{:S(2)}) collective-permute-start(bf16[4,2,128,128]{3,2,1,0:T(8,128)(2,1)S(1)} %get-tuple-element.41), channel_id=1, source_target_pairs={{0,6},{2,0},{4,2},{6,4},{1,7},{3,1},{5,3},{7,5},{8,14},{10,8},{12,... | collective-permute-start | bytes 786440 | tf_op jit(solution)/shard_map/ppermute | solution.py:293

commit v6 on v5

--- a/solution.py
+++ b/solution.py
@@ -138,7 +138,7 @@
     )(live_counts, series, tapers, turns, table)
 
 
-def pair_kernel(wanted, kept, *refs):
+def pair_kernel(wanted, base, kept, split, *refs):
     later, mine_wide, other_wide = refs[-3:]
     outs = refs[-3 - RING : -3]
     inputs = refs[: -3 - RING - kept]
@@ -148,18 +148,14 @@
     is_real = lane % (2 * GROUP) < GROUP
     first = min(wanted)
 
-    def channels(group, at, k):
-        for source in group:
-            if at < source.shape[0] // RING:
-                piece = source[RING * at : RING * (at + 1), k * rows : (k + 1) * rows, :]
-                return piece.reshape(RING * rows, 2 * BW)
-            at -= source.shape[0] // RING
-
     def widened(group, wide, blocks):
+        senders = [(source, at) for source in group for at in range(source.shape[0])]
         for block in blocks:
-            to = (block - first) * BW
-            for k in range(K):
-                wide[to : to + BW, k * 2 * BW : (k + 1) * 2 * BW] = channels(group, block, k)
+            for part, (source, at) in enumerate(senders[RING * block :][:RING]):
+                to = (block - first) * BW + part * rows
+                for k in range(K):
+                    lanes = slice(k * 2 * BW, (k + 1) * 2 * BW)
+                    wide[to : to + rows, lanes] = source[at, k * rows : (k + 1) * rows]
 
     same_of, crossed_of = {}, {}
     for target, offsets in wanted.items():
@@ -167,9 +163,9 @@
         crossed_of[target] = [target + offset // 2 for offset in offsets if offset % 2 == 1]
     same_blocks = set(wanted).union(*same_of.values())
     crossed_blocks = set().union(*crossed_of.values())
-    widened(inputs[: len(inputs) // 2], mine_wide, sorted(same_blocks))
+    widened(inputs[:split], mine_wide, sorted(same_blocks))
     widened(
-        inputs[len(inputs) // 2 :],
+        inputs[split:],
         other_wide,
         sorted(crossed_blocks | {block + 1 for block in crossed_blocks}),
     )
@@ -202,7 +198,8 @@
 
             @pl.when(distance == step)
             def _():
-                for at, offset in enumerate(offsets):
+                for offset in offsets:
+                    at = offset - base
                     group, kind = (even, same) if offset % 2 == 0 else (odd, crossed)
                     column = kind.index(target + offset // 2) * BW
                     piece = group[:, column : column + BW]
@@ -210,12 +207,12 @@
                     outs[step][at, 1] = piece[BW:]
 
 
-def pair_products(wanted, pairs, mine, other, filled=()):
+def pair_products(wanted, base, pairs, mine, other, filled=()):
     reach = sum(block.shape[0] // RING for block in mine) - min(wanted)
     whole = pl.BlockSpec(memory_space=pltpu.VMEM)
     inputs = len(mine) + len(other)
     return pl.pallas_call(
-        functools.partial(pair_kernel, wanted, len(filled)),
+        functools.partial(pair_kernel, wanted, base, len(filled), len(mine)),
         in_specs=[whole] * (inputs + len(filled)),
         out_specs=[whole] * RING,
         out_shape=[jax.ShapeDtypeStruct((pairs, 2, BW, BW), jnp.bfloat16)] * RING,
@@ -230,9 +227,7 @@
     )(*mine, *other, *filled)
 
 
-PLANE = {0: (0, 1, 2), 1: (0, 1, 2), 2: (0, 1, 2), 3: (0,)}
-REST = {0: (3, 4), 1: (3, 4)}
-AHEAD = {2: (3, 4), 3: (1, 2, 3, 4)}
+FIRST, SECOND = (0, 1, 2), (3, 4)
 
 
 def slots_kernel(sources, offsets, counts, *refs):
@@ -242,9 +237,8 @@
     def place(target):
         copies = []
         for (distance, first_set), group in zip(sources, refs):
-            wanted = PLANE if first_set else REST | AHEAD
             band = (target - distance) % RING
-            for at, offset in enumerate(wanted[target]):
+            for at, offset in enumerate(FIRST if first_set else SECOND):
                 slot = 0
                 for step in range(1, SLOTS):
                     slot += jnp.where(offsets[0, step] == offset, step, 0)
@@ -263,10 +257,7 @@
 
 
 def slots_output(offsets, counts, sources, groups, begun=None):
-    pieces = max(
-        sum(len((PLANE if first_set else REST | AHEAD)[target]) for _, first_set in sources)
-        for target in range(RING)
-    )
+    pieces = sum(len(FIRST if first_set else SECOND) for _, first_set in sources)
     whole = pl.BlockSpec(memory_space=pltpu.VMEM)
     earlier = [] if begun is None else [begun]
     return pl.pallas_call(
@@ -299,15 +290,22 @@
     next_plane = [(i, (i - 1) % RING) for i in range(RING)]
     spectra = block_spectra(live_channels, series[0], tapers, turns, table)
     mine = lax.all_to_all(spectra, ("y", "freq"), 0, 0)
-    ahead = lax.ppermute(mine[: 2 * RING], "z", next_plane)
+    near = lax.ppermute(mine[:RING], "z", next_plane)
+    far = lax.ppermute(mine[RING : 2 * RING], "z", next_plane)
+    crossing = [((z + 1) % RING * 2, z * 2 + 1) for z in range(RING)]
+    other_far = lax.ppermute(mine[RING : 2 * RING], ("z", "core"), crossing)
     other = lax.ppermute(mine, "core", swap)
-    plane = sent_along(pair_products(PLANE, 3, [mine], [other]))
-    rest = pair_products(REST, 4, [mine], [other])
-    ahead, *held = lax.optimization_barrier((ahead, *plane, *rest))
-    plane, rest = held[:RING], held[RING:]
-    other_ahead = lax.ppermute(ahead, "core", swap)
-    rest = pair_products(AHEAD, 4, [mine, ahead], [other, other_ahead], rest)
-    rest = sent_along(rest)
+    in_plane = {0: FIRST, 1: FIRST, 2: FIRST, 3: (0,)}
+    plane = pair_products(in_plane, 0, 3, [mine], [other])
+    near, *plane = lax.optimization_barrier((near, *plane))
+    pieces = [near[:1], near[1:2], near[2:]]
+    other_near = [lax.ppermute(piece, "core", swap) for piece in pieces]
+    plane = pair_products({3: (1, 2)}, 0, 3, [mine, near], [other, *other_near], plane)
+    rest = pair_products({0: SECOND, 1: SECOND}, 3, 2, [mine], [other])
+    far, other_far, _, *rest = lax.optimization_barrier((far, other_far, plane[0], *rest))
+    plane = sent_along(plane)
+    mine, other = [mine, near, far], [other, *other_near, other_far]
+    rest = sent_along(pair_products({2: SECOND, 3: SECOND}, 3, 2, mine, other, rest))
     early = [(distance, True) for distance in range(RING)] + [(0, False)]
     late = [(distance, False) for distance in range(1, RING)]
     out = slots_output(pair_offset, pair_count, early, plane + rest[:1])

time: 75.1 us -> 69.4 us (0.924)
  waiting for transfers between devices: 19.8 us -> 12.2 us
  starting transfers between devices: 11.5 us -> 13 us
    ppermute x6, waiting for transfers between devices: 10.4 us -> 4.92 us  [sent_along(): moved.append(lax.ppermute(pieces[distance], 'y', routes))]
    ppermute x2 -> x6, starting transfers between devices: 4.11 us -> 7.08 us  [the longest x1 4.11 us: body(): near = lax.ppermute(mine[:RING], 'z', next_plane)]
    ppermute x2 -> x6, waiting for transfers between devices: 9.44 us -> 7.28 us  [the longest x1 3.31 us: body(): near = lax.ppermute(mine[:RING], 'z', next_plane)]
    ppermute x6, starting transfers between devices: 7.42 us -> 5.93 us  [sent_along(): moved.append(lax.ppermute(pieces[distance], 'y', routes))]
    pallas_call x3 -> x4, Pallas kernels: 5 us -> 5.48 us  [pair_products(): pl.pallas_call(functools.partial(pair_kernel, wanted, base, len(filled),...]
  transfers between devices with their start and end apart: 9 -> 13, of which waited for: 7 -> 8; matrix products, arithmetic and copies ran while one was open for 0% -> 0% of each run, Pallas kernels for 8% -> 11%
where the time goes in v6:
time: 69.4 us; the launch traced here: 69.1 us
  blocking collectives  27.1 us (39%)
  Pallas kernels  15.3 us (22%)
  starting transfers between devices  13 us (19%)
  waiting for transfers between devices  12.2 us (18%)
  between operations  1.43 us (2%)
    all_to_all x1, blocking collectives, body(): mine = lax.all_to_all(spectra, ('y', 'freq'), 0, 0)  27.1 us
    pallas_call x1, Pallas kernels, block_spectra(): pl.pallas_call(spectra_kernel, in_specs=[pl.BlockSpec(memory_space=pl.ANY...  6.42 us
    ppermute x6, starting transfers between devices, sent_along(): moved.append(lax.ppermute(pieces[distance], 'y', routes))  5.93 us
    pallas_call x4, Pallas kernels, pair_products(): pl.pallas_call(functools.partial(pair_kernel, wanted, base, len(filled),...  5.48 us
    ppermute x6, waiting for transfers between devices, sent_along(): moved.append(lax.ppermute(pieces[distance], 'y', routes))  4.92 us
    ppermute x1, starting transfers between devices, body(): near = lax.ppermute(mine[:RING], 'z', next_plane)  4.11 us
    pallas_call x2, Pallas kernels, slots_output(): pl.pallas_call(functools.partial(slots_kernel, sources), in_specs=[pl.Blo...  3.4 us
    ppermute x1, waiting for transfers between devices, body(): near = lax.ppermute(mine[:RING], 'z', next_plane)  3.31 us
  transfers between devices with their start and end apart: 13, of which 8 were waited for; matrix products, arithmetic and copies ran while one was open for 0% of the time, Pallas kernels for 11%

profile of v6, /device:TPU:0, one launch (start us, length us, event | category | flops | bytes accessed | tf_op | source)
XLA Modules:
  0.0 69.1 jit_solution(6912084554877926289)
XLA Ops:
  0.7 6.4 %shard_map.73 = bf16[16,160,256]{2,1,0:T(8,128)(2,1)} custom-call(s32[1]{0:T(128)S(6)} %copy.26.refs_0_, bf16[32,6000]{1,0:T(8,128)(2,1)} %bitcast.2, f32[5,6000]{1,0:T(8,128)} %refs_2_.1, f32[6,1024]{1,0:T(8,128)} %constant.4.clone.refs_3_, bf16[2048,1024]{1,0:T(8,128)(2,1)} %constant.5.clone.refs_4_), custom_call_target="tpu_custom_call" | custom-call | tf_op jit(solution)/shard_map/pallas_call | solution.py:120
  7.1 27.1 %all_to_all.5.refs_0_ = bf16[16,160,256]{2,1,0:T(8,128)(2,1)S(1)} all-to-all(bf16[16,160,256]{2,1,0:T(8,128)(2,1)} %shard_map.73), channel_id=1, replica_groups=mesh['freq'=4,'z'=4,'y'=4,'core'=2] {'y','freq'}, dimensions={0} | all-to-all | bytes 2621440 | tf_op jit(solution)/shard_map/all_to_all | solution.py:292
  34.2 4.1 %collective-permute-start = (bf16[4,160,256]{2,1,0:T(8,128)(2,1)S(1)}, bf16[4,160,256]{2,1,0:T(8,128)(2,1)S(1)}, u32[]{:S(2)}, u32[]{:S(2)}) collective-permute-start(bf16[4,160,256]{2,1,0:T(8,128)(2,1)S(1)} %get-tuple-element.60), channel_id=1, source_target_pairs={{0,24},{8,0},{16,8},{24,16},{1,25},{9,1},{17,9},{25,17},{2,26},{10... | collective-permute-start | bytes 983048 | tf_op jit(solution)/shard_map/ppermute | solution.py:293
  38.3 0.4 collective-permute-start.2
  38.7 1.8 %collective-permute-start.3 = (bf16[4,160,256]{2,1,0:T(8,128)(2,1)S(1)}, bf16[4,160,256]{2,1,0:T(8,128)(2,1)S(1)}, u32[]{:S(2)}, u32[]{:S(2)}) collective-permute-start(bf16[4,160,256]{2,1,0:T(8,128)(2,1)S(1)} %get-tuple-element.59), channel_id=1, source_target_pairs={{8,1},{16,9},{24,17},{0,25},{10,3},{18,11},{26,19},{2,27},{12,5},{... | collective-permute-start | bytes 983048 | tf_op jit(solution)/shard_map/ppermute | solution.py:296
  40.6 2.5 %shard_map.74 = (bf16[3,2,128,128]{3,2,1,0:T(8,128)(2,1)S(1)}, bf16[3,2,128,128]{3,2,1,0:T(8,128)(2,1)S(1)}, bf16[3,2,128,128]{3,2,1,0:T(8,128)(2,1)S(1)}, bf16[3,2,128,128]{3,2,1,0:T(8,128)(2,1)S(1)}) custom-call(bf16[16,160,256]{2,1,0:T(8,128)(2,1)S(1)} %all_to_all.5.refs_0_, bf16[16,160,256]{2,1,0:T(8,128)(2,1)S(1)} %collective-permute-done.1.refs_1_.refs_2_.refs_3_), custom_call_target="tpu_custom_call" | custom-call | flops 1 | bytes 1 | tf_op jit(solution)/shard_map/pallas_call | solution.py:214
  43.0 3.3 %collective-permute-done.refs_1_ = bf16[4,160,256]{2,1,0:T(8,128)(2,1)S(1)} collective-permute-done((bf16[4,160,256]{2,1,0:T(8,128)(2,1)S(1)}, bf16[4,160,256]{2,1,0:T(8,128)(2,1)S(1)}, u32[]{:S(2)}, u32[]{:S(2)}) %collective-permute-start) | collective-permute-done | bytes 327712 | tf_op jit(solution)/shard_map/ppermute | solution.py:293
  46.5 0.6 collective-permute-start.4
  47.1 0.1 collective-permute-start.5
  47.1 0.8 %collective-permute-done.4.refs_3_.refs_4_ = bf16[1,160,256]{2,1,0:T(8,128)(2,1)S(1)} collective-permute-done((bf16[1,160,256]{2,1,0:T(8,128)(2,1)S(1)}, bf16[1,160,256]{2,1,0:T(8,128)(2,1)S(1)}, u32[]{:S(2)}, u32[]{:S(2)}) %collective-permute-start.4) | collective-permute-done | bytes 81952 | tf_op jit(solution)/shard_map/ppermute | solution.py:302
  48.0 0.4 collective-permute-done.5.refs_4_.refs_5_
  48.3 0.6 shard_map.75
  49.0 2.3 %collective-permute-start.11 = (bf16[3,2,128,128]{3,2,1,0:T(8,128)(2,1)S(1)}, bf16[3,2,128,128]{3,2,1,0:T(8,128)(2,1)S(1)}, u32[]{:S(2)}, u32[]{:S(2)}) collective-permute-start(bf16[3,2,128,128]{3,2,1,0:T(8,128)(2,1)S(1)} %get-tuple-element.56), channel_id=1, source_target_pairs={{0,4},{2,6},{4,0},{6,2},{1,5},{3,7},{5,1},{7,3},{8,12},{10,14},{12... | collective-permute-start | bytes 589832 | tf_op jit(solution)/shard_map/ppermute | solution.py:284
  51.3 1.2 %collective-permute-start.12 = (bf16[3,2,128,128]{3,2,1,0:T(8,128)(2,1)S(1)}, bf16[3,2,128,128]{3,2,1,0:T(8,128)(2,1)S(1)}, u32[]{:S(2)}, u32[]{:S(2)}) collective-permute-start(bf16[3,2,128,128]{3,2,1,0:T(8,128)(2,1)S(1)} %get-tuple-element.57), channel_id=1, source_target_pairs={{0,6},{2,0},{4,2},{6,4},{1,7},{3,1},{5,3},{7,5},{8,14},{10,8},{12,... | collective-permute-start | bytes 589832 | tf_op jit(solution)/shard_map/ppermute | solution.py:284
  52.5 1.2 %shard_map.76 = (bf16[2,2,128,128]{3,2,1,0:T(8,128)(2,1)S(1)}, bf16[2,2,128,128]{3,2,1,0:T(8,128)(2,1)S(1)}, bf16[2,2,128,128]{3,2,1,0:T(8,128)(2,1)S(1)}, bf16[2,2,128,128]{3,2,1,0:T(8,128)(2,1)S(1)}) custom-call(bf16[16,160,256]{2,1,0:T(8,128)(2,1)S(1)} %all_to_all.5.refs_0_, bf16[16,160,256]{2,1,0:T(8,128)(2,1)S(1)} %collective-permute-done.1.refs_1_.refs_2_.refs_3_), custom_call_target="tpu_custom_call" | custom-call | flops 1 | bytes 1 | tf_op jit(solution)/shard_map/pallas_call | solution.py:214
  53.7 2.8 %collective-permute-done.3.refs_7_ = bf16[4,160,256]{2,1,0:T(8,128)(2,1)S(1)} collective-permute-done((bf16[4,160,256]{2,1,0:T(8,128)(2,1)S(1)}, bf16[4,160,256]{2,1,0:T(8,128)(2,1)S(1)}, u32[]{:S(2)}, u32[]{:S(2)}) %collective-permute-start.3) | collective-permute-done | bytes 327712 | tf_op jit(solution)/shard_map/ppermute | solution.py:296
  56.5 1.2 %shard_map.77 = (bf16[2,2,128,128]{3,2,1,0:T(8,128)(2,1)S(1)}, bf16[2,2,128,128]{3,2,1,0:T(8,128)(2,1)S(1)}, bf16[2,2,128,128]{3,2,1,0:T(8,128)(2,1)S(1)}, bf16[2,2,128,128]{3,2,1,0:T(8,128)(2,1)S(1)}) custom-call(bf16[16,160,256]{2,1,0:T(8,128)(2,1)S(1)} %all_to_all.5.refs_0_, ...), custom_call_target="tpu_custom_call", output_to_operand_aliasing={{0}: (8, {}), {1}: (9, {}), {2}: (10, {}), {3}: (11, {})} | custom-call | flops 1 | bytes 1 | tf_op jit(solution)/shard_map/pallas_call | solution.py:214
  57.8 2.3 %collective-permute-start.8 = (bf16[2,2,128,128]{3,2,1,0:T(8,128)(2,1)S(1)}, bf16[2,2,128,128]{3,2,1,0:T(8,128)(2,1)S(1)}, u32[]{:S(2)}, u32[]{:S(2)}) collective-permute-start(bf16[2,2,128,128]{3,2,1,0:T(8,128)(2,1)S(1)} %get-tuple-element.53), channel_id=1, source_target_pairs={{0,4},{2,6},{4,0},{6,2},{1,5},{3,7},{5,1},{7,3},{8,12},{10,14},{12... | collective-permute-start | bytes 393224 | tf_op jit(solution)/shard_map/ppermute | solution.py:284
  60.1 1.8 %collective-permute-done.10.refs_1_ = bf16[3,2,128,128]{3,2,1,0:T(8,128)(2,1)S(1)} collective-permute-done((bf16[3,2,128,128]{3,2,1,0:T(8,128)(2,1)S(1)}, bf16[3,2,128,128]{3,2,1,0:T(8,128)(2,1)S(1)}, u32[]{:S(2)}, u32[]{:S(2)}) %collective-permute-start.10) | collective-permute-done | bytes 196640 | tf_op jit(solution)/shard_map/ppermute | solution.py:284
  62.6 0.5 collective-permute-done.12.refs_3_
  63.1 1.9 %shard_map.78.refs_3_ = f32[5,2,4,128,128]{4,3,2,1,0:T(8,128)} custom-call(s32[1,5]{1,0:T(1,128)S(1)} %copy-done, s32[1]{0:T(128)S(6)} %copy.27.counts, bf16[3,2,128,128]{3,2,1,0:T(8,128)(2,1)S(1)} %get-tuple-element.41.refs_0_, bf16[3,2,128,128]{3,2,1,0:T(8,128)(2,1)S(1)} %collective-permute-done.10.refs_1_, ...), custom_call_target="tpu_custom_call" | custom-call | flops 1 | bytes 1 | tf_op jit(solution)/shard_map/pallas_call | solution.py:263
  65.0 2.0 %collective-permute-done.7.refs_0_ = bf16[2,2,128,128]{3,2,1,0:T(8,128)(2,1)S(1)} collective-permute-done((bf16[2,2,128,128]{3,2,1,0:T(8,128)(2,1)S(1)}, bf16[2,2,128,128]{3,2,1,0:T(8,128)(2,1)S(1)}, u32[]{:S(2)}, u32[]{:S(2)}) %collective-permute-start.7) | collective-permute-done | bytes 131104 | tf_op jit(solution)/shard_map/ppermute | solution.py:284
  67.0 0.6 collective-permute-done.9.refs_2_
  67.6 1.5 %shard_map.79 = f32[5,2,4,128,128]{4,3,2,1,0:T(8,128)} custom-call(s32[1,5]{1,0:T(1,128)S(1)} %copy-done, s32[1]{0:T(128)S(6)} %copy.27.counts, bf16[2,2,128,128]{3,2,1,0:T(8,128)(2,1)S(1)} %collective-permute-done.7.refs_0_, bf16[2,2,128,128]{3,2,1,0:T(8,128)(2,1)S(1)} %collective-permute-done.8.refs_1_, ...), custom_call_target="tpu_custom_call", output_to_operand_aliasing={{}: (5, {})} | custom-call | flops 1 | bytes 1 | tf_op jit(solution)/shard_map/pallas_call | solution.py:263
  (15 shorter events, 0.3 us)
Async XLA Ops:
  34.2 6.4 %collective-permute-start.1 = (bf16[16,160,256]{2,1,0:T(8,128)(2,1)S(1)}, bf16[16,160,256]{2,1,0:T(8,128)(2,1)S(1)}, u32[]{:S(2)}, u32[]{:S(2)}) collective-permute-start(bf16[16,160,256]{2,1,0:T(8,128)(2,1)S(1)} %all_to_all.5.refs_0_), channel_id=1, source_target_pairs={{0,1},{1,0},{2,3},{3,2},{4,5},{5,4},{6,7},{7,6},{8,9},{9,8},{10,11... | collective-permute-start | bytes 3932168 | tf_op jit(solution)/shard_map/ppermute | solution.py:297
  34.2 12.1 %collective-permute-start = (bf16[4,160,256]{2,1,0:T(8,128)(2,1)S(1)}, bf16[4,160,256]{2,1,0:T(8,128)(2,1)S(1)}, u32[]{:S(2)}, u32[]{:S(2)}) collective-permute-start(bf16[4,160,256]{2,1,0:T(8,128)(2,1)S(1)} %get-tuple-element.60), channel_id=1, source_target_pairs={{0,24},{8,0},{16,8},{24,16},{1,25},{9,1},{17,9},{25,17},{2,26},{10... | collective-permute-start | bytes 983048 | tf_op jit(solution)/shard_map/ppermute | solution.py:293
  38.3 15.4 %collective-permute-start.2 = (bf16[4,160,256]{2,1,0:T(8,128)(2,1)S(1)}, bf16[4,160,256]{2,1,0:T(8,128)(2,1)S(1)}, u32[]{:S(2)}, u32[]{:S(2)}) collective-permute-start(bf16[4,160,256]{2,1,0:T(8,128)(2,1)S(1)} %get-tuple-element.59), channel_id=1, source_target_pairs={{0,24},{8,0},{16,8},{24,16},{1,25},{9,1},{17,9},{25,17},{2,26},{10... | collective-permute-start | bytes 983048 | tf_op jit(solution)/shard_map/ppermute | solution.py:294
  38.7 17.8 %collective-permute-start.3 = (bf16[4,160,256]{2,1,0:T(8,128)(2,1)S(1)}, bf16[4,160,256]{2,1,0:T(8,128)(2,1)S(1)}, u32[]{:S(2)}, u32[]{:S(2)}) collective-permute-start(bf16[4,160,256]{2,1,0:T(8,128)(2,1)S(1)} %get-tuple-element.59), channel_id=1, source_target_pairs={{8,1},{16,9},{24,17},{0,25},{10,3},{18,11},{26,19},{2,27},{12,5},{... | collective-permute-start | bytes 983048 | tf_op jit(solution)/shard_map/ppermute | solution.py:296
  46.4 2.0 %collective-permute-start.6 = (bf16[2,160,256]{2,1,0:T(8,128)(2,1)S(1)}, bf16[2,160,256]{2,1,0:T(8,128)(2,1)S(1)}, u32[]{:S(2)}, u32[]{:S(2)}) collective-permute-start(bf16[2,160,256]{2,1,0:T(8,128)(2,1)S(1)} %slice.20), channel_id=1, source_target_pairs={{0,1},{1,0},{2,3},{3,2},{4,5},{5,4},{6,7},{7,6},{8,9},{9,8},{10,11... | collective-permute-start | bytes 491528 | tf_op jit(solution)/shard_map/ppermute | solution.py:302
  46.5 1.5 %collective-permute-start.4 = (bf16[1,160,256]{2,1,0:T(8,128)(2,1)S(1)}, bf16[1,160,256]{2,1,0:T(8,128)(2,1)S(1)}, u32[]{:S(2)}, u32[]{:S(2)}) collective-permute-start(bf16[1,160,256]{2,1,0:T(8,128)(2,1)S(1)} %get-tuple-element.62), channel_id=1, source_target_pairs={{0,1},{1,0},{2,3},{3,2},{4,5},{5,4},{6,7},{7,6},{8,9},{9,8},{10,11... | collective-permute-start | bytes 245768 | tf_op jit(solution)/shard_map/ppermute | solution.py:302
  47.1 1.3 %collective-permute-start.5 = (bf16[1,160,256]{2,1,0:T(8,128)(2,1)S(1)}, bf16[1,160,256]{2,1,0:T(8,128)(2,1)S(1)}, u32[]{:S(2)}, u32[]{:S(2)}) collective-permute-start(bf16[1,160,256]{2,1,0:T(8,128)(2,1)S(1)} %get-tuple-element.61), channel_id=1, source_target_pairs={{0,1},{1,0},{2,3},{3,2},{4,5},{5,4},{6,7},{7,6},{8,9},{9,8},{10,11... | collective-permute-start | bytes 245768 | tf_op jit(solution)/shard_map/ppermute | solution.py:302
  48.9 13.0 %collective-permute-start.10 = (bf16[3,2,128,128]{3,2,1,0:T(8,128)(2,1)S(1)}, bf16[3,2,128,128]{3,2,1,0:T(8,128)(2,1)S(1)}, u32[]{:S(2)}, u32[]{:S(2)}) collective-permute-start(bf16[3,2,128,128]{3,2,1,0:T(8,128)(2,1)S(1)} %get-tuple-element.55), channel_id=1, source_target_pairs={{0,2},{2,4},{4,6},{6,0},{1,3},{3,5},{5,7},{7,1},{8,10},{10,12},{12... | collective-permute-start | bytes 589832 | tf_op jit(solution)/shard_map/ppermute | solution.py:284
  49.0 13.5 %collective-permute-start.11 = (bf16[3,2,128,128]{3,2,1,0:T(8,128)(2,1)S(1)}, bf16[3,2,128,128]{3,2,1,0:T(8,128)(2,1)S(1)}, u32[]{:S(2)}, u32[]{:S(2)}) collective-permute-start(bf16[3,2,128,128]{3,2,1,0:T(8,128)(2,1)S(1)} %get-tuple-element.56), channel_id=1, source_target_pairs={{0,4},{2,6},{4,0},{6,2},{1,5},{3,7},{5,1},{7,3},{8,12},{10,14},{12... | collective-permute-start | bytes 589832 | tf_op jit(solution)/shard_map/ppermute | solution.py:284
  51.3 11.7 %collective-permute-start.12 = (bf16[3,2,128,128]{3,2,1,0:T(8,128)(2,1)S(1)}, bf16[3,2,128,128]{3,2,1,0:T(8,128)(2,1)S(1)}, u32[]{:S(2)}, u32[]{:S(2)}) collective-permute-start(bf16[3,2,128,128]{3,2,1,0:T(8,128)(2,1)S(1)} %get-tuple-element.57), channel_id=1, source_target_pairs={{0,6},{2,0},{4,2},{6,4},{1,7},{3,1},{5,3},{7,5},{8,14},{10,8},{12,... | collective-permute-start | bytes 589832 | tf_op jit(solution)/shard_map/ppermute | solution.py:284
  56.5 6.6 %copy-start = (s32[1,5]{1,0:T(1,128)S(1)}, s32[1,5]{1,0:T(1,128)}, u32[]{:S(2)}) copy-start(s32[1,5]{1,0:T(1,128)} %offsets.3) | copy-start | bytes 64
  57.7 9.3 %collective-permute-start.7 = (bf16[2,2,128,128]{3,2,1,0:T(8,128)(2,1)S(1)}, bf16[2,2,128,128]{3,2,1,0:T(8,128)(2,1)S(1)}, u32[]{:S(2)}, u32[]{:S(2)}) collective-permute-start(bf16[2,2,128,128]{3,2,1,0:T(8,128)(2,1)S(1)} %get-tuple-element.52), channel_id=1, source_target_pairs={{0,2},{2,4},{4,6},{6,0},{1,3},{3,5},{5,7},{7,1},{8,10},{10,12},{12... | collective-permute-start | bytes 393224 | tf_op jit(solution)/shard_map/ppermute | solution.py:284
  57.8 9.2 %collective-permute-start.8 = (bf16[2,2,128,128]{3,2,1,0:T(8,128)(2,1)S(1)}, bf16[2,2,128,128]{3,2,1,0:T(8,128)(2,1)S(1)}, u32[]{:S(2)}, u32[]{:S(2)}) collective-permute-start(bf16[2,2,128,128]{3,2,1,0:T(8,128)(2,1)S(1)} %get-tuple-element.53), channel_id=1, source_target_pairs={{0,4},{2,6},{4,0},{6,2},{1,5},{3,7},{5,1},{7,3},{8,12},{10,14},{12... | collective-permute-start | bytes 393224 | tf_op jit(solution)/shard_map/ppermute | solution.py:284
  61.9 5.7 %collective-permute-start.9 = (bf16[2,2,128,128]{3,2,1,0:T(8,128)(2,1)S(1)}, bf16[2,2,128,128]{3,2,1,0:T(8,128)(2,1)S(1)}, u32[]{:S(2)}, u32[]{:S(2)}) collective-permute-start(bf16[2,2,128,128]{3,2,1,0:T(8,128)(2,1)S(1)} %get-tuple-element.54), channel_id=1, source_target_pairs={{0,6},{2,0},{4,2},{6,4},{1,7},{3,1},{5,3},{7,5},{8,14},{10,8},{12,... | collective-permute-start | bytes 393224 | tf_op jit(solution)/shard_map/ppermute | solution.py:284

commit v7 on v6

--- a/solution.py
+++ b/solution.py
@@ -138,6 +138,10 @@
     )(live_counts, series, tapers, turns, table)
 
 
+def plane_of(offset, base):
+    return 2 * (offset - base) - (1 if base == 0 and offset > 0 else 0)
+
+
 def pair_kernel(wanted, base, kept, split, *refs):
     later, mine_wide, other_wide = refs[-3:]
     outs = refs[-3 - RING : -3]
@@ -146,6 +150,8 @@
     rows = inputs[0].shape[1] // K
     lane = lax.broadcasted_iota(jnp.int32, (BW, BW), 1)
     is_real = lane % (2 * GROUP) < GROUP
+    row = lax.broadcasted_iota(jnp.int32, (BW, BW), 0)
+    below, diagonal = row > lane, row == lane
     first = min(wanted)
 
     def widened(group, wide, blocks):
@@ -199,15 +205,20 @@
             @pl.when(distance == step)
             def _():
                 for offset in offsets:
-                    at = offset - base
                     group, kind = (even, same) if offset % 2 == 0 else (odd, crossed)
                     column = kind.index(target + offset // 2) * BW
                     piece = group[:, column : column + BW]
-                    outs[step][at, 0] = piece[:BW]
-                    outs[step][at, 1] = piece[BW:]
-
-
-def pair_products(wanted, base, pairs, mine, other, filled=()):
+                    at = plane_of(offset, base)
+                    if offset == 0:
+                        both = piece.astype(jnp.float32)
+                        both = jnp.where(below | diagonal, both[:BW], both[BW:])
+                        outs[step][at] = both.astype(jnp.bfloat16)
+                    else:
+                        outs[step][at] = piece[:BW]
+                        outs[step][at + 1] = piece[BW:]
+
+
+def pair_products(wanted, base, planes, mine, other, filled=()):
     reach = sum(block.shape[0] // RING for block in mine) - min(wanted)
     whole = pl.BlockSpec(memory_space=pltpu.VMEM)
     inputs = len(mine) + len(other)
@@ -215,7 +226,7 @@
         functools.partial(pair_kernel, wanted, base, len(filled), len(mine)),
         in_specs=[whole] * (inputs + len(filled)),
         out_specs=[whole] * RING,
-        out_shape=[jax.ShapeDtypeStruct((pairs, 2, BW, BW), jnp.bfloat16)] * RING,
+        out_shape=[jax.ShapeDtypeStruct((planes, BW, BW), jnp.bfloat16)] * RING,
         scratch_shapes=[
             pltpu.VMEM((2 * BW, K * 2 * BW), jnp.bfloat16),
             pltpu.VMEM((reach * BW, K * 2 * BW), jnp.bfloat16),
@@ -233,18 +244,29 @@
 def slots_kernel(sources, offsets, counts, *refs):
     out, wide, done = refs[-3:]
     y, count = lax.axis_index("y"), counts[0]
+    row = lax.broadcasted_iota(jnp.int32, (BW, BW), 0)
+    column = lax.broadcasted_iota(jnp.int32, (BW, BW), 1)
+    below, diagonal = row > column, row == column
 
     def place(target):
         copies = []
         for (distance, first_set), group in zip(sources, refs):
             band = (target - distance) % RING
-            for at, offset in enumerate(FIRST if first_set else SECOND):
+            for offset in FIRST if first_set else SECOND:
                 slot = 0
                 for step in range(1, SLOTS):
                     slot += jnp.where(offsets[0, step] == offset, step, 0)
                 live = (slot < count).astype(jnp.float32)
                 piece = len(copies)
-                wide[piece] = group[at].astype(jnp.float32) * live
+                at = plane_of(offset, FIRST[0] if first_set else SECOND[0])
+                if offset == 0:
+                    both = group[at].astype(jnp.float32)
+                    across = both.T
+                    wide[piece, 0] = jnp.where(below | diagonal, both, across) * live
+                    imag = jnp.where(below, -across, jnp.where(diagonal, 0.0, both))
+                    wide[piece, 1] = imag * live
+                else:
+                    wide[piece] = group[at : at + 2].astype(jnp.float32) * live
                 copies.append(
                     pltpu.make_async_copy(wide.at[piece], out.at[slot, :, band], done.at[piece])
                 )
@@ -296,16 +318,17 @@
     other_far = lax.ppermute(mine[RING : 2 * RING], ("z", "core"), crossing)
     other = lax.ppermute(mine, "core", swap)
     in_plane = {0: FIRST, 1: FIRST, 2: FIRST, 3: (0,)}
-    plane = pair_products(in_plane, 0, 3, [mine], [other])
+    plane = pair_products(in_plane, 0, 5, [mine], [other])
     near, *plane = lax.optimization_barrier((near, *plane))
     pieces = [near[:1], near[1:2], near[2:]]
     other_near = [lax.ppermute(piece, "core", swap) for piece in pieces]
-    plane = pair_products({3: (1, 2)}, 0, 3, [mine, near], [other, *other_near], plane)
-    rest = pair_products({0: SECOND, 1: SECOND}, 3, 2, [mine], [other])
+    plane = pair_products({3: (1, 2)}, 0, 5, [mine, near], [other, *other_near], plane)
+    close = {0: SECOND, 1: SECOND, 2: SECOND}
+    rest = pair_products(close, 3, 4, [mine, near], [other, *other_near])
     far, other_far, _, *rest = lax.optimization_barrier((far, other_far, plane[0], *rest))
     plane = sent_along(plane)
     mine, other = [mine, near, far], [other, *other_near, other_far]
-    rest = sent_along(pair_products({2: SECOND, 3: SECOND}, 3, 2, mine, other, rest))
+    rest = sent_along(pair_products({3: SECOND}, 3, 4, mine, other, rest))
     early = [(distance, True) for distance in range(RING)] + [(0, False)]
     late = [(distance, False) for distance in range(1, RING)]
     out = slots_output(pair_offset, pair_count, early, plane + rest[:1])

time: 69.4 us -> 68 us (0.980)
  waiting for transfers between devices: 12.2 us -> 10.2 us
    ppermute x6, waiting for transfers between devices: 4.92 us -> 3.58 us  [sent_along(): moved.append(lax.ppermute(pieces[distance], 'y', routes))]
  transfers between devices with their start and end apart: 13 -> 13, of which waited for: 8 -> 7; matrix products, arithmetic and copies ran while one was open for 0% -> 0% of each run, Pallas kernels for 11% -> 11%
where the time goes in v7:
time: 68 us; the launch traced here: 67.8 us
  blocking collectives  27.1 us (40%)
  Pallas kernels  15.4 us (23%)
  starting transfers between devices  13.5 us (20%)
  waiting for transfers between devices  10.2 us (15%)
  between operations  1.45 us (2%)
    all_to_all x1, blocking collectives, body(): mine = lax.all_to_all(spectra, ('y', 'freq'), 0, 0)  27.1 us
    pallas_call x1, Pallas kernels, block_spectra(): pl.pallas_call(spectra_kernel, in_specs=[pl.BlockSpec(memory_space=pl.ANY...  6.42 us
    ppermute x6, starting transfers between devices, sent_along(): moved.append(lax.ppermute(pieces[distance], 'y', routes))  6.42 us
    pallas_call x4, Pallas kernels, pair_products(): pl.pallas_call(functools.partial(pair_kernel, wanted, base, len(filled),...  5.47 us
    ppermute x1, starting transfers between devices, body(): near = lax.ppermute(mine[:RING], 'z', next_plane)  4.11 us
    ppermute x6, waiting for transfers between devices, sent_along(): moved.append(lax.ppermute(pieces[distance], 'y', routes))  3.58 us
    pallas_call x2, Pallas kernels, slots_output(): pl.pallas_call(functools.partial(slots_kernel, sources), in_specs=[pl.Blo...  3.51 us
    ppermute x1, waiting for transfers between devices, body(): near = lax.ppermute(mine[:RING], 'z', next_plane)  3.29 us
  transfers between devices with their start and end apart: 13, of which 7 were waited for; matrix products, arithmetic and copies ran while one was open for 0% of the time, Pallas kernels for 11%

profile of v7, /device:TPU:0, one launch (start us, length us, event | category | flops | bytes accessed | tf_op | source)
XLA Modules:
  0.0 67.8 jit_solution(18367083804392870038)
XLA Ops:
  0.7 6.4 %shard_map.73 = bf16[16,160,256]{2,1,0:T(8,128)(2,1)} custom-call(s32[1]{0:T(128)S(6)} %copy.26.refs_0_, bf16[32,6000]{1,0:T(8,128)(2,1)} %bitcast.2, f32[5,6000]{1,0:T(8,128)} %refs_2_.1, f32[6,1024]{1,0:T(8,128)} %constant.4.clone.refs_3_, bf16[2048,1024]{1,0:T(8,128)(2,1)} %constant.5.clone.refs_4_), custom_call_target="tpu_custom_call" | custom-call | tf_op jit(solution)/shard_map/pallas_call | solution.py:120
  7.1 27.1 %all_to_all.5.refs_0_ = bf16[16,160,256]{2,1,0:T(8,128)(2,1)S(1)} all-to-all(bf16[16,160,256]{2,1,0:T(8,128)(2,1)} %shard_map.73), channel_id=1, replica_groups=mesh['freq'=4,'z'=4,'y'=4,'core'=2] {'y','freq'}, dimensions={0} | all-to-all | bytes 2621440 | tf_op jit(solution)/shard_map/all_to_all | solution.py:314
  34.2 4.1 %collective-permute-start = (bf16[4,160,256]{2,1,0:T(8,128)(2,1)S(1)}, bf16[4,160,256]{2,1,0:T(8,128)(2,1)S(1)}, u32[]{:S(2)}, u32[]{:S(2)}) collective-permute-start(bf16[4,160,256]{2,1,0:T(8,128)(2,1)S(1)} %get-tuple-element.60), channel_id=1, source_target_pairs={{0,24},{8,0},{16,8},{24,16},{1,25},{9,1},{17,9},{25,17},{2,26},{10... | collective-permute-start | bytes 983048 | tf_op jit(solution)/shard_map/ppermute | solution.py:315
  38.3 0.4 collective-permute-start.2
  38.7 1.8 %collective-permute-start.3 = (bf16[4,160,256]{2,1,0:T(8,128)(2,1)S(1)}, bf16[4,160,256]{2,1,0:T(8,128)(2,1)S(1)}, u32[]{:S(2)}, u32[]{:S(2)}) collective-permute-start(bf16[4,160,256]{2,1,0:T(8,128)(2,1)S(1)} %get-tuple-element.59), channel_id=1, source_target_pairs={{8,1},{16,9},{24,17},{0,25},{10,3},{18,11},{26,19},{2,27},{12,5},{... | collective-permute-start | bytes 983048 | tf_op jit(solution)/shard_map/ppermute | solution.py:318
  40.6 2.5 %shard_map.74 = (bf16[5,128,128]{2,1,0:T(8,128)(2,1)S(1)}, bf16[5,128,128]{2,1,0:T(8,128)(2,1)S(1)}, bf16[5,128,128]{2,1,0:T(8,128)(2,1)S(1)}, bf16[5,128,128]{2,1,0:T(8,128)(2,1)S(1)}) custom-call(bf16[16,160,256]{2,1,0:T(8,128)(2,1)S(1)} %all_to_all.5.refs_0_, bf16[16,160,256]{2,1,0:T(8,128)(2,1)S(1)} %collective-permute-done.1.refs_1_.refs_2_.refs_3_), custom_call_target="tpu_custom_call" | custom-call | flops 1 | bytes 1 | tf_op jit(solution)/shard_map/pallas_call | solution.py:225
  43.1 3.3 %collective-permute-done.refs_1_ = bf16[4,160,256]{2,1,0:T(8,128)(2,1)S(1)} collective-permute-done((bf16[4,160,256]{2,1,0:T(8,128)(2,1)S(1)}, bf16[4,160,256]{2,1,0:T(8,128)(2,1)S(1)}, u32[]{:S(2)}, u32[]{:S(2)}) %collective-permute-start) | collective-permute-done | bytes 327712 | tf_op jit(solution)/shard_map/ppermute | solution.py:315
  46.5 0.6 collective-permute-start.4
  47.1 0.1 collective-permute-start.5
  47.1 0.8 %collective-permute-done.4.refs_3_.refs_4_ = bf16[1,160,256]{2,1,0:T(8,128)(2,1)S(1)} collective-permute-done((bf16[1,160,256]{2,1,0:T(8,128)(2,1)S(1)}, bf16[1,160,256]{2,1,0:T(8,128)(2,1)S(1)}, u32[]{:S(2)}, u32[]{:S(2)}) %collective-permute-start.4) | collective-permute-done | bytes 81952 | tf_op jit(solution)/shard_map/ppermute | solution.py:324
  48.0 0.4 collective-permute-done.5.refs_4_.refs_5_
  48.3 0.6 shard_map.75
  49.0 2.3 %collective-permute-start.11 = (bf16[5,128,128]{2,1,0:T(8,128)(2,1)S(1)}, bf16[5,128,128]{2,1,0:T(8,128)(2,1)S(1)}, u32[]{:S(2)}, u32[]{:S(2)}) collective-permute-start(bf16[5,128,128]{2,1,0:T(8,128)(2,1)S(1)} %get-tuple-element.56), channel_id=1, source_target_pairs={{0,4},{2,6},{4,0},{6,2},{1,5},{3,7},{5,1},{7,3},{8,12},{10,14},{12... | collective-permute-start | bytes 491528 | tf_op jit(solution)/shard_map/ppermute | solution.py:306
  51.3 1.2 %collective-permute-start.12 = (bf16[5,128,128]{2,1,0:T(8,128)(2,1)S(1)}, bf16[5,128,128]{2,1,0:T(8,128)(2,1)S(1)}, u32[]{:S(2)}, u32[]{:S(2)}) collective-permute-start(bf16[5,128,128]{2,1,0:T(8,128)(2,1)S(1)} %get-tuple-element.57), channel_id=1, source_target_pairs={{0,6},{2,0},{4,2},{6,4},{1,7},{3,1},{5,3},{7,5},{8,14},{10,8},{12,... | collective-permute-start | bytes 491528 | tf_op jit(solution)/shard_map/ppermute | solution.py:306
  52.5 1.8 %shard_map.76 = (bf16[4,128,128]{2,1,0:T(8,128)(2,1)S(1)}, bf16[4,128,128]{2,1,0:T(8,128)(2,1)S(1)}, bf16[4,128,128]{2,1,0:T(8,128)(2,1)S(1)}, bf16[4,128,128]{2,1,0:T(8,128)(2,1)S(1)}) custom-call(bf16[16,160,256]{2,1,0:T(8,128)(2,1)S(1)} %all_to_all.5.refs_0_, bf16[4,160,256]{2,1,0:T(8,128)(2,1)S(1)} %collective-permute-done.refs_1_, ...), custom_call_target="tpu_custom_call" | custom-call | flops 1 | bytes 1 | tf_op jit(solution)/shard_map/pallas_call | solution.py:225
  54.3 2.2 %collective-permute-done.3.refs_7_ = bf16[4,160,256]{2,1,0:T(8,128)(2,1)S(1)} collective-permute-done((bf16[4,160,256]{2,1,0:T(8,128)(2,1)S(1)}, bf16[4,160,256]{2,1,0:T(8,128)(2,1)S(1)}, u32[]{:S(2)}, u32[]{:S(2)}) %collective-permute-start.3) | collective-permute-done | bytes 327712 | tf_op jit(solution)/shard_map/ppermute | solution.py:318
  56.5 0.6 shard_map.77
  57.2 2.3 %collective-permute-start.8 = (bf16[4,128,128]{2,1,0:T(8,128)(2,1)S(1)}, bf16[4,128,128]{2,1,0:T(8,128)(2,1)S(1)}, u32[]{:S(2)}, u32[]{:S(2)}) collective-permute-start(bf16[4,128,128]{2,1,0:T(8,128)(2,1)S(1)} %get-tuple-element.53), channel_id=1, source_target_pairs={{0,4},{2,6},{4,0},{6,2},{1,5},{3,7},{5,1},{7,3},{8,12},{10,14},{12... | collective-permute-start | bytes 393224 | tf_op jit(solution)/shard_map/ppermute | solution.py:306
  59.5 0.7 %collective-permute-done.10.refs_1_ = bf16[5,128,128]{2,1,0:T(8,128)(2,1)S(1)} collective-permute-done((bf16[5,128,128]{2,1,0:T(8,128)(2,1)S(1)}, bf16[5,128,128]{2,1,0:T(8,128)(2,1)S(1)}, u32[]{:S(2)}, u32[]{:S(2)}) %collective-permute-start.10) | collective-permute-done | bytes 163872 | tf_op jit(solution)/shard_map/ppermute | solution.py:306
  60.2 0.5 collective-permute-start.9
  61.3 2.0 %shard_map.78.refs_3_ = f32[5,2,4,128,128]{4,3,2,1,0:T(8,128)} custom-call(s32[1,5]{1,0:T(1,128)S(1)} %copy-done, s32[1]{0:T(128)S(6)} %copy.27.counts, bf16[5,128,128]{2,1,0:T(8,128)(2,1)S(1)} %get-tuple-element.41.refs_0_, bf16[5,128,128]{2,1,0:T(8,128)(2,1)S(1)} %collective-permute-done.10.refs_1_, ...), custom_call_target="tpu_custom_call" | custom-call | flops 1 | bytes 1 | tf_op jit(solution)/shard_map/pallas_call | solution.py:285
  63.4 2.2 %collective-permute-done.7.refs_0_ = bf16[4,128,128]{2,1,0:T(8,128)(2,1)S(1)} collective-permute-done((bf16[4,128,128]{2,1,0:T(8,128)(2,1)S(1)}, bf16[4,128,128]{2,1,0:T(8,128)(2,1)S(1)}, u32[]{:S(2)}, u32[]{:S(2)}) %collective-permute-start.7) | collective-permute-done | bytes 131104 | tf_op jit(solution)/shard_map/ppermute | solution.py:306
  65.6 0.7 collective-permute-done.9.refs_2_
  66.3 1.5 %shard_map.79 = f32[5,2,4,128,128]{4,3,2,1,0:T(8,128)} custom-call(s32[1,5]{1,0:T(1,128)S(1)} %copy-done, s32[1]{0:T(128)S(6)} %copy.27.counts, bf16[4,128,128]{2,1,0:T(8,128)(2,1)S(1)} %collective-permute-done.7.refs_0_, bf16[4,128,128]{2,1,0:T(8,128)(2,1)S(1)} %collective-permute-done.8.refs_1_, ...), custom_call_target="tpu_custom_call", output_to_operand_aliasing={{}: (5, {})} | custom-call | flops 1 | bytes 1 | tf_op jit(solution)/shard_map/pallas_call | solution.py:285
  (15 shorter events, 0.3 us)
Async XLA Ops:
  34.2 6.4 %collective-permute-start.1 = (bf16[16,160,256]{2,1,0:T(8,128)(2,1)S(1)}, bf16[16,160,256]{2,1,0:T(8,128)(2,1)S(1)}, u32[]{:S(2)}, u32[]{:S(2)}) collective-permute-start(bf16[16,160,256]{2,1,0:T(8,128)(2,1)S(1)} %all_to_all.5.refs_0_), channel_id=1, source_target_pairs={{0,1},{1,0},{2,3},{3,2},{4,5},{5,4},{6,7},{7,6},{8,9},{9,8},{10,11... | collective-permute-start | bytes 3932168 | tf_op jit(solution)/shard_map/ppermute | solution.py:319
  34.2 12.1 %collective-permute-start = (bf16[4,160,256]{2,1,0:T(8,128)(2,1)S(1)}, bf16[4,160,256]{2,1,0:T(8,128)(2,1)S(1)}, u32[]{:S(2)}, u32[]{:S(2)}) collective-permute-start(bf16[4,160,256]{2,1,0:T(8,128)(2,1)S(1)} %get-tuple-element.60), channel_id=1, source_target_pairs={{0,24},{8,0},{16,8},{24,16},{1,25},{9,1},{17,9},{25,17},{2,26},{10... | collective-permute-start | bytes 983048 | tf_op jit(solution)/shard_map/ppermute | solution.py:315
  38.3 16.0 %collective-permute-start.2 = (bf16[4,160,256]{2,1,0:T(8,128)(2,1)S(1)}, bf16[4,160,256]{2,1,0:T(8,128)(2,1)S(1)}, u32[]{:S(2)}, u32[]{:S(2)}) collective-permute-start(bf16[4,160,256]{2,1,0:T(8,128)(2,1)S(1)} %get-tuple-element.59), channel_id=1, source_target_pairs={{0,24},{8,0},{16,8},{24,16},{1,25},{9,1},{17,9},{25,17},{2,26},{10... | collective-permute-start | bytes 983048 | tf_op jit(solution)/shard_map/ppermute | solution.py:316
  38.7 17.8 %collective-permute-start.3 = (bf16[4,160,256]{2,1,0:T(8,128)(2,1)S(1)}, bf16[4,160,256]{2,1,0:T(8,128)(2,1)S(1)}, u32[]{:S(2)}, u32[]{:S(2)}) collective-permute-start(bf16[4,160,256]{2,1,0:T(8,128)(2,1)S(1)} %get-tuple-element.59), channel_id=1, source_target_pairs={{8,1},{16,9},{24,17},{0,25},{10,3},{18,11},{26,19},{2,27},{12,5},{... | collective-permute-start | bytes 983048 | tf_op jit(solution)/shard_map/ppermute | solution.py:318
  46.4 2.0 %collective-permute-start.6 = (bf16[2,160,256]{2,1,0:T(8,128)(2,1)S(1)}, bf16[2,160,256]{2,1,0:T(8,128)(2,1)S(1)}, u32[]{:S(2)}, u32[]{:S(2)}) collective-permute-start(bf16[2,160,256]{2,1,0:T(8,128)(2,1)S(1)} %slice.20), channel_id=1, source_target_pairs={{0,1},{1,0},{2,3},{3,2},{4,5},{5,4},{6,7},{7,6},{8,9},{9,8},{10,11... | collective-permute-start | bytes 491528 | tf_op jit(solution)/shard_map/ppermute | solution.py:324
  46.5 1.5 %collective-permute-start.4 = (bf16[1,160,256]{2,1,0:T(8,128)(2,1)S(1)}, bf16[1,160,256]{2,1,0:T(8,128)(2,1)S(1)}, u32[]{:S(2)}, u32[]{:S(2)}) collective-permute-start(bf16[1,160,256]{2,1,0:T(8,128)(2,1)S(1)} %get-tuple-element.62), channel_id=1, source_target_pairs={{0,1},{1,0},{2,3},{3,2},{4,5},{5,4},{6,7},{7,6},{8,9},{9,8},{10,11... | collective-permute-start | bytes 245768 | tf_op jit(solution)/shard_map/ppermute | solution.py:324
  47.1 1.3 %collective-permute-start.5 = (bf16[1,160,256]{2,1,0:T(8,128)(2,1)S(1)}, bf16[1,160,256]{2,1,0:T(8,128)(2,1)S(1)}, u32[]{:S(2)}, u32[]{:S(2)}) collective-permute-start(bf16[1,160,256]{2,1,0:T(8,128)(2,1)S(1)} %get-tuple-element.61), channel_id=1, source_target_pairs={{0,1},{1,0},{2,3},{3,2},{4,5},{5,4},{6,7},{7,6},{8,9},{9,8},{10,11... | collective-permute-start | bytes 245768 | tf_op jit(solution)/shard_map/ppermute | solution.py:324
  48.9 11.3 %collective-permute-start.10 = (bf16[5,128,128]{2,1,0:T(8,128)(2,1)S(1)}, bf16[5,128,128]{2,1,0:T(8,128)(2,1)S(1)}, u32[]{:S(2)}, u32[]{:S(2)}) collective-permute-start(bf16[5,128,128]{2,1,0:T(8,128)(2,1)S(1)} %get-tuple-element.55), channel_id=1, source_target_pairs={{0,2},{2,4},{4,6},{6,0},{1,3},{3,5},{5,7},{7,1},{8,10},{10,12},{12... | collective-permute-start | bytes 491528 | tf_op jit(solution)/shard_map/ppermute | solution.py:306
  49.0 12.3 %collective-permute-start.11 = (bf16[5,128,128]{2,1,0:T(8,128)(2,1)S(1)}, bf16[5,128,128]{2,1,0:T(8,128)(2,1)S(1)}, u32[]{:S(2)}, u32[]{:S(2)}) collective-permute-start(bf16[5,128,128]{2,1,0:T(8,128)(2,1)S(1)} %get-tuple-element.56), channel_id=1, source_target_pairs={{0,4},{2,6},{4,0},{6,2},{1,5},{3,7},{5,1},{7,3},{8,12},{10,14},{12... | collective-permute-start | bytes 491528 | tf_op jit(solution)/shard_map/ppermute | solution.py:306
  51.3 10.0 %collective-permute-start.12 = (bf16[5,128,128]{2,1,0:T(8,128)(2,1)S(1)}, bf16[5,128,128]{2,1,0:T(8,128)(2,1)S(1)}, u32[]{:S(2)}, u32[]{:S(2)}) collective-permute-start(bf16[5,128,128]{2,1,0:T(8,128)(2,1)S(1)} %get-tuple-element.57), channel_id=1, source_target_pairs={{0,6},{2,0},{4,2},{6,4},{1,7},{3,1},{5,3},{7,5},{8,14},{10,8},{12,... | collective-permute-start | bytes 491528 | tf_op jit(solution)/shard_map/ppermute | solution.py:306
  56.5 4.8 %copy-start = (s32[1,5]{1,0:T(1,128)S(1)}, s32[1,5]{1,0:T(1,128)}, u32[]{:S(2)}) copy-start(s32[1,5]{1,0:T(1,128)} %offsets.3) | copy-start | bytes 64
  57.1 8.5 %collective-permute-start.7 = (bf16[4,128,128]{2,1,0:T(8,128)(2,1)S(1)}, bf16[4,128,128]{2,1,0:T(8,128)(2,1)S(1)}, u32[]{:S(2)}, u32[]{:S(2)}) collective-permute-start(bf16[4,128,128]{2,1,0:T(8,128)(2,1)S(1)} %get-tuple-element.52), channel_id=1, source_target_pairs={{0,2},{2,4},{4,6},{6,0},{1,3},{3,5},{5,7},{7,1},{8,10},{10,12},{12... | collective-permute-start | bytes 393224 | tf_op jit(solution)/shard_map/ppermute | solution.py:306
  57.2 8.4 %collective-permute-start.8 = (bf16[4,128,128]{2,1,0:T(8,128)(2,1)S(1)}, bf16[4,128,128]{2,1,0:T(8,128)(2,1)S(1)}, u32[]{:S(2)}, u32[]{:S(2)}) collective-permute-start(bf16[4,128,128]{2,1,0:T(8,128)(2,1)S(1)} %get-tuple-element.53), channel_id=1, source_target_pairs={{0,4},{2,6},{4,0},{6,2},{1,5},{3,7},{5,1},{7,3},{8,12},{10,14},{12... | collective-permute-start | bytes 393224 | tf_op jit(solution)/shard_map/ppermute | solution.py:306
  60.2 6.1 %collective-permute-start.9 = (bf16[4,128,128]{2,1,0:T(8,128)(2,1)S(1)}, bf16[4,128,128]{2,1,0:T(8,128)(2,1)S(1)}, u32[]{:S(2)}, u32[]{:S(2)}) collective-permute-start(bf16[4,128,128]{2,1,0:T(8,128)(2,1)S(1)} %get-tuple-element.54), channel_id=1, source_target_pairs={{0,6},{2,0},{4,2},{6,4},{1,7},{3,1},{5,3},{7,5},{8,14},{10,8},{12,... | collective-permute-start | bytes 393224 | tf_op jit(solution)/shard_map/ppermute | solution.py:306
